TPU v7x, 32 devices: a whole 2x2x4 slice. The times are simulated.
32 devices in a mesh: seq: 8 (over z, y), head: 4 (over x, core).
Axes of the slice: x: 2, y: 2, z: 4, core: 2. Of those that a mesh axis runs over, the one named last changes fastest.
Arguments:
- queries: bfloat16 [8192, 1024], P('seq', 'head'), may hold values from -6 to 6
- key_rows: bfloat16 [8192, 1024], P('seq', 'head'), may hold values from -6 to 6
- value_rows: bfloat16 [8192, 1024], P('seq', 'head'), may hold values from -6 to 6
- attn_out: bfloat16 [8192, 1024], P('seq', 'head'), may hold values from -6 to 6
- gate_pre: bfloat16 [8192, 1024], P('seq', 'head'), may hold values from -6 to 6
- out_grad: bfloat16 [8192, 1024], P('seq', 'head'), may hold values from -6 to 6
- segments: int32 [8192], P('seq'), may hold values from 0 to 1, never falling along the last dimension, each value on 1 to 6145 neighbouring positions
- projections: bfloat16 [4, 1024, 1024], P(None, None, 'head'), may hold values from -0.1875 to 0.1875
Outputs:
- input_grad: bfloat16 [8192, 1024], P('seq', 'head')
Inputs may be any that keep to these rules, and one draw needn't show every extreme that they name: `segments`: each user's rows are contiguous and ordered; a user has 1 to 6145 rows and one user has exactly 6145, so no user spans more than 6 + 1 = 7 shards of 1024 rows.
All inputs are finite; a program needn't handle non-finite values.
Results may differ from a plain program's by a relative error of at most 0.0064.
Values may be sent and summed in bfloat16 or wider, within the bound.
A program may use at most 128 MiB of HBM per device.

v0:
```python
import jax
import jax.numpy as jnp
from jax import lax
from jax.sharding import PartitionSpec as P

HEAD_DIM = 128
WINDOW = 6


def from_behind(block, axis, distance):
    devices = range(lax.axis_size(axis))
    route = [(i - distance, i) for i in devices if i - distance in devices]
    return lax.ppermute(block, axis, route)


def silu_slope(values_in):
    sigma = jax.nn.sigmoid(values_in)
    return sigma * (1.0 + values_in * (1.0 - sigma))


def norm_backward(attn_out, gate_pre, out_grad):
    row_count, width = attn_out.shape
    head_count = width // HEAD_DIM
    saved = attn_out.astype(jnp.float32).reshape(row_count, head_count, HEAD_DIM)
    centred = saved - jnp.mean(saved, axis=-1, keepdims=True)
    inverse = lax.rsqrt(jnp.mean(centred * centred, axis=-1, keepdims=True) + 1e-06)
    normed = centred * inverse
    gate_in = gate_pre.astype(jnp.float32)
    grad_in = out_grad.astype(jnp.float32)
    gate_grad = grad_in * normed.reshape(row_count, width) * silu_slope(gate_in)
    normed_grad = (grad_in * jax.nn.silu(gate_in)).reshape(row_count, head_count, HEAD_DIM)
    attn_grad = inverse * (
        normed_grad
        - jnp.mean(normed_grad, axis=-1, keepdims=True)
        - normed * jnp.mean(normed_grad * normed, axis=-1, keepdims=True)
    )
    return (
        attn_grad.reshape(row_count, width).astype(jnp.bfloat16),
        gate_grad.astype(jnp.bfloat16),
    )


def contract_last(left, right):
    return lax.dot_general(
        left, right, (((1,), (1,)), ((), ())), preferred_element_type=jnp.float32
    )


def contract_first(left, right):
    return lax.dot_general(
        left, right, (((0,), (0,)), ((), ())), preferred_element_type=jnp.float32
    )


def block_grads(query_in, grad_in, key_in, value_in, allowed):
    scale = HEAD_DIM ** (-0.5)
    head_count = query_in.shape[1] // HEAD_DIM
    query_parts, key_parts, value_parts = ([], [], [])
    for head_idx in range(head_count):
        columns = slice(head_idx * HEAD_DIM, (head_idx + 1) * HEAD_DIM)
        query_head = query_in[:, columns]
        grad_head = grad_in[:, columns]
        key_head = key_in[:, columns]
        value_head = value_in[:, columns]
        scores = contract_last(query_head, key_head) * scale
        weights = jnp.where(allowed, jax.nn.silu(scores), 0.0).astype(jnp.bfloat16)
        slope_in = contract_last(grad_head, value_head)
        score_grad = jnp.where(allowed, slope_in * silu_slope(scores) * scale, 0.0).astype(
            jnp.bfloat16
        )
        query_parts.append(jnp.dot(score_grad, key_head, preferred_element_type=jnp.float32))
        key_parts.append(contract_first(score_grad, query_head))
        value_parts.append(contract_first(weights, grad_head))
    return (
        jnp.concatenate(query_parts, axis=1),
        jnp.concatenate(key_parts, axis=1),
        jnp.concatenate(value_parts, axis=1),
    )


def per_device(queries, key_rows, value_rows, attn_out, gate_pre, out_grad, segments, projections):
    attn_grad, gate_grad = norm_backward(attn_out, gate_pre, out_grad)
    row_count = queries.shape[0]
    owners = (segments + 1).astype(jnp.bfloat16)
    causal = lax.broadcasted_iota(jnp.int32, (row_count, row_count), 0) >= lax.broadcasted_iota(
        jnp.int32, (row_count, row_count), 1
    )

    def attend(query_in, grad_in, owner_q, key_in, value_in, owner_k, diagonal):
        allowed = owner_q[:, None] == owner_k[None, :]
        if diagonal:
            allowed = allowed & causal
        return block_grads(query_in, grad_in, key_in, value_in, allowed)

    query_acc, key_acc, value_acc = attend(
        queries, attn_grad, owners, key_rows, value_rows, owners, True
    )
    for distance in range(1, WINDOW + 1):
        far_queries, far_grads, far_owners = from_behind(
            (queries, attn_grad, owners), "seq", -distance
        )
        part_query, part_key, part_value = attend(
            far_queries, far_grads, far_owners, key_rows, value_rows, owners, False
        )
        key_acc = key_acc + part_key
        value_acc = value_acc + part_value
        query_acc = query_acc + from_behind(part_query, "seq", distance)
    stacked = jnp.stack(
        [
            query_acc.astype(jnp.bfloat16),
            key_acc.astype(jnp.bfloat16),
            value_acc.astype(jnp.bfloat16),
            gate_grad,
        ]
    )
    partial_sum = jnp.einsum(
        "prh,pdh->rd", stacked, projections, preferred_element_type=jnp.float32
    )
    return lax.psum_scatter(partial_sum, "head", scatter_dimension=1, tiled=True).astype(
        jnp.bfloat16
    )


def solution(mesh):
    return jax.shard_map(
        per_device,
        mesh=mesh,
        in_specs=(
            P("seq", "head"),
            P("seq", "head"),
            P("seq", "head"),
            P("seq", "head"),
            P("seq", "head"),
            P("seq", "head"),
            P("seq"),
            P(None, None, "head"),
        ),
        out_specs=P("seq", "head"),
        check_vma=False,
    )
```

profile of v0, /device:TPU:0, one launch (start us, length us, event | category | flops | bytes accessed | tf_op | source)
XLA Modules:
  0.0 500.0 jit_solution(16484630652338471316)
XLA Ops:
  23.7 2.9 fusion.60
  26.6 2.6 select_convert_fusion.2
  29.2 2.3 convolution_bitcast_fusion.13
  34.8 2.9 fusion.61
  37.6 2.6 select_convert_fusion.3
  49.0 16.0 %collective-permute-done.22 = bf16[1024,256]{1,0:T(8,128)(2,1)S(1)} collective-permute-done((bf16[1024,256]{1,0:T(8,128)(2,1)}, bf16[1024,256]{1,0:T(8,128)(2,1)S(1)}, u32[]{:S(2)}, u32[]{:S(2)}) %collective-permute-start.22) | collective-permute-done | bytes 524320 | tf_op jit(solution)/shard_map/ppermute | solution.py:13
  67.7 12.1 %collective-permute-done.2 = bf16[1024,256]{1,0:T(8,128)(2,1)S(1)} collective-permute-done((bf16[1024,256]{1,0:T(8,128)(2,1)}, bf16[1024,256]{1,0:T(8,128)(2,1)S(1)}, u32[]{:S(2)}, u32[]{:S(2)}) %collective-permute-start.2) | collective-permute-done | bytes 524320 | tf_op jit(solution)/shard_map/ppermute | solution.py:13
  82.5 11.2 %collective-permute-done.6 = bf16[1024,256]{1,0:T(8,128)(2,1)S(1)} collective-permute-done((bf16[1024,256]{1,0:T(8,128)(2,1)}, bf16[1024,256]{1,0:T(8,128)(2,1)S(1)}, u32[]{:S(2)}, u32[]{:S(2)}) %collective-permute-start.6) | collective-permute-done | bytes 524320 | tf_op jit(solution)/shard_map/ppermute | solution.py:13
  97.7 32.5 %collective-permute-done.17 = bf16[1024,256]{0,1:T(8,128)(2,1)S(1)} collective-permute-done((bf16[1024,256]{0,1:T(8,128)(2,1)}, bf16[1024,256]{0,1:T(8,128)(2,1)S(1)}, u32[]{:S(2)}, u32[]{:S(2)}) %collective-permute-start.17) | collective-permute-done | bytes 524320 | tf_op jit(solution)/shard_map/ppermute | solution.py:13
  131.5 2.6 fusion.17
  134.1 2.6 fusion.16
  139.7 8.4 %collective-permute-done.21 = bf16[1024,256]{0,1:T(8,128)(2,1)S(1)} collective-permute-done((bf16[1024,256]{0,1:T(8,128)(2,1)}, bf16[1024,256]{0,1:T(8,128)(2,1)S(1)}, u32[]{:S(2)}, u32[]{:S(2)}) %collective-permute-start.21) | collective-permute-done | bytes 524320 | tf_op jit(solution)/shard_map/ppermute | solution.py:13
  150.6 3.2 fusion.21
  153.8 2.6 fusion.20
  159.4 4.5 collective-permute-done.1
  165.2 3.2 fusion.1
  168.4 3.6 fusion
  176.7 12.2 %collective-permute-done.5 = bf16[1024,256]{0,1:T(8,128)(2,1)} collective-permute-done((bf16[1024,256]{0,1:T(8,128)(2,1)}, bf16[1024,256]{0,1:T(8,128)(2,1)}, u32[]{:S(2)}, u32[]{:S(2)}) %collective-permute-start.5) | collective-permute-done | bytes 524320 | tf_op jit(solution)/shard_map/ppermute | solution.py:13
  190.3 3.2 fusion.5
  193.5 3.7 fusion.4
  201.6 9.0 %collective-permute-done.10 = bf16[1024,256]{1,0:T(8,128)(2,1)} collective-permute-done((bf16[1024,256]{1,0:T(8,128)(2,1)}, bf16[1024,256]{1,0:T(8,128)(2,1)}, u32[]{:S(2)}, u32[]{:S(2)}) %collective-permute-start.10) | collective-permute-done | bytes 524320 | tf_op jit(solution)/shard_map/ppermute | solution.py:13
  214.7 49.0 %collective-permute-start.19 = (f32[1024,256]{0,1:T(8,128)}, f32[1024,256]{0,1:T(8,128)}, u32[]{:S(2)}, u32[]{:S(2)}) collective-permute-start(f32[1024,256]{0,1:T(8,128)} %pad_maximum_fusion.4), channel_id=1, source_target_pairs={{0,20},{4,24},{8,28},{1,21},{5,25},{9,29},{2,22},{6,26},{10,30},{3... | collective-permute-start | bytes 3145736 | tf_op jit(solution)/shard_map/ppermute | solution.py:13
  263.7 2.3 collective-permute-start.23
  266.0 3.2 fusion.9
  273.8 4.6 fusion.8
  278.4 2.3 pad_maximum_fusion
  280.8 2.5 fusion.315
  284.4 2.3 collective-permute-start.3
  286.6 3.7 fusion.179
  291.4 2.3 collective-permute-start.7
  293.7 2.7 collective-permute-start.11
  296.3 5.9 %fusion.13 = bf16[1024,1024]{1,0:T(8,128)(2,1)} fusion(f32[1024,1024]{1,0:T(8,128)} %fusion.179, bf16[1024]{0:T(1024)(128)(2,1)S(1)} %add_convert_fusion, bf16[1024]{0:T(1024)(128)(2,1)S(1)} %collective-permute-done.12, bf16[1024,256]{0,1:T(8,128)(2,1)} %collective-permute-done.13, bf16[1024,256]{1,0:T(8,128)(2,1)} %param.10), kind=kOutput, calls=%fused_computation.37 | convolution fusion | flops 282066944 | bytes 6819840 | tf_op jit(solution)/shard_map/dot_general | solution.py:44
  302.2 3.2 fusion.291
  305.4 3.7 fusion.184
  309.1 5.8 %fusion.12 = bf16[1024,1024]{1,0:T(8,128)(2,1)} fusion(f32[1024,1024]{1,0:T(8,128)} %fusion.184, bf16[1024]{0:T(1024)(128)(2,1)S(1)} %add_convert_fusion, bf16[1024]{0:T(1024)(128)(2,1)S(1)} %collective-permute-done.12, bf16[1024,256]{0,1:T(8,128)(2,1)} %collective-permute-done.13, bf16[1024,256]{1,0:T(8,128)(2,1)} %param.10), kind=kOutput, calls=%fused_computation.36 | convolution fusion | flops 282066944 | bytes 6819840 | tf_op jit(solution)/shard_map/dot_general | solution.py:44
  314.9 2.5 fusion.312
  331.3 2.5 fusion.65
  334.4 2.5 fusion.62
  337.5 2.5 fusion.71
  340.5 2.5 fusion.68
  343.6 2.4 fusion.77
  346.0 2.5 fusion.74
  348.6 2.5 fusion.83
  353.4 2.5 fusion.80
  364.1 15.4 %collective-permute-done.15 = f32[1024,256]{0,1:T(8,128)S(1)} collective-permute-done((f32[1024,256]{0,1:T(8,128)S(1)}, f32[1024,256]{0,1:T(8,128)S(1)}, u32[]{:S(2)}, u32[]{:S(2)}) %collective-permute-start.15) | collective-permute-done | bytes 1048608 | tf_op jit(solution)/shard_map/ppermute | solution.py:13
  379.4 3.2 fusion.157
  382.6 4.4 convolution_bitcast_fusion
  387.1 103.8 %reduce-scatter.2.cloned.1.call-done = f32[1024,256]{1,0:T(8,128)} async-done(((f32[1024,1024]{1,0:T(8,128)}), f32[1024,256]{1,0:T(8,128)}) %reduce-scatter.2.cloned.1.call-update) | async-done | bytes 1048592 | tf_op jit(solution)/shard_map/reduce_scatter | solution.py:119
  (205 shorter events, 98.9 us)
Async XLA Ops:
  6.5 376.1 %copy-start = (bf16[4,1024,256]{2,1,0:T(8,128)(2,1)S(1)}, bf16[4,1024,256]{2,1,0:T(8,128)(2,1)}, u32[]{:S(2)}) copy-start(bf16[4,1024,256]{2,1,0:T(8,128)(2,1)} %param.15) | copy-start | bytes 6291460
  6.5 13.0 %copy-start.1 = (bf16[1024,256]{1,0:T(8,128)(2,1)S(1)}, bf16[1024,256]{1,0:T(8,128)(2,1)}, u32[]{:S(2)}) copy-start(bf16[1024,256]{1,0:T(8,128)(2,1)} %param.9) | copy-start | bytes 1572868
  6.5 484.3 %reduce-scatter.2.cloned.1.call-start = ((), (), s32[]{:S(2)}) async-start(), calls=%async_computation.1 | async-start | bytes 5242880 | tf_op jit(solution)/shard_map/reduce_scatter | solution.py:119
  7.4 131.0 %collective-permute-start.20 = (bf16[1024]{0:T(1024)(128)(2,1)S(1)}, bf16[1024]{0:T(1024)(128)(2,1)S(1)}, u32[]{:S(2)}, u32[]{:S(2)}) collective-permute-start(bf16[1024]{0:T(1024)(128)(2,1)S(1)} %add_convert_fusion), channel_id=1, source_target_pairs={{24,0},{28,4},{25,1},{29,5},{26,2},{30,6},{27,3},{31,7}} | collective-permute-start | bytes 6152 | tf_op jit(solution)/shard_map/ppermute | solution.py:13
  8.7 87.8 %collective-permute-start.16 = (bf16[1024]{0:T(1024)(128)(2,1)S(1)}, bf16[1024]{0:T(1024)(128)(2,1)S(1)}, u32[]{:S(2)}, u32[]{:S(2)}) collective-permute-start(bf16[1024]{0:T(1024)(128)(2,1)S(1)} %add_convert_fusion), channel_id=1, source_target_pairs={{20,0},{24,4},{28,8},{21,1},{25,5},{29,9},{22,2},{26,6},{30,10},{2... | collective-permute-start | bytes 6152 | tf_op jit(solution)/shard_map/ppermute | solution.py:13
  10.0 281.4 %collective-permute-start.12 = (bf16[1024]{0:T(1024)(128)(2,1)S(1)}, bf16[1024]{0:T(1024)(128)(2,1)S(1)}, u32[]{:S(2)}, u32[]{:S(2)}) collective-permute-start(bf16[1024]{0:T(1024)(128)(2,1)S(1)} %add_convert_fusion), channel_id=1, source_target_pairs={{16,0},{20,4},{24,8},{28,12},{17,1},{21,5},{25,9},{29,13},{18,2},{... | collective-permute-start | bytes 6152 | tf_op jit(solution)/shard_map/ppermute | solution.py:13
  11.3 203.4 %collective-permute-start.8 = (bf16[1024]{0:T(1024)(128)(2,1)S(1)}, bf16[1024]{0:T(1024)(128)(2,1)S(1)}, u32[]{:S(2)}, u32[]{:S(2)}) collective-permute-start(bf16[1024]{0:T(1024)(128)(2,1)S(1)} %add_convert_fusion), channel_id=1, source_target_pairs={{12,0},{16,4},{20,8},{24,12},{28,16},{13,1},{17,5},{21,9},{25,13},... | collective-permute-start | bytes 6152 | tf_op jit(solution)/shard_map/ppermute | solution.py:13
  12.6 31.6 %collective-permute-start.18 = (bf16[1024,256]{1,0:T(8,128)(2,1)}, bf16[1024,256]{1,0:T(8,128)(2,1)}, u32[]{:S(2)}, u32[]{:S(2)}) collective-permute-start(bf16[1024,256]{1,0:T(8,128)(2,1)} %param.8), channel_id=1, source_target_pairs={{20,0},{24,4},{28,8},{21,1},{25,5},{29,9},{22,2},{26,6},{30,10},{2... | collective-permute-start | bytes 1572872 | tf_op jit(solution)/shard_map/ppermute | solution.py:13
  44.1 20.8 %collective-permute-start.22 = (bf16[1024,256]{1,0:T(8,128)(2,1)}, bf16[1024,256]{1,0:T(8,128)(2,1)S(1)}, u32[]{:S(2)}, u32[]{:S(2)}) collective-permute-start(bf16[1024,256]{1,0:T(8,128)(2,1)} %param.8), channel_id=1, source_target_pairs={{24,0},{28,4},{25,1},{29,5},{26,2},{30,6},{27,3},{31,7}} | collective-permute-start | bytes 1572872 | tf_op jit(solution)/shard_map/ppermute | solution.py:13
  65.0 14.8 %collective-permute-start.2 = (bf16[1024,256]{1,0:T(8,128)(2,1)}, bf16[1024,256]{1,0:T(8,128)(2,1)S(1)}, u32[]{:S(2)}, u32[]{:S(2)}) collective-permute-start(bf16[1024,256]{1,0:T(8,128)(2,1)} %param.8), channel_id=1, source_target_pairs={{4,0},{8,4},{12,8},{16,12},{20,16},{24,20},{28,24},{5,1},{9,5},{13... | collective-permute-start | bytes 1572872 | tf_op jit(solution)/shard_map/ppermute | solution.py:13
  79.8 13.9 %collective-permute-start.6 = (bf16[1024,256]{1,0:T(8,128)(2,1)}, bf16[1024,256]{1,0:T(8,128)(2,1)S(1)}, u32[]{:S(2)}, u32[]{:S(2)}) collective-permute-start(bf16[1024,256]{1,0:T(8,128)(2,1)} %param.8), channel_id=1, source_target_pairs={{8,0},{12,4},{16,8},{20,12},{24,16},{28,20},{9,1},{13,5},{17,9},{2... | collective-permute-start | bytes 1572872 | tf_op jit(solution)/shard_map/ppermute | solution.py:13
  93.7 36.5 %collective-permute-start.17 = (bf16[1024,256]{0,1:T(8,128)(2,1)}, bf16[1024,256]{0,1:T(8,128)(2,1)S(1)}, u32[]{:S(2)}, u32[]{:S(2)}) collective-permute-start(bf16[1024,256]{0,1:T(8,128)(2,1)} %get-tuple-element.7), channel_id=1, source_target_pairs={{20,0},{24,4},{28,8},{21,1},{25,5},{29,9},{22,2},{26,6},{30,10},{2... | collective-permute-start | bytes 1572872 | tf_op jit(solution)/shard_map/ppermute | solution.py:13
  96.4 79.0 %collective-permute-start.4 = (bf16[1024]{0:T(1024)(128)(2,1)S(1)}, bf16[1024]{0:T(1024)(128)(2,1)S(1)}, u32[]{:S(2)}, u32[]{:S(2)}) collective-permute-start(bf16[1024]{0:T(1024)(128)(2,1)S(1)} %add_convert_fusion), channel_id=1, source_target_pairs={{8,0},{12,4},{16,8},{20,12},{24,16},{28,20},{9,1},{13,5},{17,9},{2... | collective-permute-start | bytes 6152 | tf_op jit(solution)/shard_map/ppermute | solution.py:13
  130.2 3.9 copy-start.50
  130.2 17.8 %collective-permute-start.21 = (bf16[1024,256]{0,1:T(8,128)(2,1)}, bf16[1024,256]{0,1:T(8,128)(2,1)S(1)}, u32[]{:S(2)}, u32[]{:S(2)}) collective-permute-start(bf16[1024,256]{0,1:T(8,128)(2,1)} %get-tuple-element.7), channel_id=1, source_target_pairs={{24,0},{28,4},{25,1},{29,5},{26,2},{30,6},{27,3},{31,7}} | collective-permute-start | bytes 1572872 | tf_op jit(solution)/shard_map/ppermute | solution.py:13
  136.7 17.1 %copy-start.6 = (bf16[1024,1024]{1,0:T(8,128)(2,1)}, bf16[1024,1024]{1,0:T(8,128)(2,1)S(1)}, u32[]{:S(2)}) copy-start(bf16[1024,1024]{1,0:T(8,128)(2,1)S(1)} %fusion.16) | copy-start | bytes 6291460
  138.4 19.8 %collective-permute-start = (bf16[1024]{0:T(1024)(128)(2,1)S(1)}, bf16[1024]{0:T(1024)(128)(2,1)S(1)}, u32[]{:S(2)}, u32[]{:S(2)}) collective-permute-start(bf16[1024]{0:T(1024)(128)(2,1)S(1)} %add_convert_fusion), channel_id=1, source_target_pairs={{4,0},{8,4},{12,8},{16,12},{20,16},{24,20},{28,24},{5,1},{9,5},{13... | collective-permute-start | bytes 6152 | tf_op jit(solution)/shard_map/ppermute | solution.py:13
  148.9 15.1 %collective-permute-start.1 = (bf16[1024,256]{0,1:T(8,128)(2,1)}, bf16[1024,256]{0,1:T(8,128)(2,1)}, u32[]{:S(2)}, u32[]{:S(2)}) collective-permute-start(bf16[1024,256]{0,1:T(8,128)(2,1)} %get-tuple-element.7), channel_id=1, source_target_pairs={{4,0},{8,4},{12,8},{16,12},{20,16},{24,20},{28,24},{5,1},{9,5},{13... | collective-permute-start | bytes 1572872 | tf_op jit(solution)/shard_map/ppermute | solution.py:13
  156.4 12.0 %copy-start.10 = (bf16[1024,1024]{1,0:T(8,128)(2,1)}, bf16[1024,1024]{1,0:T(8,128)(2,1)S(1)}, u32[]{:S(2)}) copy-start(bf16[1024,1024]{1,0:T(8,128)(2,1)S(1)} %fusion.20) | copy-start | bytes 6291460
  156.4 8.8 %copy-start.47 = (bf16[1024,256]{1,0:T(8,128)(2,1)S(1)}, bf16[1024,256]{1,0:T(8,128)(2,1)}, u32[]{:S(2)}) copy-start(bf16[1024,256]{1,0:T(8,128)(2,1)} %param.10) | copy-start | bytes 1572868
  158.1 135.5 %collective-permute-start.13 = (bf16[1024,256]{0,1:T(8,128)(2,1)}, bf16[1024,256]{0,1:T(8,128)(2,1)}, u32[]{:S(2)}, u32[]{:S(2)}) collective-permute-start(bf16[1024,256]{0,1:T(8,128)(2,1)} %get-tuple-element.7), channel_id=1, source_target_pairs={{16,0},{20,4},{24,8},{28,12},{17,1},{21,5},{25,9},{29,13},{18,2},{... | collective-permute-start | bytes 1572872 | tf_op jit(solution)/shard_map/ppermute | solution.py:13
  163.9 24.9 %collective-permute-start.5 = (bf16[1024,256]{0,1:T(8,128)(2,1)}, bf16[1024,256]{0,1:T(8,128)(2,1)}, u32[]{:S(2)}, u32[]{:S(2)}) collective-permute-start(bf16[1024,256]{0,1:T(8,128)(2,1)} %get-tuple-element.7), channel_id=1, source_target_pairs={{8,0},{12,4},{16,8},{20,12},{24,16},{28,20},{9,1},{13,5},{17,9},{2... | collective-permute-start | bytes 1572872 | tf_op jit(solution)/shard_map/ppermute | solution.py:13
  168.4 3.6 copy-start.17
  172.1 21.5 %copy-start.14 = (bf16[1024,1024]{1,0:T(8,128)(2,1)}, bf16[1024,1024]{1,0:T(8,128)(2,1)S(1)}, u32[]{:S(2)}) copy-start(bf16[1024,1024]{1,0:T(8,128)(2,1)S(1)} %fusion) | copy-start | bytes 6291460
  172.1 18.2 %copy-start.48 = (bf16[1024,256]{1,0:T(8,128)(2,1)S(1)}, bf16[1024,256]{1,0:T(8,128)(2,1)}, u32[]{:S(2)}) copy-start(bf16[1024,256]{1,0:T(8,128)(2,1)} %param.10) | copy-start | bytes 1572868
  175.4 88.2 %collective-permute-start.9 = (bf16[1024,256]{0,1:T(8,128)(2,1)}, bf16[1024,256]{0,1:T(8,128)(2,1)}, u32[]{:S(2)}, u32[]{:S(2)}) collective-permute-start(bf16[1024,256]{0,1:T(8,128)(2,1)} %get-tuple-element.7), channel_id=1, source_target_pairs={{12,0},{16,4},{20,8},{24,12},{28,16},{13,1},{17,5},{21,9},{25,13},... | collective-permute-start | bytes 1572872 | tf_op jit(solution)/shard_map/ppermute | solution.py:13
  188.9 21.8 %collective-permute-start.10 = (bf16[1024,256]{1,0:T(8,128)(2,1)}, bf16[1024,256]{1,0:T(8,128)(2,1)}, u32[]{:S(2)}, u32[]{:S(2)}) collective-permute-start(bf16[1024,256]{1,0:T(8,128)(2,1)} %param.8), channel_id=1, source_target_pairs={{12,0},{16,4},{20,8},{24,12},{28,16},{13,1},{17,5},{21,9},{25,13},... | collective-permute-start | bytes 1572872 | tf_op jit(solution)/shard_map/ppermute | solution.py:13
  193.5 3.7 copy-start.21
  197.2 13.4 %copy-start.19 = (bf16[1024,1024]{1,0:T(8,128)(2,1)}, bf16[1024,1024]{1,0:T(8,128)(2,1)S(1)}, u32[]{:S(2)}) copy-start(bf16[1024,1024]{1,0:T(8,128)(2,1)S(1)} %fusion.4) | copy-start | bytes 6291460
  201.6 64.4 %copy-start.49 = (bf16[1024,256]{1,0:T(8,128)(2,1)S(1)}, bf16[1024,256]{1,0:T(8,128)(2,1)}, u32[]{:S(2)}) copy-start(bf16[1024,256]{1,0:T(8,128)(2,1)} %param.10) | copy-start | bytes 1572868
  210.6 73.7 %collective-permute-start.14 = (bf16[1024,256]{1,0:T(8,128)(2,1)}, bf16[1024,256]{1,0:T(8,128)(2,1)}, u32[]{:S(2)}, u32[]{:S(2)}) collective-permute-start(bf16[1024,256]{1,0:T(8,128)(2,1)} %param.8), channel_id=1, source_target_pairs={{16,0},{20,4},{24,8},{28,12},{17,1},{21,5},{25,9},{29,13},{18,2},{... | collective-permute-start | bytes 1572872 | tf_op jit(solution)/shard_map/ppermute | solution.py:13
  214.7 141.3 %collective-permute-start.19 = (f32[1024,256]{0,1:T(8,128)}, f32[1024,256]{0,1:T(8,128)}, u32[]{:S(2)}, u32[]{:S(2)}) collective-permute-start(f32[1024,256]{0,1:T(8,128)} %pad_maximum_fusion.4), channel_id=1, source_target_pairs={{0,20},{4,24},{8,28},{1,21},{5,25},{9,29},{2,22},{6,26},{10,30},{3... | collective-permute-start | bytes 3145736 | tf_op jit(solution)/shard_map/ppermute | solution.py:13
  263.7 100.4 %collective-permute-start.23 = (f32[1024,256]{0,1:T(8,128)}, f32[1024,256]{0,1:T(8,128)}, u32[]{:S(2)}, u32[]{:S(2)}) collective-permute-start(f32[1024,256]{0,1:T(8,128)} %pad_maximum_fusion.5), channel_id=1, source_target_pairs={{0,24},{4,28},{1,25},{5,29},{2,26},{6,30},{3,27},{7,31}} | collective-permute-start | bytes 3145736 | tf_op jit(solution)/shard_map/ppermute | solution.py:13
  278.4 4.8 copy-start.27
  278.4 4.8 copy-start.28
  280.8 9.5 %copy-start.29 = (f32[1024,128]{0,1:T(8,128)S(1)}, f32[1024,128]{0,1:T(8,128)}, u32[]{:S(2)}) copy-start(f32[1024,128]{0,1:T(8,128)} %fusion.294) | copy-start | bytes 1572868
  284.4 79.7 %collective-permute-start.3 = (f32[1024,256]{0,1:T(8,128)}, f32[1024,256]{0,1:T(8,128)}, u32[]{:S(2)}, u32[]{:S(2)}) collective-permute-start(f32[1024,256]{0,1:T(8,128)} %pad_maximum_fusion), channel_id=1, source_target_pairs={{0,4},{4,8},{8,12},{12,16},{16,20},{20,24},{24,28},{1,5},{5,9},{9,... | collective-permute-start | bytes 3145736 | tf_op jit(solution)/shard_map/ppermute | solution.py:13
  291.4 72.7 %collective-permute-start.7 = (f32[1024,256]{0,1:T(8,128)}, f32[1024,256]{0,1:T(8,128)}, u32[]{:S(2)}, u32[]{:S(2)}) collective-permute-start(f32[1024,256]{0,1:T(8,128)} %pad_maximum_fusion.1), channel_id=1, source_target_pairs={{0,8},{4,12},{8,16},{12,20},{16,24},{20,28},{1,9},{5,13},{9,17},{1... | collective-permute-start | bytes 3145736 | tf_op jit(solution)/shard_map/ppermute | solution.py:13
  293.7 70.4 %collective-permute-start.11 = (f32[1024,256]{0,1:T(8,128)}, f32[1024,256]{0,1:T(8,128)}, u32[]{:S(2)}, u32[]{:S(2)}) collective-permute-start(f32[1024,256]{0,1:T(8,128)} %pad_maximum_fusion.2), channel_id=1, source_target_pairs={{0,12},{4,16},{8,20},{12,24},{16,28},{1,13},{5,17},{9,21},{13,25},... | collective-permute-start | bytes 3145736 | tf_op jit(solution)/shard_map/ppermute | solution.py:13
  314.9 4.6 copy-start.51
  353.4 4.1 copy-start.42
  353.4 4.1 copy-start.43
  353.4 4.1 copy-start.44
  353.4 4.1 copy-start.45
  356.0 23.4 %collective-permute-start.15 = (f32[1024,256]{0,1:T(8,128)S(1)}, f32[1024,256]{0,1:T(8,128)S(1)}, u32[]{:S(2)}, u32[]{:S(2)}) collective-permute-start(f32[1024,256]{0,1:T(8,128)S(1)} %copy-done.32), channel_id=1, source_target_pairs={{0,16},{4,20},{8,24},{12,28},{1,17},{5,21},{9,25},{13,29},{2,18},{... | collective-permute-start | bytes 3145736 | tf_op jit(solution)/shard_map/ppermute | solution.py:13
  363.1 16.3 %copy-start.30 = (f32[1024,128]{0,1:T(8,128)S(1)}, f32[1024,128]{0,1:T(8,128)}, u32[]{:S(2)}) copy-start(f32[1024,128]{0,1:T(8,128)} %fusion.303) | copy-start | bytes 1572868
  363.1 16.3 %copy-start.31 = (f32[1024,128]{0,1:T(8,128)S(1)}, f32[1024,128]{0,1:T(8,128)}, u32[]{:S(2)}) copy-start(f32[1024,128]{0,1:T(8,128)} %fusion.324) | copy-start | bytes 1572868
  364.0 18.6 %copy-start.39 = (bf16[1024,256]{0,1:T(8,128)(2,1)S(1)}, bf16[1024,256]{0,1:T(8,128)(2,1)}, u32[]{:S(2)}) copy-start(bf16[1024,256]{0,1:T(8,128)(2,1)} %get-tuple-element.8) | copy-start | bytes 1572868
  (32 other events, 74.9 us)
Sparse Core Ops, SparseCore 0:
  387.2 103.6 reduce-scatter.1
where the time goes:
time: 510 us; the launch traced here: 500 us
  waiting for transfers between devices  225 us (44%)
  matrix products  149 us (29%)
  starting transfers between devices  83.9 us (16%)
  other arithmetic  19.3 us (4%)
  between operations  14.8 us (3%)
  local copies, waits for them, and re-layouts  8.45 us (2%)
    ppermute x24, waiting for transfers between devices, from_behind(): return lax.ppermute(block, axis, route)  121 us
    reduce_scatter x1, waiting for transfers between devices, per_device(): lax.psum_scatter(partial_sum, 'head', scatter_dimension=1, tiled=True)  104 us
    ppermute x24, starting transfers between devices, from_behind(): return lax.ppermute(block, axis, route)  83.9 us
    dot_general x28, matrix products, contract_last(): lax.dot_general(left, right, (((1,), (1,)), ((), ())), preferred_element_...  70.8 us
    dot_general x28, matrix products, contract_first(): lax.dot_general(left, right, (((0,), (0,)), ((), ())), preferred_element_...  50.3 us
    dot_general x14, matrix products, block_grads(): jnp.dot(score_grad, key_head, preferred_element_type=jnp.float32)  23 us
  transfers between devices with their start and end apart: 25, of which 10 were waited for; matrix products, arithmetic and copies ran while one was open for 33% of the time, Pallas kernels for 0%

commit v1 on v0

v1 whole, which is shorter than its diff:
```python
import functools

import jax
import jax.numpy as jnp
from jax import lax
from jax.experimental import pallas as pl
from jax.experimental.pallas import tpu as pltpu
from jax.sharding import PartitionSpec as P

HEAD_DIM = 128
WINDOW = 6
PAIR = 2
TILE = 512
SCALE = HEAD_DIM ** (-0.5)
BF16 = jnp.bfloat16
F32 = jnp.float32


def dot(left, right, dims):
    return lax.dot_general(left, right, (dims, ((), ())), preferred_element_type=F32)


def prepare_kernel(
    place, queries, keys, values, attn_out, gate_pre, out_grad,
    query_own, query_other, key_own, key_other, gate_grad,
):
    lane = place[0]
    for slot, (to_query, to_key) in enumerate(((query_own, key_own), (query_other, key_other))):
        head = lane if slot == 0 else 1 - lane
        cols = pl.ds(pl.multiple_of(head * HEAD_DIM, HEAD_DIM), HEAD_DIM)
        to_query[0] = queries[:, cols]
        to_key[0] = keys[:, cols]
        to_key[1] = values[:, cols]
        saved = attn_out[:, cols].astype(F32)
        centred = saved - jnp.mean(saved, axis=-1, keepdims=True)
        inverse = lax.rsqrt(jnp.mean(centred * centred, axis=-1, keepdims=True) + 1e-06)
        normed = centred * inverse
        gate_in = gate_pre[:, cols].astype(F32)
        grad_in = out_grad[:, cols].astype(F32)
        sigma = jax.nn.sigmoid(gate_in)
        gate_grad[:, cols] = (
            grad_in * normed * (sigma * (1.0 + gate_in * (1.0 - sigma)))
        ).astype(BF16)
        normed_grad = grad_in * (gate_in * sigma)
        to_query[1] = (
            inverse
            * (
                normed_grad
                - jnp.mean(normed_grad, axis=-1, keepdims=True)
                - normed * jnp.mean(normed_grad * normed, axis=-1, keepdims=True)
            )
        ).astype(BF16)


def prepare(lane, queries, keys, values, attn_out, gate_pre, out_grad):
    rows, width = queries.shape
    step = min(rows, 256)
    wide = pl.BlockSpec((step, width), lambda i, place: (i, 0))
    pair = pl.BlockSpec((2, step, HEAD_DIM), lambda i, place: (0, i, 0))
    pair_shape = jax.ShapeDtypeStruct((2, rows, HEAD_DIM), BF16)
    return pl.pallas_call(
        prepare_kernel,
        grid_spec=pltpu.PrefetchScalarGridSpec(
            num_scalar_prefetch=1,
            grid=(rows // step,),
            in_specs=[wide] * 6,
            out_specs=[pair] * 4 + [wide],
        ),
        out_shape=[pair_shape] * 4 + [jax.ShapeDtypeStruct((rows, width), BF16)],
        compiler_params=pltpu.CompilerParams(vmem_limit_bytes=32 * 2**20),
        cost_estimate=pl.CostEstimate(
            flops=40 * rows * width, bytes_accessed=22 * rows * width, transcendentals=rows * width
        ),
        name="prepare",
    )(lane, queries, keys, values, attn_out, gate_pre, out_grad)


def attend_kernel(first, last, ids, segs, seg_rows, *refs):
    refs = list(refs)
    sources = [refs.pop(0) for _ in range(4 if first else 6)]
    query_out, own_out, other_out, query_in, key_in, key_acc, query_acc, sems = refs
    rows = query_in.shape[2]
    per = rows // TILE
    count = 2 * per

    targets = [query_in.at[0], query_in.at[1], key_in.at[0], key_in.at[1]]
    if not first:
        targets += [key_acc.at[0], key_acc.at[1]]
    copies = [
        pltpu.make_async_copy(source, target, sems.at[n])
        for n, (source, target) in enumerate(zip(sources, targets))
    ]
    for copy in copies:
        copy.start()
    query_acc[...] = jnp.zeros_like(query_acc)
    if first:
        key_acc[...] = jnp.zeros_like(key_acc)
    for copy in copies:
        copy.wait()

    def body(index, carry):
        q_idx, k_idx = index // count, index % count
        q_blk, k_blk = q_idx // per, k_idx // per
        q_off = pl.multiple_of((q_idx % per) * TILE, TILE)
        k_off = pl.multiple_of((k_idx % per) * TILE, TILE)
        q_shard, k_shard = ids[q_blk], ids[2 + k_blk]
        q_first, k_first = q_shard * rows + q_off, k_shard * rows + k_off
        q_last, k_last = q_first + TILE - 1, k_first + TILE - 1
        live = (ids[4] > 0) & (k_first <= q_last) & (segs[k_last] >= segs[q_first])
        full = (k_last <= q_first) & (segs[k_first] == segs[q_last])
        q_rows, k_rows = pl.ds(q_off, TILE), pl.ds(k_off, TILE)

        def work(masked):
            query = query_in[q_blk, 0, q_rows, :]
            grad = query_in[q_blk, 1, q_rows, :]
            key = key_in[k_blk, 0, k_rows, :]
            value = key_in[k_blk, 1, k_rows, :]
            half = dot(key, query, ((1,), (1,))) * (SCALE / 2)
            slope_in = dot(value, grad, ((1,), (1,)))
            tanh = jnp.tanh(half)
            upper = 1.0 + tanh
            weights = half * upper
            score_grad = slope_in * (upper + weights * (1.0 - tanh))
            if masked:
                seg_q = seg_rows[pl.ds(q_shard, 1), q_rows]
                seg_k = seg_rows[pl.ds(k_shard, 1), k_rows]
                seg_k = jnp.transpose(jnp.broadcast_to(seg_k, (HEAD_DIM, TILE)))[:, :1]
                place_k = k_first + lax.broadcasted_iota(jnp.int32, (TILE, TILE), 0)
                place_q = q_first + lax.broadcasted_iota(jnp.int32, (TILE, TILE), 1)
                allowed = (seg_q == seg_k) & (place_k <= place_q)
                weights = jnp.where(allowed, weights, 0.0)
                score_grad = jnp.where(allowed, score_grad, 0.0)
            weights = weights.astype(BF16)
            score_grad = score_grad.astype(BF16)
            key_acc[k_blk, 0, k_rows, :] += dot(score_grad, query, ((1,), (0,)))
            key_acc[k_blk, 1, k_rows, :] += dot(weights, grad, ((1,), (0,)))
            query_acc[q_blk, q_rows, :] += dot(score_grad, key, ((0,), (0,)))

        @pl.when(live & full)
        def _():
            work(False)

        @pl.when(live & jnp.logical_not(full))
        def _():
            work(True)

        return carry

    lax.fori_loop(0, count * count, body, 0)
    query_out[...] = (query_acc[...] * (SCALE / 2)).astype(query_out.dtype)
    for blk, out in enumerate((own_out, other_out)):
        if last:
            out[0] = (key_acc[blk, 0] * (SCALE / 2)).astype(BF16)
            out[1] = key_acc[blk, 1].astype(BF16)
        else:
            out[...] = key_acc[blk]


def attend(first, last, ids, segs, seg_rows, queries, keys, acc):
    rows = queries[0].shape[1]
    any_spec = pl.BlockSpec(memory_space=pl.ANY)
    vmem = pl.BlockSpec(memory_space=pltpu.VMEM)
    acc = () if first else tuple(acc)
    acc_shape = jax.ShapeDtypeStruct((2, rows, HEAD_DIM), BF16 if last else F32)
    pairs = (2 * rows) ** 2
    return pl.pallas_call(
        functools.partial(attend_kernel, first, last),
        grid_spec=pltpu.PrefetchScalarGridSpec(
            num_scalar_prefetch=2,
            grid=(),
            in_specs=[vmem] + [any_spec] * (4 + len(acc)),
            out_specs=[vmem] * 3,
            scratch_shapes=[
                pltpu.VMEM((2, 2, rows, HEAD_DIM), BF16),
                pltpu.VMEM((2, 2, rows, HEAD_DIM), BF16),
                pltpu.VMEM((2, 2, rows, HEAD_DIM), F32),
                pltpu.VMEM((2, rows, HEAD_DIM), F32),
                pltpu.SemaphoreType.DMA((6,)),
            ],
        ),
        out_shape=[
            jax.ShapeDtypeStruct((2, rows, HEAD_DIM), F32 if first else BF16),
            acc_shape,
            acc_shape,
        ],
        compiler_params=pltpu.CompilerParams(vmem_limit_bytes=48 * 2**20),
        cost_estimate=pl.CostEstimate(
            flops=10 * pairs * HEAD_DIM, bytes_accessed=14 * rows * HEAD_DIM * 4, transcendentals=pairs
        ),
        name="attend",
    )(ids, segs, seg_rows, *queries, *keys, *acc)


def project_kernel(
    place, query_own, key_own, query_other, key_other, gate_grad, weights, out, stacked
):
    @pl.when(pl.program_id(0) == 0)
    def _():
        lane = place[0]
        own = pl.ds(pl.multiple_of(lane * HEAD_DIM, HEAD_DIM), HEAD_DIM)
        other = pl.ds(pl.multiple_of((1 - lane) * HEAD_DIM, HEAD_DIM), HEAD_DIM)
        stacked[0, :, own] = query_own[...]
        stacked[0, :, other] = query_other[...]
        for part in range(2):
            stacked[1 + part, :, own] = key_own[part]
            stacked[1 + part, :, other] = key_other[part]
        stacked[3] = gate_grad[...]

    total = dot(stacked[0], weights[0], ((1,), (1,)))
    for part in range(1, 4):
        total = total + dot(stacked[part], weights[part], ((1,), (1,)))
    out[0] = total.astype(out.dtype)


def project(place, count, grads, projections, dtype):
    gate_grad = grads[-1]
    rows, width = gate_grad.shape
    whole = lambda array: pl.BlockSpec(array.shape, lambda i, place: (0,) * array.ndim)
    return pl.pallas_call(
        project_kernel,
        grid_spec=pltpu.PrefetchScalarGridSpec(
            num_scalar_prefetch=1,
            grid=(count,),
            in_specs=[whole(grad) for grad in grads]
            + [pl.BlockSpec((4, width, width), lambda i, place: (0, place[1 + i], 0))],
            out_specs=pl.BlockSpec((1, rows, width), lambda i, place: (i, 0, 0)),
            scratch_shapes=[pltpu.VMEM((4, rows, width), BF16)],
        ),
        out_shape=jax.ShapeDtypeStruct((count, rows, width), dtype),
        compiler_params=pltpu.CompilerParams(vmem_limit_bytes=40 * 2**20),
        cost_estimate=pl.CostEstimate(
            flops=8 * count * rows * width * width,
            bytes_accessed=rows * width * (8 + 4 * count),
            transcendentals=0,
        ),
        name="project",
    )(place, *grads, projections)


def per_device(queries, key_rows, value_rows, attn_out, gate_pre, out_grad, segments, projections):
    rows = queries.shape[0]
    shards, groups = lax.axis_size("seq"), lax.axis_size("head")
    shard, group = lax.axis_index("seq"), lax.axis_index("head")
    pairs = shards // PAIR
    pair, lane = shard // PAIR, shard % PAIR

    def swap(block):
        return lax.ppermute(block, "seq", [(i, i ^ 1) for i in range(shards)])

    def shift(block, distance):
        return lax.ppermute(
            block,
            "seq",
            [(i, i + PAIR * distance) for i in range(shards) if 0 <= i + PAIR * distance < shards],
        )

    segs = lax.all_gather(segments, "seq", tiled=True)
    seg_rows = segs.astype(F32).reshape(shards, rows)
    lane_arg = jnp.reshape(lane, (1,)).astype(jnp.int32)
    query_own, query_other, key_own, key_other, gate_grad = prepare(
        lane_arg, queries, key_rows, value_rows, attn_out, gate_pre, out_grad
    )
    block_a, block_b = query_own, swap(query_other)
    keys = (key_own, swap(key_other))

    reach = min((WINDOW + 1) // PAIR, pairs - 1)
    acc, query_sum = None, None
    for distance in range(reach + 1):
        if distance > 0:
            block_a, block_b = shift(block_a, -1), shift(block_b, -1)
        far = PAIR * jnp.minimum(pair + distance, pairs - 1)
        ids = jnp.stack(
            [far + lane, far + 1 - lane, shard, shard ^ 1, (pair + distance < pairs)]
        ).astype(jnp.int32)
        part, acc_own, acc_other = attend(
            distance == 0, distance == reach, ids, segs, seg_rows, (block_a, block_b), keys, acc
        )
        acc = (acc_own, acc_other)
        if distance == 0:
            query_sum = part
        else:
            query_sum = query_sum + shift(part, distance).astype(F32)
    query_sum = query_sum.astype(BF16)
    acc_other = swap(acc[1])
    query_other = swap(query_sum[1])
    grads = (query_sum[0], acc[0], query_other, acc_other, gate_grad)

    def blocks_of(targets):
        return jnp.stack([lane] + targets).astype(jnp.int32)

    bits = []
    while (1 << len(bits)) < groups:
        bits.append(1 << len(bits))
    kept = list(range(groups))

    def across(block, bit):
        return lax.ppermute(block, "head", [(i, i ^ bit) for i in range(groups)])

    near = [offset for offset in kept if offset & 1 == 0]
    sent = [offset for offset in kept if offset & 1 == 1]
    away = project(blocks_of([group ^ o for o in sent]), len(sent), grads, projections, BF16)
    arrived = across(away, 1)
    total = project(blocks_of([group ^ o for o in near]), len(near), grads, projections, F32)
    total = total + arrived.astype(F32)
    for bit in bits[1:]:
        sent = [n for n, offset in enumerate(near) if offset & bit]
        held = [n for n, offset in enumerate(near) if not offset & bit]
        arrived = across(jnp.stack([total[n] for n in sent]).astype(BF16), bit)
        total = jnp.stack([total[n] for n in held]) + arrived.astype(F32)
        near = [near[n] for n in held]
    return total[0].astype(BF16)


def solution(mesh):
    return jax.shard_map(
        per_device,
        mesh=mesh,
        in_specs=(
            P("seq", "head"),
            P("seq", "head"),
            P("seq", "head"),
            P("seq", "head"),
            P("seq", "head"),
            P("seq", "head"),
            P("seq"),
            P(None, None, "head"),
        ),
        out_specs=P("seq", "head"),
        check_vma=False,
    )
```

time: 510 us -> 202 us (0.40)
  the two profiles are of different devices: /device:TPU:0 before, /device:TPU:24 now
where the time goes in v1:
time: 202 us; the launch traced here: 198 us
  waiting for transfers between devices  82 us (41%)
  blocking collectives  41.3 us (20%)
  Pallas kernels  32.7 us (16%)
  starting transfers between devices  25.4 us (13%)
  local copies, waits for them, and re-layouts  13 us (6%)
  other arithmetic  2.87 us (1%)
    ppermute x9, waiting for transfers between devices, shift(): lax.ppermute(block, 'seq', [(i, i + PAIR * distance) for i in range(shard...  53.6 us
    all_gather x1, blocking collectives, per_device(): segs = lax.all_gather(segments, 'seq', tiled=True)  41.3 us
    pallas_call x4, Pallas kernels, attend(): pl.pallas_call(functools.partial(attend_kernel, first, last), grid_spec=p...  22 us
    ppermute x9, starting transfers between devices, shift(): lax.ppermute(block, 'seq', [(i, i + PAIR * distance) for i in range(shard...  20.6 us
    ppermute x4, waiting for transfers between devices, swap(): return lax.ppermute(block, 'seq', [(i, i ^ 1) for i in range(shards)])  15.6 us
    ppermute x2, waiting for transfers between devices, across(): return lax.ppermute(block, 'head', [(i, i ^ bit) for i in range(groups)])  12.8 us
    unnamed x28, local copies, waits for them, and re-layouts  11.9 us
    pallas_call x2, Pallas kernels, project(): pl.pallas_call(project_kernel, grid_spec=pltpu.PrefetchScalarGridSpec(num...  7.91 us
  transfers between devices with their start and end apart: 15, of which 7 were waited for; matrix products, arithmetic and copies ran while one was open for 1% of the time, Pallas kernels for 13%

profile of v1, /device:TPU:24, one launch (start us, length us, event | category | flops | bytes accessed | tf_op | source)
XLA Modules:
  0.0 197.6 jit_solution(1169483086180992618)
XLA Ops:
  0.0 1.1 copy-done.1
  1.1 1.0 copy-done.2
  2.1 1.0 copy-done.3
  3.1 1.0 copy-done.4
  4.2 1.0 copy-done.5
  5.2 1.0 copy-done.6
  6.3 2.8 %prepare.1 = (bf16[2,1024,128]{2,1,0:T(8,128)(2,1)S(1)}, bf16[2,1024,128]{2,1,0:T(8,128)(2,1)S(1)}, bf16[2,1024,128]{2,1,0:T(8,128)(2,1)S(1)}, bf16[2,1024,128]{2,1,0:T(8,128)(2,1)}, bf16[1024,256]{1,0:T(8,128)(2,1)S(1)}) custom-call(s32[1]{0:T(128)} %bitcast.place, bf16[1024,256]{1,0:T(8,128)(2,1)S(1)} %copy-done.1, bf16[1024,256]{1,0:T(8,128)(2,1)S(1)} %copy-done.2, ...), custom_call_target="tpu_custom_call" | custom-call | flops 10485760 | bytes 5767168 | tf_op jit(solution)/shard_map/prepare/pallas_call | solution.py:61
  9.1 1.5 collective-permute-start
  10.6 2.4 %collective-permute-start.2 = (bf16[2,1024,128]{2,1,0:T(8,128)(2,1)S(1)}, bf16[2,1024,128]{2,1,0:T(8,128)(2,1)S(1)}, u32[]{:S(2)}, u32[]{:S(2)}) collective-permute-start(bf16[2,1024,128]{2,1,0:T(8,128)(2,1)S(1)} %get-tuple-element.22.refs_0_), channel_id=1, source_target_pairs={{8,0},{12,4},{16,8},{20,12},{24,16},{28,20},{9,1},{13,5},{17,9},{2... | collective-permute-start | bytes 1572872 | tf_op jit(solution)/shard_map/ppermute | solution.py:251
  13.0 0.8 copy-done.7
  13.8 9.0 %collective-permute-done.refs_1_ = bf16[2,1024,128]{2,1,0:T(8,128)(2,1)S(1)} collective-permute-done((bf16[2,1024,128]{2,1,0:T(8,128)(2,1)S(1)}, bf16[2,1024,128]{2,1,0:T(8,128)(2,1)S(1)}, u32[]{:S(2)}, u32[]{:S(2)}) %collective-permute-start) | collective-permute-done | bytes 524320 | tf_op jit(solution)/shard_map/ppermute | solution.py:248
  22.7 3.2 %collective-permute-start.3 = (bf16[2,1024,128]{2,1,0:T(8,128)(2,1)S(1)}, bf16[2,1024,128]{2,1,0:T(8,128)(2,1)}, u32[]{:S(2)}, u32[]{:S(2)}) collective-permute-start(bf16[2,1024,128]{2,1,0:T(8,128)(2,1)S(1)} %collective-permute-done.refs_1_), channel_id=1, source_target_pairs={{8,0},{12,4},{16,8},{20,12},{24,16},{28,20},{9,1},{13,5},{17,9},{2... | collective-permute-start | bytes 1572872 | tf_op jit(solution)/shard_map/ppermute | solution.py:251
  25.9 0.8 copy-done.9
  26.7 1.5 collective-permute-start.1
  28.2 1.6 collective-permute-start.5
  29.8 7.7 %collective-permute-done.3.refs_1_ = bf16[2,1024,128]{2,1,0:T(8,128)(2,1)} collective-permute-done((bf16[2,1024,128]{2,1,0:T(8,128)(2,1)S(1)}, bf16[2,1024,128]{2,1,0:T(8,128)(2,1)}, u32[]{:S(2)}, u32[]{:S(2)}) %collective-permute-start.3) | collective-permute-done | bytes 524320 | tf_op jit(solution)/shard_map/ppermute | solution.py:251
  37.5 4.5 %collective-permute-start.6 = (bf16[2,1024,128]{2,1,0:T(8,128)(2,1)}, bf16[2,1024,128]{2,1,0:T(8,128)(2,1)S(1)}, u32[]{:S(2)}, u32[]{:S(2)}) collective-permute-start(bf16[2,1024,128]{2,1,0:T(8,128)(2,1)} %collective-permute-done.3.refs_1_), channel_id=1, source_target_pairs={{8,0},{12,4},{16,8},{20,12},{24,16},{28,20},{9,1},{13,5},{17,9},{2... | collective-permute-start | bytes 1572872 | tf_op jit(solution)/shard_map/ppermute | solution.py:251
  42.0 41.3 %all_gather.3.segs = s32[8192]{0:T(1024)S(1)} all-gather(s32[1024]{0:T(1024)S(1)} %copy-done.13), channel_id=1, replica_groups=mesh['seq'=8,'head'=4] {'seq'}, dimensions={0}, use_global_device_ids=true | all-gather | bytes 36864 | tf_op jit(solution)/shard_map/all_gather | solution.py:257
  83.4 0.1 stack.104.ids
  83.5 0.1 stack.109.ids
  83.6 0.1 stack.114.ids
  83.7 0.1 stack.119.ids
  83.7 1.0 copy-done.8
  84.8 1.0 copy-done.10
  85.8 13.2 %attend.4 = (f32[2,1024,128]{2,1,0:T(8,128)S(1)}, f32[2,1024,128]{2,1,0:T(8,128)S(1)}, f32[2,1024,128]{2,1,0:T(8,128)S(1)}) custom-call(s32[5]{0:T(128)S(1)} %stack.104.ids, s32[8192]{0:T(1024)S(1)} %all_gather.3.segs, f32[8,1024]{1,0:T(8,128)S(1)} %reshape.5.seg_rows, bf16[2,1024,128]{2,1,0:T(8,128)(2,1)S(1)} %copy-done.8, ...), custom_call_target="tpu_custom_call" | custom-call | flops 5368709120 | bytes 7340032 | tf_op jit(solution)/shard_map/attend/pallas_call | solution.py:166
  99.1 1.0 copy-done.11
  100.1 1.3 collective-permute-start.8
  101.4 3.6 %collective-permute-start.9 = (bf16[2,1024,128]{2,1,0:T(8,128)(2,1)S(1)}, bf16[2,1024,128]{2,1,0:T(8,128)(2,1)S(1)}, u32[]{:S(2)}, u32[]{:S(2)}) collective-permute-start(bf16[2,1024,128]{2,1,0:T(8,128)(2,1)S(1)} %collective-permute-done.6.refs_1_), channel_id=1, source_target_pairs={{8,0},{12,4},{16,8},{20,12},{24,16},{28,20},{9,1},{13,5},{17,9},{2... | collective-permute-start | bytes 1572872 | tf_op jit(solution)/shard_map/ppermute | solution.py:251
  105.1 2.8 %attend.5 = (bf16[2,1024,128]{2,1,0:T(8,128)(2,1)S(1)}, f32[2,1024,128]{2,1,0:T(8,128)S(1)}, f32[2,1024,128]{2,1,0:T(8,128)S(1)}) custom-call(s32[5]{0:T(128)S(1)} %stack.109.ids, s32[8192]{0:T(1024)S(1)} %all_gather.3.segs, f32[8,1024]{1,0:T(8,128)S(1)} %reshape.5.seg_rows, bf16[2,1024,128]{2,1,0:T(8,128)(2,1)S(1)} %collective-permute-done.2.refs_0_, ...), custom_call_target="tpu_custom_call" | custom-call | flops 5368709120 | bytes 7340032 | tf_op jit(solution)/shard_map/attend/pallas_call | solution.py:166
  107.9 1.0 copy-done.12
  108.9 1.3 collective-permute-start.4
  110.1 2.8 %attend.6 = (bf16[2,1024,128]{2,1,0:T(8,128)(2,1)S(1)}, f32[2,1024,128]{2,1,0:T(8,128)S(1)}, f32[2,1024,128]{2,1,0:T(8,128)S(1)}) custom-call(s32[5]{0:T(128)S(1)} %stack.114.ids, s32[8192]{0:T(1024)S(1)} %all_gather.3.segs, f32[8,1024]{1,0:T(8,128)S(1)} %reshape.5.seg_rows, bf16[2,1024,128]{2,1,0:T(8,128)(2,1)S(1)} %collective-permute-done.5.refs_0_, ...), custom_call_target="tpu_custom_call" | custom-call | flops 5368709120 | bytes 7340032 | tf_op jit(solution)/shard_map/attend/pallas_call | solution.py:166
  112.9 1.5 collective-permute-start.7
  114.4 2.3 %collective-permute-done.9.refs_1_ = bf16[2,1024,128]{2,1,0:T(8,128)(2,1)S(1)} collective-permute-done((bf16[2,1024,128]{2,1,0:T(8,128)(2,1)S(1)}, bf16[2,1024,128]{2,1,0:T(8,128)(2,1)S(1)}, u32[]{:S(2)}, u32[]{:S(2)}) %collective-permute-start.9) | collective-permute-done | bytes 524320 | tf_op jit(solution)/shard_map/ppermute | solution.py:251
  116.7 3.1 %attend.7 = (bf16[2,1024,128]{2,1,0:T(8,128)(2,1)S(1)}, bf16[2,1024,128]{2,1,0:T(8,128)(2,1)S(1)}, bf16[2,1024,128]{2,1,0:T(8,128)(2,1)}) custom-call(s32[5]{0:T(128)S(1)} %stack.119.ids, s32[8192]{0:T(1024)S(1)} %all_gather.3.segs, f32[8,1024]{1,0:T(8,128)S(1)} %reshape.5.seg_rows, bf16[2,1024,128]{2,1,0:T(8,128)(2,1)S(1)} %collective-permute-done.8.refs_0_, ...), custom_call_target="tpu_custom_call" | custom-call | flops 5368709120 | bytes 7340032 | tf_op jit(solution)/shard_map/attend/pallas_call | solution.py:166
  119.9 1.3 collective-permute-start.10
  121.2 0.1 collective-permute-start.12
  121.3 14.9 %collective-permute-done.4 = bf16[2,1024,128]{2,1,0:T(8,128)(2,1)S(1)} collective-permute-done((bf16[2,1024,128]{2,1,0:T(8,128)(2,1)S(1)}, bf16[2,1024,128]{2,1,0:T(8,128)(2,1)S(1)}, u32[]{:S(2)}, u32[]{:S(2)}) %collective-permute-start.4) | collective-permute-done | bytes 524320 | tf_op jit(solution)/shard_map/ppermute | solution.py:251
  136.2 28.8 %collective-permute-done.7 = bf16[2,1024,128]{2,1,0:T(8,128)(2,1)S(1)} collective-permute-done((bf16[2,1024,128]{2,1,0:T(8,128)(2,1)S(1)}, bf16[2,1024,128]{2,1,0:T(8,128)(2,1)S(1)}, u32[]{:S(2)}, u32[]{:S(2)}) %collective-permute-start.7) | collective-permute-done | bytes 524320 | tf_op jit(solution)/shard_map/ppermute | solution.py:251
  165.0 0.3 add_convert_fusion
  165.3 0.7 slice_bitcast_fusion
  166.1 6.6 %collective-permute-done.11.query_other = bf16[1024,128]{1,0:T(8,128)(2,1)} collective-permute-done((bf16[1024,128]{1,0:T(8,128)(2,1)}, bf16[1024,128]{1,0:T(8,128)(2,1)}, u32[]{:S(2)}, u32[]{:S(2)}) %collective-permute-start.11) | collective-permute-done | bytes 262176 | tf_op jit(solution)/shard_map/ppermute | solution.py:248
  172.7 4.4 %project.3 = bf16[2,1024,256]{2,1,0:T(8,128)(2,1)} custom-call(s32[3]{0:T(128)S(1)} %pad_add_fusion.1.place, bf16[1024,128]{1,0:T(8,128)(2,1)S(1)} %get-tuple-element.40.query_own, bf16[2,1024,128]{2,1,0:T(8,128)(2,1)S(1)} %get-tuple-element.36.key_own, bf16[1024,128]{1,0:T(8,128)(2,1)} %collective-permute-done.11.query_other, ...), custom_call_target="tpu_custom_call" | custom-call | flops 1073741824 | bytes 4194304 | tf_op jit(solution)/shard_map/project/pallas_call | solution.py:219
  177.1 3.6 %project.2 = f32[2,1024,256]{2,1,0:T(8,128)S(1)} custom-call(s32[3]{0:T(128)S(1)} %pad_add_fusion.place, bf16[1024,128]{1,0:T(8,128)(2,1)S(1)} %get-tuple-element.40.query_own, bf16[2,1024,128]{2,1,0:T(8,128)(2,1)S(1)} %get-tuple-element.36.key_own, bf16[1024,128]{1,0:T(8,128)(2,1)} %collective-permute-done.11.query_other, ...), custom_call_target="tpu_custom_call" | custom-call | flops 1073741824 | bytes 4194304 | tf_op jit(solution)/shard_map/project/pallas_call | solution.py:219
  180.7 1.5 convert_add_fusion
  182.2 1.6 collective-permute-start.14
  183.8 12.8 %collective-permute-done.14 = bf16[1,1024,256]{2,1,0:T(8,128)(2,1)S(1)} collective-permute-done((bf16[1,1024,256]{2,1,0:T(8,128)(2,1)S(1)}, bf16[1,1024,256]{2,1,0:T(8,128)(2,1)S(1)}, u32[]{:S(2)}, u32[]{:S(2)}) %collective-permute-start.14) | collective-permute-done | bytes 524320 | tf_op jit(solution)/shard_map/ppermute | solution.py:297
  196.6 1.0 fusion.1
  (31 shorter events, 0.3 us)
Async XLA Ops:
  0.0 42.0 %copy-start.13 = (s32[1024]{0:T(1024)S(1)}, s32[1024]{0:T(1024)}, u32[]{:S(2)}) copy-start(s32[1024]{0:T(1024)} %param.14) | copy-start | bytes 12292
  0.0 1.1 copy-start.1
  1.1 1.0 copy-start.2
  2.1 1.0 copy-start.3
  3.1 1.0 copy-start.4
  4.2 1.0 copy-start.5
  5.2 1.0 copy-start.6
  9.1 13.7 %collective-permute-start = (bf16[2,1024,128]{2,1,0:T(8,128)(2,1)S(1)}, bf16[2,1024,128]{2,1,0:T(8,128)(2,1)S(1)}, u32[]{:S(2)}, u32[]{:S(2)}) collective-permute-start(bf16[2,1024,128]{2,1,0:T(8,128)(2,1)S(1)} %get-tuple-element.23), channel_id=1, source_target_pairs={{0,4},{4,0},{8,12},{12,8},{16,20},{20,16},{24,28},{28,24},{1,5},{5... | collective-permute-start | bytes 1572872 | tf_op jit(solution)/shard_map/ppermute | solution.py:248
  10.6 17.6 %collective-permute-start.2 = (bf16[2,1024,128]{2,1,0:T(8,128)(2,1)S(1)}, bf16[2,1024,128]{2,1,0:T(8,128)(2,1)S(1)}, u32[]{:S(2)}, u32[]{:S(2)}) collective-permute-start(bf16[2,1024,128]{2,1,0:T(8,128)(2,1)S(1)} %get-tuple-element.22.refs_0_), channel_id=1, source_target_pairs={{8,0},{12,4},{16,8},{20,12},{24,16},{28,20},{9,1},{13,5},{17,9},{2... | collective-permute-start | bytes 1572872 | tf_op jit(solution)/shard_map/ppermute | solution.py:251
  13.0 0.8 copy-start.7
  22.7 14.7 %collective-permute-start.3 = (bf16[2,1024,128]{2,1,0:T(8,128)(2,1)S(1)}, bf16[2,1024,128]{2,1,0:T(8,128)(2,1)}, u32[]{:S(2)}, u32[]{:S(2)}) collective-permute-start(bf16[2,1024,128]{2,1,0:T(8,128)(2,1)S(1)} %collective-permute-done.refs_1_), channel_id=1, source_target_pairs={{8,0},{12,4},{16,8},{20,12},{24,16},{28,20},{9,1},{13,5},{17,9},{2... | collective-permute-start | bytes 1572872 | tf_op jit(solution)/shard_map/ppermute | solution.py:251
  25.9 0.8 copy-start.9
  26.7 57.1 %collective-permute-start.1 = (bf16[2,1024,128]{2,1,0:T(8,128)(2,1)}, bf16[2,1024,128]{2,1,0:T(8,128)(2,1)S(1)}, u32[]{:S(2)}, u32[]{:S(2)}) collective-permute-start(bf16[2,1024,128]{2,1,0:T(8,128)(2,1)} %get-tuple-element.25), channel_id=1, source_target_pairs={{0,4},{4,0},{8,12},{12,8},{16,20},{20,16},{24,28},{28,24},{1,5},{5... | collective-permute-start | bytes 1572872 | tf_op jit(solution)/shard_map/ppermute | solution.py:248
  28.2 71.9 %collective-permute-start.5 = (bf16[2,1024,128]{2,1,0:T(8,128)(2,1)S(1)}, bf16[2,1024,128]{2,1,0:T(8,128)(2,1)S(1)}, u32[]{:S(2)}, u32[]{:S(2)}) collective-permute-start(bf16[2,1024,128]{2,1,0:T(8,128)(2,1)S(1)} %collective-permute-done.2.refs_0_), channel_id=1, source_target_pairs={{8,0},{12,4},{16,8},{20,12},{24,16},{28,20},{9,1},{13,5},{17,9},{2... | collective-permute-start | bytes 1572872 | tf_op jit(solution)/shard_map/ppermute | solution.py:251
  37.5 63.9 %collective-permute-start.6 = (bf16[2,1024,128]{2,1,0:T(8,128)(2,1)}, bf16[2,1024,128]{2,1,0:T(8,128)(2,1)S(1)}, u32[]{:S(2)}, u32[]{:S(2)}) collective-permute-start(bf16[2,1024,128]{2,1,0:T(8,128)(2,1)} %collective-permute-done.3.refs_1_), channel_id=1, source_target_pairs={{8,0},{12,4},{16,8},{20,12},{24,16},{28,20},{9,1},{13,5},{17,9},{2... | collective-permute-start | bytes 1572872 | tf_op jit(solution)/shard_map/ppermute | solution.py:251
  83.7 1.0 copy-start.8
  84.8 1.0 copy-start.10
  99.1 1.0 copy-start.11
  100.1 14.3 %collective-permute-start.8 = (bf16[2,1024,128]{2,1,0:T(8,128)(2,1)S(1)}, bf16[2,1024,128]{2,1,0:T(8,128)(2,1)S(1)}, u32[]{:S(2)}, u32[]{:S(2)}) collective-permute-start(bf16[2,1024,128]{2,1,0:T(8,128)(2,1)S(1)} %collective-permute-done.5.refs_0_), channel_id=1, source_target_pairs={{8,0},{12,4},{16,8},{20,12},{24,16},{28,20},{9,1},{13,5},{17,9},{2... | collective-permute-start | bytes 1572872 | tf_op jit(solution)/shard_map/ppermute | solution.py:251
  101.4 15.3 %collective-permute-start.9 = (bf16[2,1024,128]{2,1,0:T(8,128)(2,1)S(1)}, bf16[2,1024,128]{2,1,0:T(8,128)(2,1)S(1)}, u32[]{:S(2)}, u32[]{:S(2)}) collective-permute-start(bf16[2,1024,128]{2,1,0:T(8,128)(2,1)S(1)} %collective-permute-done.6.refs_1_), channel_id=1, source_target_pairs={{8,0},{12,4},{16,8},{20,12},{24,16},{28,20},{9,1},{13,5},{17,9},{2... | collective-permute-start | bytes 1572872 | tf_op jit(solution)/shard_map/ppermute | solution.py:251
  107.9 1.0 copy-start.12
  108.9 27.4 %collective-permute-start.4 = (bf16[2,1024,128]{2,1,0:T(8,128)(2,1)S(1)}, bf16[2,1024,128]{2,1,0:T(8,128)(2,1)S(1)}, u32[]{:S(2)}, u32[]{:S(2)}) collective-permute-start(bf16[2,1024,128]{2,1,0:T(8,128)(2,1)S(1)} %get-tuple-element.29), channel_id=1, source_target_pairs={{0,8},{4,12},{8,16},{12,20},{16,24},{20,28},{1,9},{5,13},{9,17},{1... | collective-permute-start | bytes 1572872 | tf_op jit(solution)/shard_map/ppermute | solution.py:251
  112.9 52.0 %collective-permute-start.7 = (bf16[2,1024,128]{2,1,0:T(8,128)(2,1)S(1)}, bf16[2,1024,128]{2,1,0:T(8,128)(2,1)S(1)}, u32[]{:S(2)}, u32[]{:S(2)}) collective-permute-start(bf16[2,1024,128]{2,1,0:T(8,128)(2,1)S(1)} %get-tuple-element.32), channel_id=1, source_target_pairs={{0,16},{4,20},{8,24},{12,28},{1,17},{5,21},{9,25},{13,29},{2,18},{... | collective-permute-start | bytes 1572872 | tf_op jit(solution)/shard_map/ppermute | solution.py:251
  119.9 45.1 %collective-permute-start.10 = (bf16[2,1024,128]{2,1,0:T(8,128)(2,1)S(1)}, bf16[2,1024,128]{2,1,0:T(8,128)(2,1)S(1)}, u32[]{:S(2)}, u32[]{:S(2)}) collective-permute-start(bf16[2,1024,128]{2,1,0:T(8,128)(2,1)S(1)} %get-tuple-element.35), channel_id=1, source_target_pairs={{0,24},{4,28},{1,25},{5,29},{2,26},{6,30},{3,27},{7,31}} | collective-permute-start | bytes 1572872 | tf_op jit(solution)/shard_map/ppermute | solution.py:251
  121.2 44.9 %collective-permute-start.12 = (bf16[2,1024,128]{2,1,0:T(8,128)(2,1)}, bf16[2,1024,128]{2,1,0:T(8,128)(2,1)}, u32[]{:S(2)}, u32[]{:S(2)}) collective-permute-start(bf16[2,1024,128]{2,1,0:T(8,128)(2,1)} %get-tuple-element.37), channel_id=1, source_target_pairs={{0,4},{4,0},{8,12},{12,8},{16,20},{20,16},{24,28},{28,24},{1,5},{5... | collective-permute-start | bytes 1572872 | tf_op jit(solution)/shard_map/ppermute | solution.py:248
  165.0 7.7 %copy-start = (bf16[4,1024,256]{2,1,0:T(8,128)(2,1)S(1)}, bf16[4,1024,256]{2,1,0:T(8,128)(2,1)}, u32[]{:S(2)}) copy-start(bf16[4,1024,256]{2,1,0:T(8,128)(2,1)} %weights.3) | copy-start | bytes 6291460
  166.0 6.7 %collective-permute-start.11 = (bf16[1024,128]{1,0:T(8,128)(2,1)}, bf16[1024,128]{1,0:T(8,128)(2,1)}, u32[]{:S(2)}, u32[]{:S(2)}) collective-permute-start(bf16[1024,128]{1,0:T(8,128)(2,1)} %get-tuple-element.39), channel_id=1, source_target_pairs={{0,4},{4,0},{8,12},{12,8},{16,20},{20,16},{24,28},{28,24},{1,5},{5... | collective-permute-start | bytes 786440 | tf_op jit(solution)/shard_map/ppermute | solution.py:248
  177.0 3.6 %collective-permute-start.13 = (bf16[2,1024,256]{2,1,0:T(8,128)(2,1)}, bf16[2,1024,256]{2,1,0:T(8,128)(2,1)}, u32[]{:S(2)}, u32[]{:S(2)}) collective-permute-start(bf16[2,1024,256]{2,1,0:T(8,128)(2,1)} %project.3), channel_id=1, source_target_pairs={{0,1},{1,0},{2,3},{3,2},{4,5},{5,4},{6,7},{7,6},{8,9},{9,8},{10,11... | collective-permute-start | bytes 3145736 | tf_op jit(solution)/shard_map/ppermute | solution.py:297
  182.2 14.4 %collective-permute-start.14 = (bf16[1,1024,256]{2,1,0:T(8,128)(2,1)S(1)}, bf16[1,1024,256]{2,1,0:T(8,128)(2,1)S(1)}, u32[]{:S(2)}, u32[]{:S(2)}) collective-permute-start(bf16[1,1024,256]{2,1,0:T(8,128)(2,1)S(1)} %slice.29), channel_id=1, source_target_pairs={{0,2},{1,3},{2,0},{3,1},{4,6},{5,7},{6,4},{7,5},{8,10},{9,11},{10,... | collective-permute-start | bytes 1572872 | tf_op jit(solution)/shard_map/ppermute | solution.py:297

commit v2 on v1

v2 whole, which is shorter than its diff:
```python
import functools

import jax
import jax.numpy as jnp
from jax import lax
from jax.experimental import pallas as pl
from jax.experimental.pallas import tpu as pltpu
from jax.sharding import PartitionSpec as P

HEAD_DIM = 128
WINDOW = 6
PAIR = 2
TILE = 512
CHUNK = 256
SCALE = HEAD_DIM ** (-0.5)
VMEM_BYTES = 60 * 2**20
BF16 = jnp.bfloat16
F32 = jnp.float32


def dot(left, right, dims):
    return lax.dot_general(left, right, (dims, ((), ())), preferred_element_type=F32)


def prepare_kernel(
    shards, queries, keys, values, attn_out, gate_pre, out_grad, segments,
    query_own, query_other, key_own, key_other, gate_grad, seg_all, send_sems, recv_sems,
):
    me = lax.axis_index("seq")
    lane = lax.rem(me, PAIR)
    step = pl.program_id(0)

    def seg_copies():
        return [
            pltpu.make_async_remote_copy(
                src_ref=segments,
                dst_ref=seg_all.at[me],
                send_sem=send_sems.at[offset],
                recv_sem=recv_sems.at[offset],
                device_id={"seq": lax.rem(me + offset, shards)},
                device_id_type=pl.DeviceIdType.MESH,
            )
            for offset in range(1, shards)
        ]

    @pl.when(step == 0)
    def _():
        barrier = pltpu.get_barrier_semaphore()
        for offset in range(1, shards):
            pl.semaphore_signal(
                barrier,
                inc=1,
                device_id={"seq": lax.rem(me + offset, shards)},
                device_id_type=pl.DeviceIdType.MESH,
            )

    @pl.when(step == 1)
    def _():
        pl.semaphore_wait(pltpu.get_barrier_semaphore(), shards - 1)
        for copy in seg_copies():
            copy.start()
        own = pltpu.make_async_copy(segments, seg_all.at[me], send_sems.at[0])
        own.start()
        own.wait()

    for slot, (to_query, to_key) in enumerate(((query_own, key_own), (query_other, key_other))):
        head = lane if slot == 0 else 1 - lane
        cols = pl.ds(pl.multiple_of(head * HEAD_DIM, HEAD_DIM), HEAD_DIM)
        to_query[0] = queries[:, cols]
        to_key[0] = keys[:, cols]
        to_key[1] = values[:, cols]
        saved = attn_out[:, cols].astype(F32)
        centred = saved - jnp.mean(saved, axis=-1, keepdims=True)
        inverse = lax.rsqrt(jnp.mean(centred * centred, axis=-1, keepdims=True) + 1e-06)
        normed = centred * inverse
        gate_in = gate_pre[:, cols].astype(F32)
        grad_in = out_grad[:, cols].astype(F32)
        sigma = jax.nn.sigmoid(gate_in)
        gate_grad[:, cols] = (
            grad_in * normed * (sigma * (1.0 + gate_in * (1.0 - sigma)))
        ).astype(BF16)
        normed_grad = grad_in * (gate_in * sigma)
        to_query[1] = (
            inverse
            * (
                normed_grad
                - jnp.mean(normed_grad, axis=-1, keepdims=True)
                - normed * jnp.mean(normed_grad * normed, axis=-1, keepdims=True)
            )
        ).astype(BF16)

    @pl.when(step == pl.num_programs(0) - 1)
    def _():
        for copy in seg_copies():
            copy.wait()


def prepare(shards, queries, keys, values, attn_out, gate_pre, out_grad, segments):
    rows, width = queries.shape
    step = min(rows // 2, 256)
    wide = pl.BlockSpec((step, width), lambda i: (i, 0))
    pair = pl.BlockSpec((2, step, HEAD_DIM), lambda i: (0, i, 0))
    pair_shape = jax.ShapeDtypeStruct((2, rows, HEAD_DIM), BF16)
    any_spec = pl.BlockSpec(memory_space=pl.ANY)
    return pl.pallas_call(
        functools.partial(prepare_kernel, shards),
        grid=(rows // step,),
        in_specs=[wide] * 6 + [any_spec],
        out_specs=[pair] * 4 + [wide, any_spec],
        out_shape=[pair_shape] * 4
        + [
            jax.ShapeDtypeStruct((rows, width), BF16),
            jax.ShapeDtypeStruct((shards,) + segments.shape, segments.dtype),
        ],
        scratch_shapes=[
            pltpu.SemaphoreType.DMA((shards,)),
            pltpu.SemaphoreType.DMA((shards,)),
        ],
        compiler_params=pltpu.CompilerParams(
            vmem_limit_bytes=VMEM_BYTES, collective_id=0, has_side_effects=True
        ),
        cost_estimate=pl.CostEstimate(
            flops=40 * rows * width, bytes_accessed=22 * rows * width, transcendentals=rows * width
        ),
        name="prepare",
    )(queries, keys, values, attn_out, gate_pre, out_grad, segments)


def attend_kernel(first, last, ids, segs, seg_rows, *refs):
    refs = list(refs)
    sources = [refs.pop(0) for _ in range(4 if first else 6)]
    query_own, query_other, own_out, other_out, query_in, key_in, key_acc, query_acc, sems = refs
    rows = query_in.shape[2]
    per = rows // TILE
    count = 2 * per

    targets = [query_in.at[0], query_in.at[1], key_in.at[0], key_in.at[1]]
    if not first:
        targets += [key_acc.at[0], key_acc.at[1]]
    copies = [
        pltpu.make_async_copy(source, target, sems.at[n])
        for n, (source, target) in enumerate(zip(sources, targets))
    ]
    for copy in copies:
        copy.start()
    query_acc[...] = jnp.zeros_like(query_acc)
    if first:
        key_acc[...] = jnp.zeros_like(key_acc)
    for copy in copies:
        copy.wait()

    def body(index, carry):
        q_idx, k_idx = index // count, index % count
        q_blk, k_blk = q_idx // per, k_idx // per
        q_off = pl.multiple_of((q_idx % per) * TILE, TILE)
        k_off = pl.multiple_of((k_idx % per) * TILE, TILE)
        q_shard, k_shard = ids[q_blk], ids[2 + k_blk]
        q_first, k_first = q_shard * rows + q_off, k_shard * rows + k_off
        q_last, k_last = q_first + TILE - 1, k_first + TILE - 1
        live = (ids[4] > 0) & (k_first <= q_last) & (segs[k_last] >= segs[q_first])
        full = (k_last <= q_first) & (segs[k_first] == segs[q_last])
        q_rows = pl.ds(q_off, TILE)

        def work(masked):
            query = query_in[q_blk, 0, q_rows, :]
            grad = query_in[q_blk, 1, q_rows, :]
            if masked:
                seg_q = seg_rows[pl.ds(q_shard, 1), q_rows]
                place_q = q_first + lax.broadcasted_iota(jnp.int32, (CHUNK, TILE), 1)

            def products(chunk):
                spot = pl.ds(k_off + chunk * CHUNK, CHUNK)
                key = key_in[k_blk, 0, spot, :]
                value = key_in[k_blk, 1, spot, :]
                return (
                    spot,
                    key,
                    dot(key, query, ((1,), (1,))),
                    dot(value, grad, ((1,), (1,))),
                )

            chunks = TILE // CHUNK
            ready, query_part = products(0), None
            for chunk in range(chunks):
                spot, key, scores, slope_in = ready
                if chunk + 1 < chunks:
                    ready = products(chunk + 1)
                half = scores * (SCALE / 2)
                tanh = jnp.tanh(half)
                upper = 1.0 + tanh
                weights = half * upper
                score_grad = slope_in * (upper + weights * (1.0 - tanh))
                if masked:
                    seg_k = seg_rows[pl.ds(k_shard, 1), spot]
                    seg_k = jnp.transpose(jnp.broadcast_to(seg_k, (HEAD_DIM, CHUNK)))[:, :1]
                    place_k = (k_first + chunk * CHUNK) + lax.broadcasted_iota(
                        jnp.int32, (CHUNK, TILE), 0
                    )
                    allowed = (seg_q == seg_k) & (place_k <= place_q)
                    weights = jnp.where(allowed, weights, 0.0)
                    score_grad = jnp.where(allowed, score_grad, 0.0)
                weights = weights.astype(BF16)
                score_grad = score_grad.astype(BF16)
                key_acc[k_blk, 0, spot, :] += dot(score_grad, query, ((1,), (0,)))
                key_acc[k_blk, 1, spot, :] += dot(weights, grad, ((1,), (0,)))
                part = dot(score_grad, key, ((0,), (0,)))
                query_part = part if query_part is None else query_part + part
            query_acc[q_blk, q_rows, :] += query_part

        @pl.when(live & full)
        def _():
            work(False)

        @pl.when(live & jnp.logical_not(full))
        def _():
            work(True)

        return carry

    lax.fori_loop(0, count * count, body, 0)
    for blk, out in enumerate((query_own, query_other)):
        out[...] = (query_acc[blk] * (SCALE / 2)).astype(out.dtype)
    for blk, out in enumerate((own_out, other_out)):
        if last:
            out[0] = (key_acc[blk, 0] * (SCALE / 2)).astype(BF16)
            out[1] = key_acc[blk, 1].astype(BF16)
        else:
            out[...] = key_acc[blk]


def attend(first, last, ids, segs, seg_rows, queries, keys, acc):
    rows = queries[0].shape[1]
    any_spec = pl.BlockSpec(memory_space=pl.ANY)
    vmem = pl.BlockSpec(memory_space=pltpu.VMEM)
    acc = () if first else tuple(acc)
    acc_shape = jax.ShapeDtypeStruct((2, rows, HEAD_DIM), BF16 if last else F32)
    pairs = (2 * rows) ** 2
    return pl.pallas_call(
        functools.partial(attend_kernel, first, last),
        grid_spec=pltpu.PrefetchScalarGridSpec(
            num_scalar_prefetch=2,
            grid=(),
            in_specs=[vmem] + [any_spec] * (4 + len(acc)),
            out_specs=[vmem] * 4,
            scratch_shapes=[
                pltpu.VMEM((2, 2, rows, HEAD_DIM), BF16),
                pltpu.VMEM((2, 2, rows, HEAD_DIM), BF16),
                pltpu.VMEM((2, 2, rows, HEAD_DIM), F32),
                pltpu.VMEM((2, rows, HEAD_DIM), F32),
                pltpu.SemaphoreType.DMA((6,)),
            ],
        ),
        out_shape=[
            jax.ShapeDtypeStruct((rows, HEAD_DIM), F32 if first else BF16),
            jax.ShapeDtypeStruct((rows, HEAD_DIM), BF16),
            acc_shape,
            acc_shape,
        ],
        compiler_params=pltpu.CompilerParams(vmem_limit_bytes=VMEM_BYTES),
        cost_estimate=pl.CostEstimate(
            flops=10 * pairs * HEAD_DIM, bytes_accessed=14 * rows * HEAD_DIM * 4, transcendentals=pairs
        ),
        name="attend",
    )(ids, segs, seg_rows, *queries, *keys, *acc)


def project_early_kernel(place, key_own, key_other, gate_grad, weights, out, stacked):
    @pl.when(pl.program_id(0) == 0)
    def _():
        own = pl.ds(pl.multiple_of(place[0] * HEAD_DIM, HEAD_DIM), HEAD_DIM)
        other = pl.ds(pl.multiple_of((1 - place[0]) * HEAD_DIM, HEAD_DIM), HEAD_DIM)
        for part in range(2):
            stacked[part, :, own] = key_own[part]
            stacked[part, :, other] = key_other[part]

    out[0] = (
        dot(stacked[0], weights[1], ((1,), (1,)))
        + dot(stacked[1], weights[2], ((1,), (1,)))
        + dot(gate_grad[...], weights[3], ((1,), (1,)))
    )


def project_late_kernel(place, query_own, query_other, early, weights, out, stacked):
    @pl.when(pl.program_id(0) == 0)
    def _():
        own = pl.ds(pl.multiple_of(place[0] * HEAD_DIM, HEAD_DIM), HEAD_DIM)
        other = pl.ds(pl.multiple_of((1 - place[0]) * HEAD_DIM, HEAD_DIM), HEAD_DIM)
        stacked[:, own] = query_own[...]
        stacked[:, other] = query_other[...]

    out[0] = (early[0] + dot(stacked[...], weights[0], ((1,), (1,)))).astype(out.dtype)


def project(place, skip, count, grads, early, projections, dtype):
    width = projections.shape[2]
    rows = grads[0].shape[-2]
    whole = lambda array: pl.BlockSpec(array.shape, lambda i, place: (0,) * array.ndim)
    if early is None:
        kernel, deep, stacked = project_early_kernel, 4, (2, rows, width)
        partial = []
    else:
        kernel, deep, stacked = project_late_kernel, 1, (rows, width)
        partial = [pl.BlockSpec((1, rows, width), lambda i, place: (skip + i, 0, 0))]
    return pl.pallas_call(
        kernel,
        grid_spec=pltpu.PrefetchScalarGridSpec(
            num_scalar_prefetch=1,
            grid=(count,),
            in_specs=[whole(grad) for grad in grads]
            + partial
            + [pl.BlockSpec((deep, width, width), lambda i, place: (0, place[1 + skip + i], 0))],
            out_specs=pl.BlockSpec((1, rows, width), lambda i, place: (i, 0, 0)),
            scratch_shapes=[pltpu.VMEM(stacked, BF16)],
        ),
        out_shape=jax.ShapeDtypeStruct((count, rows, width), dtype),
        compiler_params=pltpu.CompilerParams(vmem_limit_bytes=VMEM_BYTES),
        cost_estimate=pl.CostEstimate(
            flops=2 * deep * count * rows * width * width,
            bytes_accessed=rows * width * (8 + 4 * count),
            transcendentals=0,
        ),
        name="project_early" if early is None else "project_late",
    )(place, *grads, *([] if early is None else [early]), projections)


def per_device(queries, key_rows, value_rows, attn_out, gate_pre, out_grad, segments, projections):
    rows = queries.shape[0]
    shards, groups = lax.axis_size("seq"), lax.axis_size("head")
    shard, group = lax.axis_index("seq"), lax.axis_index("head")
    pairs = shards // PAIR
    pair, lane = shard // PAIR, shard % PAIR

    def shift(block, distance, cross=0):
        route = [(i, (i + PAIR * distance) ^ cross) for i in range(shards)]
        return lax.ppermute(block, "seq", [hop for hop in route if 0 <= hop[1] < shards])

    query_own, query_other, key_own, key_other, gate_grad, seg_all = prepare(
        shards, queries, key_rows, value_rows, attn_out, gate_pre, out_grad,
        segments.reshape(-1, HEAD_DIM),
    )
    segs = seg_all.reshape(shards * rows)
    seg_rows = seg_all.reshape(shards, rows).astype(F32)
    block_a, block_b = query_own, shift(query_other, 0, 1)
    keys = (key_own, shift(key_other, 0, 1))

    reach = min((WINDOW + 1) // PAIR, pairs - 1)
    acc, own_sum, other_sum = None, None, None
    for distance in range(reach + 1):
        if distance > 0:
            block_a, block_b = shift(block_a, -1), shift(block_b, -1)
        far = PAIR * jnp.minimum(pair + distance, pairs - 1)
        ids = jnp.stack(
            [far + lane, far + 1 - lane, shard, shard ^ 1, (pair + distance < pairs)]
        ).astype(jnp.int32)
        part_own, part_other, acc_own, acc_other = attend(
            distance == 0, distance == reach, ids, segs, seg_rows, (block_a, block_b), keys, acc
        )
        acc = (acc_own, acc_other)
        part_other = shift(part_other, distance, 1).astype(F32)
        if distance == 0:
            own_sum, other_sum = part_own, part_other
        else:
            own_sum = own_sum + shift(part_own, distance).astype(F32)
            other_sum = other_sum + part_other
    late = (own_sum.astype(BF16), other_sum.astype(BF16))
    early = (acc[0], shift(acc[1], 0, 1), gate_grad)

    bits = []
    while (1 << len(bits)) < groups:
        bits.append(1 << len(bits))
    kept = list(range(groups))

    def across(block, bit):
        return lax.ppermute(block, "head", [(i, i ^ bit) for i in range(groups)])

    sent = [offset for offset in kept if offset & 1 == 1]
    near = [offset for offset in kept if offset & 1 == 0]
    place = jnp.stack([lane] + [group ^ offset for offset in sent + near]).astype(jnp.int32)
    base = project(place, 0, groups, early, None, projections, F32)
    away = project(place, 0, len(sent), late, base, projections, BF16)
    arrived = across(away, 1)
    total = project(place, len(sent), len(near), late, base, projections, F32)
    total = total + arrived.astype(F32)
    for bit in bits[1:]:
        sent = [n for n, offset in enumerate(near) if offset & bit]
        held = [n for n, offset in enumerate(near) if not offset & bit]
        arrived = across(jnp.stack([total[n] for n in sent]).astype(BF16), bit)
        total = jnp.stack([total[n] for n in held]) + arrived.astype(F32)
        near = [near[n] for n in held]
    return total[0].astype(BF16)


def solution(mesh):
    return jax.shard_map(
        per_device,
        mesh=mesh,
        in_specs=(
            P("seq", "head"),
            P("seq", "head"),
            P("seq", "head"),
            P("seq", "head"),
            P("seq", "head"),
            P("seq", "head"),
            P("seq"),
            P(None, None, "head"),
        ),
        out_specs=P("seq", "head"),
        check_vma=False,
    )
```

time: 202 us -> 177 us (0.88)
  the two profiles are of different devices: /device:TPU:24 before, /device:TPU:0 now
where the time goes in v2:
time: 177 us; the launch traced here: 175 us
  Pallas kernels  90.4 us (51%)
  waiting for transfers between devices  50.6 us (29%)
  starting transfers between devices  22.1 us (12%)
  local copies, waits for them, and re-layouts  6.28 us (4%)
  other arithmetic  5.24 us (3%)
    pallas_call x4, Pallas kernels, attend(): pl.pallas_call(functools.partial(attend_kernel, first, last), grid_spec=p...  64.1 us
    ppermute x16, waiting for transfers between devices, shift(): lax.ppermute(block, 'seq', [hop for hop in route if 0 <= hop[1] < shards])  37.8 us
    ppermute x16, starting transfers between devices, shift(): lax.ppermute(block, 'seq', [hop for hop in route if 0 <= hop[1] < shards])  20.5 us
    pallas_call x3, Pallas kernels, project(): pl.pallas_call(kernel, grid_spec=pltpu.PrefetchScalarGridSpec(num_scalar_...  14.2 us
    ppermute x2, waiting for transfers between devices, across(): return lax.ppermute(block, 'head', [(i, i ^ bit) for i in range(groups)])  12.8 us
    pallas_call x1, Pallas kernels, prepare(): pl.pallas_call(functools.partial(prepare_kernel, shards), grid=(rows // s...  12.1 us
  transfers between devices with their start and end apart: 18, of which 8 were waited for; matrix products, arithmetic and copies ran while one was open for 4% of the time, Pallas kernels for 39%

profile of v2, /device:TPU:0, one launch (start us, length us, event | category | flops | bytes accessed | tf_op | source)
XLA Modules:
  0.0 174.8 jit_solution(11839661907196080551)
XLA Ops:
  0.0 12.1 %prepare.1 = (bf16[2,1024,128]{2,1,0:T(8,128)(2,1)}, bf16[2,1024,128]{2,1,0:T(8,128)(2,1)}, bf16[2,1024,128]{2,1,0:T(8,128)(2,1)}, bf16[2,1024,128]{2,1,0:T(8,12...) custom-call(bf16[1024,256]{1,0:T(8,128)(2,1)} %queries.1, bf16[1024,256]{1,0:T(8,128)(2,1)} %keys.1, ...), custom_call_target="tpu_custom_call" | custom-call | flops 10485760 | bytes 5767168 | tf_op jit(solution)/shard_map/prepare/pallas_call | solution.py:105
  12.1 0.6 collective-permute-start
  12.7 1.3 collective-permute-start.2
  14.0 11.7 %collective-permute-done.refs_1_ = bf16[2,1024,128]{2,1,0:T(8,128)(2,1)S(1)} collective-permute-done((bf16[2,1024,128]{2,1,0:T(8,128)(2,1)}, bf16[2,1024,128]{2,1,0:T(8,128)(2,1)S(1)}, u32[]{:S(2)}, u32[]{:S(2)}) %collective-permute-start) | collective-permute-done | bytes 524320 | tf_op jit(solution)/shard_map/ppermute | solution.py:335
  25.8 1.3 collective-permute-start.3
  27.1 0.6 collective-permute-start.1
  27.7 0.2 collective-permute-done.2.refs_0_
  27.9 1.3 collective-permute-start.5
  29.2 13.3 %collective-permute-done.3.refs_1_ = bf16[2,1024,128]{2,1,0:T(8,128)(2,1)S(1)} collective-permute-done((bf16[2,1024,128]{2,1,0:T(8,128)(2,1)S(1)}, bf16[2,1024,128]{2,1,0:T(8,128)(2,1)S(1)}, u32[]{:S(2)}, u32[]{:S(2)}) %collective-permute-start.3) | collective-permute-done | bytes 524320 | tf_op jit(solution)/shard_map/ppermute | solution.py:335
  42.5 1.3 collective-permute-start.6
  43.8 0.8 convert_bitcast_fusion
  44.6 0.6 copy.11
  45.2 0.6 stack.102.ids
  45.8 0.6 stack.107.ids
  46.4 0.6 stack.112.ids
  47.0 0.6 stack.117.ids
  47.6 0.8 copy-done.1
  48.4 16.7 %attend.4 = (f32[1024,128]{1,0:T(8,128)}, bf16[1024,128]{1,0:T(8,128)(2,1)}, f32[2,1024,128]{2,1,0:T(8,128)}, f32[2,1024,128]{2,1,0:T(8,128)}) custom-call(s32[5]{0:T(128)} %stack.102.ids, s32[8192]{0:T(1024)} %bitcast.28, f32[8,1024]{1,0:T(8,128)} %bitcast.32, bf16[2,1024,128]{2,1,0:T(8,128)(2,1)} %get-tuple-element.28.refs_0_, ...), custom_call_target="tpu_custom_call" | custom-call | flops 5368709120 | bytes 7340032 | tf_op jit(solution)/shard_map/attend/pallas_call | solution.py:238
  65.2 0.6 collective-permute-start.11
  65.8 1.3 collective-permute-start.8
  67.1 1.3 collective-permute-start.9
  68.4 22.5 %attend.5 = (bf16[1024,128]{1,0:T(8,128)(2,1)}, bf16[1024,128]{1,0:T(8,128)(2,1)}, f32[2,1024,128]{2,1,0:T(8,128)}, f32[2,1024,128]{2,1,0:T(8,128)}) custom-call(s32[5]{0:T(128)} %stack.107.ids, s32[8192]{0:T(1024)} %bitcast.29, f32[8,1024]{1,0:T(8,128)} %bitcast.33, bf16[2,1024,128]{2,1,0:T(8,128)(2,1)} %copy-done.3, bf16[2,1024,128]{2,1,0:T(8,128)(2,1)} %copy-done.5, ...), custom_call_target="tpu_custom_call" | custom-call | flops 5368709120 | bytes 7340032 | tf_op jit(solution)/shard_map/attend/pallas_call | solution.py:238
  90.9 3.6 %collective-permute-start.12 = (bf16[1024,128]{1,0:T(8,128)(2,1)}, bf16[1024,128]{1,0:T(8,128)(2,1)S(1)}, u32[]{:S(2)}, u32[]{:S(2)}) collective-permute-start(bf16[1024,128]{1,0:T(8,128)(2,1)} %get-tuple-element.43), channel_id=1, source_target_pairs={{0,12},{4,8},{8,20},{12,16},{16,28},{20,24},{1,13},{5,9},{9,21},{1... | collective-permute-start | bytes 786440 | tf_op jit(solution)/shard_map/ppermute | solution.py:335
  94.5 19.3 %attend.6 = (bf16[1024,128]{1,0:T(8,128)(2,1)}, bf16[1024,128]{1,0:T(8,128)(2,1)}, f32[2,1024,128]{2,1,0:T(8,128)}, f32[2,1024,128]{2,1,0:T(8,128)}) custom-call(s32[5]{0:T(128)} %stack.112.ids, s32[8192]{0:T(1024)} %bitcast.30, f32[8,1024]{1,0:T(8,128)} %bitcast.34, bf16[2,1024,128]{2,1,0:T(8,128)(2,1)} %copy-done.2, bf16[2,1024,128]{2,1,0:T(8,128)(2,1)} %copy-done.4, ...), custom_call_target="tpu_custom_call" | custom-call | flops 5368709120 | bytes 7340032 | tf_op jit(solution)/shard_map/attend/pallas_call | solution.py:238
  113.8 1.5 collective-permute-start.13
  115.3 0.8 copy-done.8
  116.1 0.2 copy-done.9
  116.3 5.6 %attend.7 = (bf16[1024,128]{1,0:T(8,128)(2,1)}, bf16[1024,128]{1,0:T(8,128)(2,1)}, bf16[2,1024,128]{2,1,0:T(8,128)(2,1)}, bf16[2,1024,128]{2,1,0:T(8,128)(2,1)}) custom-call(s32[5]{0:T(128)} %stack.117.ids, s32[8192]{0:T(1024)} %bitcast.31, f32[8,1024]{1,0:T(8,128)} %bitcast.35, bf16[2,1024,128]{2,1,0:T(8,128)(2,1)} %copy-done.8, ...), custom_call_target="tpu_custom_call" | custom-call | flops 5368709120 | bytes 7340032 | tf_op jit(solution)/shard_map/attend/pallas_call | solution.py:238
  121.9 1.3 collective-permute-start.14
  123.2 1.3 collective-permute-start.4
  124.5 1.3 collective-permute-start.7
  125.9 1.3 collective-permute-start.10
  127.2 0.6 collective-permute-start.15
  127.8 0.6 stack.95.place
  128.4 1.8 %collective-permute-done.14 = bf16[1024,128]{1,0:T(8,128)(2,1)S(1)} collective-permute-done((bf16[1024,128]{1,0:T(8,128)(2,1)}, bf16[1024,128]{1,0:T(8,128)(2,1)S(1)}, u32[]{:S(2)}, u32[]{:S(2)}) %collective-permute-start.14) | collective-permute-done | bytes 262176 | tf_op jit(solution)/shard_map/ppermute | solution.py:335
  130.2 0.9 add_convert_fusion.query_other
  131.1 4.6 %collective-permute-done.4 = bf16[1024,128]{1,0:T(8,128)(2,1)S(1)} collective-permute-done((bf16[1024,128]{1,0:T(8,128)(2,1)S(1)}, bf16[1024,128]{1,0:T(8,128)(2,1)S(1)}, u32[]{:S(2)}, u32[]{:S(2)}) %collective-permute-start.4) | collective-permute-done | bytes 262176 | tf_op jit(solution)/shard_map/ppermute | solution.py:335
  135.7 3.1 %collective-permute-done.7 = bf16[1024,128]{1,0:T(8,128)(2,1)S(1)} collective-permute-done((bf16[1024,128]{1,0:T(8,128)(2,1)S(1)}, bf16[1024,128]{1,0:T(8,128)(2,1)S(1)}, u32[]{:S(2)}, u32[]{:S(2)}) %collective-permute-start.7) | collective-permute-done | bytes 262176 | tf_op jit(solution)/shard_map/ppermute | solution.py:335
  138.9 2.9 %collective-permute-done.10 = bf16[1024,128]{1,0:T(8,128)(2,1)S(1)} collective-permute-done((bf16[1024,128]{1,0:T(8,128)(2,1)}, bf16[1024,128]{1,0:T(8,128)(2,1)S(1)}, u32[]{:S(2)}, u32[]{:S(2)}) %collective-permute-start.10) | collective-permute-done | bytes 262176 | tf_op jit(solution)/shard_map/ppermute | solution.py:335
  141.8 0.8 add_convert_fusion.1.query_own
  142.6 0.8 copy-done.7
  143.4 6.7 %project_early.1.early = f32[4,1024,256]{2,1,0:T(8,128)} custom-call(s32[5]{0:T(128)} %stack.95.place, bf16[2,1024,128]{2,1,0:T(8,128)(2,1)} %get-tuple-element.46.key_own, bf16[2,1024,128]{2,1,0:T(8,128)(2,1)} %copy-done.7, bf16[1024,256]{1,0:T(8,128)(2,1)} %get-tuple-element.48.gate_grad, bf16[4,1024,256]{2,1,0:T(8,128)(2,1)} %weights.5), custom_call_target="tpu_custom_call" | custom-call | flops 2147483648 | bytes 6291456 | tf_op jit(solution)/shard_map/project_early/pallas_call | solution.py:304
  150.1 3.6 %project_late.3 = bf16[2,1024,256]{2,1,0:T(8,128)(2,1)} custom-call(s32[5]{0:T(128)} %stack.95.place, bf16[1024,128]{1,0:T(8,128)(2,1)} %add_convert_fusion.1.query_own, bf16[1024,128]{1,0:T(8,128)(2,1)} %add_convert_fusion.query_other, f32[4,1024,256]{2,1,0:T(8,128)} %project_early.1.early, bf16[4,1024,256]{2,1,0:T(8,128)(2,1)} %weights.5), custom_call_target="tpu_custom_call" | custom-call | flops 268435456 | bytes 4194304 | tf_op jit(solution)/shard_map/project_late/pallas_call | solution.py:304
  153.7 3.9 %project_late.2 = f32[2,1024,256]{2,1,0:T(8,128)} custom-call(s32[5]{0:T(128)} %stack.95.place, bf16[1024,128]{1,0:T(8,128)(2,1)} %add_convert_fusion.1.query_own, bf16[1024,128]{1,0:T(8,128)(2,1)} %add_convert_fusion.query_other, f32[4,1024,256]{2,1,0:T(8,128)} %project_early.1.early, bf16[4,1024,256]{2,1,0:T(8,128)(2,1)} %weights.5), custom_call_target="tpu_custom_call" | custom-call | flops 268435456 | bytes 4194304 | tf_op jit(solution)/shard_map/project_late/pallas_call | solution.py:304
  157.6 1.8 %convert_add_fusion = f32[2,1024,256]{2,1,0:T(8,128)S(1)} fusion(f32[2,1024,256]{2,1,0:T(8,128)} %project_late.2, bf16[2,1024,256]{2,1,0:T(8,128)(2,1)S(1)} %collective-permute-done.16), kind=kLoop, calls=%fused_computation | loop fusion | flops 1048576 | bytes 5242880 | tf_op jit(solution)/shard_map/add | solution.py:383
  159.5 1.6 collective-permute-start.17
  161.1 12.8 %collective-permute-done.17 = bf16[1,1024,256]{2,1,0:T(8,128)(2,1)S(1)} collective-permute-done((bf16[1,1024,256]{2,1,0:T(8,128)(2,1)S(1)}, bf16[1,1024,256]{2,1,0:T(8,128)(2,1)S(1)}, u32[]{:S(2)}, u32[]{:S(2)}) %collective-permute-start.17) | collective-permute-done | bytes 524320 | tf_op jit(solution)/shard_map/ppermute | solution.py:374
  173.9 1.0 fusion.1
  (32 shorter events, 0.1 us)
Async XLA Ops:
  12.1 13.7 %collective-permute-start = (bf16[2,1024,128]{2,1,0:T(8,128)(2,1)}, bf16[2,1024,128]{2,1,0:T(8,128)(2,1)S(1)}, u32[]{:S(2)}, u32[]{:S(2)}) collective-permute-start(bf16[2,1024,128]{2,1,0:T(8,128)(2,1)} %get-tuple-element.29), channel_id=1, source_target_pairs={{0,4},{4,0},{8,12},{12,8},{16,20},{20,16},{24,28},{28,24},{1,5},{5... | collective-permute-start | bytes 1572872 | tf_op jit(solution)/shard_map/ppermute | solution.py:335
  12.7 15.2 %collective-permute-start.2 = (bf16[2,1024,128]{2,1,0:T(8,128)(2,1)}, bf16[2,1024,128]{2,1,0:T(8,128)(2,1)S(1)}, u32[]{:S(2)}, u32[]{:S(2)}) collective-permute-start(bf16[2,1024,128]{2,1,0:T(8,128)(2,1)} %get-tuple-element.28.refs_0_), channel_id=1, source_target_pairs={{8,0},{12,4},{16,8},{20,12},{24,16},{28,20},{9,1},{13,5},{17,9},{2... | collective-permute-start | bytes 1572872 | tf_op jit(solution)/shard_map/ppermute | solution.py:335
  25.8 21.9 %copy-start.6 = (bf16[2,1024,128]{2,1,0:T(8,128)(2,1)}, bf16[2,1024,128]{2,1,0:T(8,128)(2,1)S(1)}, u32[]{:S(2)}) copy-start(bf16[2,1024,128]{2,1,0:T(8,128)(2,1)S(1)} %collective-permute-done.refs_1_) | copy-start | bytes 1572868
  25.8 16.7 %collective-permute-start.3 = (bf16[2,1024,128]{2,1,0:T(8,128)(2,1)S(1)}, bf16[2,1024,128]{2,1,0:T(8,128)(2,1)S(1)}, u32[]{:S(2)}, u32[]{:S(2)}) collective-permute-start(bf16[2,1024,128]{2,1,0:T(8,128)(2,1)S(1)} %collective-permute-done.refs_1_), channel_id=1, source_target_pairs={{8,0},{12,4},{16,8},{20,12},{24,16},{28,20},{9,1},{13,5},{17,9},{2... | collective-permute-start | bytes 1572872 | tf_op jit(solution)/shard_map/ppermute | solution.py:335
  27.1 20.6 %collective-permute-start.1 = (bf16[2,1024,128]{2,1,0:T(8,128)(2,1)}, bf16[2,1024,128]{2,1,0:T(8,128)(2,1)S(1)}, u32[]{:S(2)}, u32[]{:S(2)}) collective-permute-start(bf16[2,1024,128]{2,1,0:T(8,128)(2,1)} %get-tuple-element.31), channel_id=1, source_target_pairs={{0,4},{4,0},{8,12},{12,8},{16,20},{20,16},{24,28},{28,24},{1,5},{5... | collective-permute-start | bytes 1572872 | tf_op jit(solution)/shard_map/ppermute | solution.py:335
  27.9 37.2 %copy-start.3 = (bf16[2,1024,128]{2,1,0:T(8,128)(2,1)}, bf16[2,1024,128]{2,1,0:T(8,128)(2,1)S(1)}, u32[]{:S(2)}) copy-start(bf16[2,1024,128]{2,1,0:T(8,128)(2,1)S(1)} %collective-permute-done.2.refs_0_) | copy-start | bytes 1572868
  27.9 37.9 %collective-permute-start.5 = (bf16[2,1024,128]{2,1,0:T(8,128)(2,1)S(1)}, bf16[2,1024,128]{2,1,0:T(8,128)(2,1)S(1)}, u32[]{:S(2)}, u32[]{:S(2)}) collective-permute-start(bf16[2,1024,128]{2,1,0:T(8,128)(2,1)S(1)} %collective-permute-done.2.refs_0_), channel_id=1, source_target_pairs={{8,0},{12,4},{16,8},{20,12},{24,16},{28,20},{9,1},{13,5},{17,9},{2... | collective-permute-start | bytes 1572872 | tf_op jit(solution)/shard_map/ppermute | solution.py:335
  42.5 22.6 %copy-start.5 = (bf16[2,1024,128]{2,1,0:T(8,128)(2,1)}, bf16[2,1024,128]{2,1,0:T(8,128)(2,1)S(1)}, u32[]{:S(2)}) copy-start(bf16[2,1024,128]{2,1,0:T(8,128)(2,1)S(1)} %collective-permute-done.3.refs_1_) | copy-start | bytes 1572868
  42.5 24.6 %collective-permute-start.6 = (bf16[2,1024,128]{2,1,0:T(8,128)(2,1)S(1)}, bf16[2,1024,128]{2,1,0:T(8,128)(2,1)S(1)}, u32[]{:S(2)}, u32[]{:S(2)}) collective-permute-start(bf16[2,1024,128]{2,1,0:T(8,128)(2,1)S(1)} %collective-permute-done.3.refs_1_), channel_id=1, source_target_pairs={{8,0},{12,4},{16,8},{20,12},{24,16},{28,20},{9,1},{13,5},{17,9},{2... | collective-permute-start | bytes 1572872 | tf_op jit(solution)/shard_map/ppermute | solution.py:335
  47.6 0.8 copy-start.1
  65.2 59.4 %collective-permute-start.11 = (bf16[1024,128]{1,0:T(8,128)(2,1)}, bf16[1024,128]{1,0:T(8,128)(2,1)S(1)}, u32[]{:S(2)}, u32[]{:S(2)}) collective-permute-start(bf16[1024,128]{1,0:T(8,128)(2,1)} %get-tuple-element.42), channel_id=1, source_target_pairs={{0,4},{4,0},{8,12},{12,8},{16,20},{20,16},{24,28},{28,24},{1,5},{5... | collective-permute-start | bytes 786440 | tf_op jit(solution)/shard_map/ppermute | solution.py:335
  65.8 25.1 %copy-start.2 = (bf16[2,1024,128]{2,1,0:T(8,128)(2,1)}, bf16[2,1024,128]{2,1,0:T(8,128)(2,1)S(1)}, u32[]{:S(2)}) copy-start(bf16[2,1024,128]{2,1,0:T(8,128)(2,1)S(1)} %collective-permute-done.5.refs_0_) | copy-start | bytes 1572868
  65.8 49.5 %collective-permute-start.8 = (bf16[2,1024,128]{2,1,0:T(8,128)(2,1)S(1)}, bf16[2,1024,128]{2,1,0:T(8,128)(2,1)S(1)}, u32[]{:S(2)}, u32[]{:S(2)}) collective-permute-start(bf16[2,1024,128]{2,1,0:T(8,128)(2,1)S(1)} %collective-permute-done.5.refs_0_), channel_id=1, source_target_pairs={{8,0},{12,4},{16,8},{20,12},{24,16},{28,20},{9,1},{13,5},{17,9},{2... | collective-permute-start | bytes 1572872 | tf_op jit(solution)/shard_map/ppermute | solution.py:335
  67.1 23.8 %copy-start.4 = (bf16[2,1024,128]{2,1,0:T(8,128)(2,1)}, bf16[2,1024,128]{2,1,0:T(8,128)(2,1)S(1)}, u32[]{:S(2)}) copy-start(bf16[2,1024,128]{2,1,0:T(8,128)(2,1)S(1)} %collective-permute-done.6.refs_1_) | copy-start | bytes 1572868
  67.1 48.2 %collective-permute-start.9 = (bf16[2,1024,128]{2,1,0:T(8,128)(2,1)S(1)}, bf16[2,1024,128]{2,1,0:T(8,128)(2,1)S(1)}, u32[]{:S(2)}, u32[]{:S(2)}) collective-permute-start(bf16[2,1024,128]{2,1,0:T(8,128)(2,1)S(1)} %collective-permute-done.6.refs_1_), channel_id=1, source_target_pairs={{8,0},{12,4},{16,8},{20,12},{24,16},{28,20},{9,1},{13,5},{17,9},{2... | collective-permute-start | bytes 1572872 | tf_op jit(solution)/shard_map/ppermute | solution.py:335
  90.9 34.9 %collective-permute-start.12 = (bf16[1024,128]{1,0:T(8,128)(2,1)}, bf16[1024,128]{1,0:T(8,128)(2,1)S(1)}, u32[]{:S(2)}, u32[]{:S(2)}) collective-permute-start(bf16[1024,128]{1,0:T(8,128)(2,1)} %get-tuple-element.43), channel_id=1, source_target_pairs={{0,12},{4,8},{8,20},{12,16},{16,28},{20,24},{1,13},{5,9},{9,21},{1... | collective-permute-start | bytes 786440 | tf_op jit(solution)/shard_map/ppermute | solution.py:335
  113.8 13.4 %collective-permute-start.13 = (bf16[1024,128]{1,0:T(8,128)(2,1)}, bf16[1024,128]{1,0:T(8,128)(2,1)S(1)}, u32[]{:S(2)}, u32[]{:S(2)}) collective-permute-start(bf16[1024,128]{1,0:T(8,128)(2,1)} %get-tuple-element.44), channel_id=1, source_target_pairs={{0,20},{4,16},{8,28},{12,24},{1,21},{5,17},{9,29},{13,25},{2,22},{... | collective-permute-start | bytes 786440 | tf_op jit(solution)/shard_map/ppermute | solution.py:335
  115.3 0.8 copy-start.8
  115.3 1.0 copy-start.9
  116.3 6.9 %copy-start.10 = (bf16[1024,128]{1,0:T(8,128)(2,1)S(1)}, bf16[1024,128]{1,0:T(8,128)(2,1)}, u32[]{:S(2)}) copy-start(bf16[1024,128]{1,0:T(8,128)(2,1)} %get-tuple-element.35) | copy-start | bytes 786436
  116.3 8.3 %copy-start.11 = (bf16[1024,128]{1,0:T(8,128)(2,1)S(1)}, bf16[1024,128]{1,0:T(8,128)(2,1)}, u32[]{:S(2)}) copy-start(bf16[1024,128]{1,0:T(8,128)(2,1)} %get-tuple-element.38) | copy-start | bytes 786436
  116.3 25.5 %copy-start = (f32[1024,128]{1,0:T(8,128)S(1)}, f32[1024,128]{1,0:T(8,128)}, u32[]{:S(2)}) copy-start(f32[1024,128]{1,0:T(8,128)} %get-tuple-element.32) | copy-start | bytes 1572868
  121.9 8.4 %collective-permute-start.14 = (bf16[1024,128]{1,0:T(8,128)(2,1)}, bf16[1024,128]{1,0:T(8,128)(2,1)S(1)}, u32[]{:S(2)}, u32[]{:S(2)}) collective-permute-start(bf16[1024,128]{1,0:T(8,128)(2,1)} %get-tuple-element.45), channel_id=1, source_target_pairs={{0,28},{4,24},{1,29},{5,25},{2,30},{6,26},{3,31},{7,27}} | collective-permute-start | bytes 786440 | tf_op jit(solution)/shard_map/ppermute | solution.py:335
  123.2 12.5 %collective-permute-start.4 = (bf16[1024,128]{1,0:T(8,128)(2,1)S(1)}, bf16[1024,128]{1,0:T(8,128)(2,1)S(1)}, u32[]{:S(2)}, u32[]{:S(2)}) collective-permute-start(bf16[1024,128]{1,0:T(8,128)(2,1)S(1)} %copy-done.10), channel_id=1, source_target_pairs={{0,8},{4,12},{8,16},{12,20},{16,24},{20,28},{1,9},{5,13},{9,17},{1... | collective-permute-start | bytes 786440 | tf_op jit(solution)/shard_map/ppermute | solution.py:335
  124.5 14.3 %collective-permute-start.7 = (bf16[1024,128]{1,0:T(8,128)(2,1)S(1)}, bf16[1024,128]{1,0:T(8,128)(2,1)S(1)}, u32[]{:S(2)}, u32[]{:S(2)}) collective-permute-start(bf16[1024,128]{1,0:T(8,128)(2,1)S(1)} %copy-done.11), channel_id=1, source_target_pairs={{0,16},{4,20},{8,24},{12,28},{1,17},{5,21},{9,25},{13,29},{2,18},{... | collective-permute-start | bytes 786440 | tf_op jit(solution)/shard_map/ppermute | solution.py:335
  125.9 15.9 %collective-permute-start.10 = (bf16[1024,128]{1,0:T(8,128)(2,1)}, bf16[1024,128]{1,0:T(8,128)(2,1)S(1)}, u32[]{:S(2)}, u32[]{:S(2)}) collective-permute-start(bf16[1024,128]{1,0:T(8,128)(2,1)} %get-tuple-element.41), channel_id=1, source_target_pairs={{0,24},{4,28},{1,25},{5,29},{2,26},{6,30},{3,27},{7,31}} | collective-permute-start | bytes 786440 | tf_op jit(solution)/shard_map/ppermute | solution.py:335
  127.2 15.4 %collective-permute-start.15 = (bf16[2,1024,128]{2,1,0:T(8,128)(2,1)}, bf16[2,1024,128]{2,1,0:T(8,128)(2,1)S(1)}, u32[]{:S(2)}, u32[]{:S(2)}) collective-permute-start(bf16[2,1024,128]{2,1,0:T(8,128)(2,1)} %get-tuple-element.47), channel_id=1, source_target_pairs={{0,4},{4,0},{8,12},{12,8},{16,20},{20,16},{24,28},{28,24},{1,5},{5... | collective-permute-start | bytes 1572872 | tf_op jit(solution)/shard_map/ppermute | solution.py:335
  142.6 0.8 copy-start.7
  153.7 3.9 %collective-permute-start.16 = (bf16[2,1024,256]{2,1,0:T(8,128)(2,1)}, bf16[2,1024,256]{2,1,0:T(8,128)(2,1)S(1)}, u32[]{:S(2)}, u32[]{:S(2)}) collective-permute-start(bf16[2,1024,256]{2,1,0:T(8,128)(2,1)} %project_late.3), channel_id=1, source_target_pairs={{0,1},{1,0},{2,3},{3,2},{4,5},{5,4},{6,7},{7,6},{8,9},{9,8},{10,11... | collective-permute-start | bytes 3145736 | tf_op jit(solution)/shard_map/ppermute | solution.py:374
  159.5 14.4 %collective-permute-start.17 = (bf16[1,1024,256]{2,1,0:T(8,128)(2,1)S(1)}, bf16[1,1024,256]{2,1,0:T(8,128)(2,1)S(1)}, u32[]{:S(2)}, u32[]{:S(2)}) collective-permute-start(bf16[1,1024,256]{2,1,0:T(8,128)(2,1)S(1)} %slice.17), channel_id=1, source_target_pairs={{0,2},{1,3},{2,0},{3,1},{4,6},{5,7},{6,4},{7,5},{8,10},{9,11},{10,... | collective-permute-start | bytes 1572872 | tf_op jit(solution)/shard_map/ppermute | solution.py:374

commit v3 on v2

v3 whole, which is shorter than its diff:
```python
import functools

import jax
import jax.numpy as jnp
from jax import lax
from jax.experimental import pallas as pl
from jax.experimental.pallas import tpu as pltpu
from jax.sharding import PartitionSpec as P

HEAD_DIM = 128
WINDOW = 6
PAIR = 2
TILE = 512
SCALE = HEAD_DIM ** (-0.5)
VMEM_BYTES = 60 * 2**20
BF16 = jnp.bfloat16
F32 = jnp.float32


def dot(left, right, dims):
    return lax.dot_general(left, right, (dims, ((), ())), preferred_element_type=F32)


def prepare_kernel(
    shards, queries, keys, values, attn_out, gate_pre, out_grad, segments,
    query_own, key_own, other, gate_grad, seg_all, send_sems, recv_sems,
):
    me = lax.axis_index("seq")
    lane = lax.rem(me, PAIR)
    step = pl.program_id(0)

    def seg_copies():
        return [
            pltpu.make_async_remote_copy(
                src_ref=segments,
                dst_ref=seg_all.at[me],
                send_sem=send_sems.at[offset],
                recv_sem=recv_sems.at[offset],
                device_id={"seq": lax.rem(me + offset, shards)},
                device_id_type=pl.DeviceIdType.MESH,
            )
            for offset in range(1, shards)
        ]

    @pl.when(step == 0)
    def _():
        barrier = pltpu.get_barrier_semaphore()
        for offset in range(1, shards):
            pl.semaphore_signal(
                barrier,
                inc=1,
                device_id={"seq": lax.rem(me + offset, shards)},
                device_id_type=pl.DeviceIdType.MESH,
            )

    @pl.when(step == 1)
    def _():
        pl.semaphore_wait(pltpu.get_barrier_semaphore(), shards - 1)
        for copy in seg_copies():
            copy.start()
        own = pltpu.make_async_copy(segments, seg_all.at[me], send_sems.at[0])
        own.start()
        own.wait()

    for slot, (to_query, to_key) in enumerate(
        ((query_own, key_own), (other.at[pl.ds(0, 2)], other.at[pl.ds(2, 2)]))
    ):
        head = lane if slot == 0 else 1 - lane
        cols = pl.ds(pl.multiple_of(head * HEAD_DIM, HEAD_DIM), HEAD_DIM)
        to_query[0] = queries[:, cols]
        to_key[0] = keys[:, cols]
        to_key[1] = values[:, cols]
        saved = attn_out[:, cols].astype(F32)
        centred = saved - jnp.mean(saved, axis=-1, keepdims=True)
        inverse = lax.rsqrt(jnp.mean(centred * centred, axis=-1, keepdims=True) + 1e-06)
        normed = centred * inverse
        gate_in = gate_pre[:, cols].astype(F32)
        grad_in = out_grad[:, cols].astype(F32)
        sigma = jax.nn.sigmoid(gate_in)
        gate_grad[:, cols] = (
            grad_in * normed * (sigma * (1.0 + gate_in * (1.0 - sigma)))
        ).astype(BF16)
        normed_grad = grad_in * (gate_in * sigma)
        to_query[1] = (
            inverse
            * (
                normed_grad
                - jnp.mean(normed_grad, axis=-1, keepdims=True)
                - normed * jnp.mean(normed_grad * normed, axis=-1, keepdims=True)
            )
        ).astype(BF16)

    @pl.when(step == pl.num_programs(0) - 1)
    def _():
        for copy in seg_copies():
            copy.wait()


def prepare(shards, queries, keys, values, attn_out, gate_pre, out_grad, segments):
    rows, width = queries.shape
    step = min(rows // 2, 256)
    wide = pl.BlockSpec((step, width), lambda i: (i, 0))
    heads = lambda deep: pl.BlockSpec((deep, step, HEAD_DIM), lambda i: (0, i, 0))
    head_shape = lambda deep: jax.ShapeDtypeStruct((deep, rows, HEAD_DIM), BF16)
    any_spec = pl.BlockSpec(memory_space=pl.ANY)
    return pl.pallas_call(
        functools.partial(prepare_kernel, shards),
        grid=(rows // step,),
        in_specs=[wide] * 6 + [any_spec],
        out_specs=[heads(2), heads(2), heads(4), wide, any_spec],
        out_shape=[
            head_shape(2),
            head_shape(2),
            head_shape(4),
            jax.ShapeDtypeStruct((rows, width), BF16),
            jax.ShapeDtypeStruct((shards,) + segments.shape, segments.dtype),
        ],
        scratch_shapes=[
            pltpu.SemaphoreType.DMA((shards,)),
            pltpu.SemaphoreType.DMA((shards,)),
        ],
        compiler_params=pltpu.CompilerParams(
            vmem_limit_bytes=VMEM_BYTES, collective_id=0, has_side_effects=True
        ),
        cost_estimate=pl.CostEstimate(
            flops=40 * rows * width, bytes_accessed=22 * rows * width, transcendentals=rows * width
        ),
        name="prepare",
    )(queries, keys, values, attn_out, gate_pre, out_grad, segments)


def attend_kernel(plan, first, last, ids, segs, seg_rows, *refs):
    blocks, refs = refs[: len(plan.blocks)], refs[len(plan.blocks) :]
    if not first:
        accs, refs = refs[:2], refs[2:]
    outs, (held, query_acc, key_acc, sems) = refs[:2], refs[2:]
    rows = held.shape[2]
    per = rows // TILE

    copies = [
        pltpu.make_async_copy(block, held.at[n], sems.at[n]) for n, block in enumerate(blocks)
    ]
    if first:
        query_acc[...] = jnp.zeros_like(query_acc)
        key_acc[...] = jnp.zeros_like(key_acc)
    else:
        copies += [
            pltpu.make_async_copy(source, target, sems.at[len(blocks) + n])
            for n, (source, target) in enumerate(zip(accs, (query_acc, key_acc)))
        ]
    for copy in copies:
        copy.start()
    for copy in copies:
        copy.wait()

    def run(q_start, q_count, k_start, k_count, to_query, to_key):
        k_tiles = k_count * per

        def body(index, carry):
            q_idx, k_idx = index // k_tiles, index % k_tiles
            q_blk, k_blk = q_idx // per, k_idx // per
            q_off = pl.multiple_of((q_idx % per) * TILE, TILE)
            k_off = pl.multiple_of((k_idx % per) * TILE, TILE)
            q_held, k_held = q_start + q_blk, k_start + k_blk
            valid = (ids[q_held] >= 0) & (ids[k_held] >= 0)
            q_shard, k_shard = jnp.maximum(ids[q_held], 0), jnp.maximum(ids[k_held], 0)
            q_first, k_first = q_shard * rows + q_off, k_shard * rows + k_off
            q_last, k_last = q_first + TILE - 1, k_first + TILE - 1
            live = valid & (k_first <= q_last) & (segs[k_last] >= segs[q_first])
            full = (k_last <= q_first) & (segs[k_first] == segs[q_last])
            q_rows, k_rows = pl.ds(q_off, TILE), pl.ds(k_off, TILE)

            def work(masked):
                query = held[q_held, 0, q_rows, :]
                grad = held[q_held, 1, q_rows, :]
                key = held[k_held, 0, k_rows, :]
                value = held[k_held, 1, k_rows, :]
                half = dot(key, query, ((1,), (1,))) * (SCALE / 2)
                slope_in = dot(value, grad, ((1,), (1,)))
                tanh = jnp.tanh(half)
                upper = 1.0 + tanh
                weights = half * upper
                score_grad = slope_in * (upper + weights * (1.0 - tanh))
                if masked:
                    seg_q = seg_rows[pl.ds(q_shard, 1), q_rows]
                    seg_k = seg_rows[pl.ds(k_shard, 1), k_rows]
                    seg_k = jnp.transpose(jnp.broadcast_to(seg_k, (HEAD_DIM, TILE)))[:, :1]
                    place_k = k_first + lax.broadcasted_iota(jnp.int32, (TILE, TILE), 0)
                    place_q = q_first + lax.broadcasted_iota(jnp.int32, (TILE, TILE), 1)
                    allowed = (seg_q == seg_k) & (place_k <= place_q)
                    weights = jnp.where(allowed, weights, 0.0)
                    score_grad = jnp.where(allowed, score_grad, 0.0)
                score_grad = score_grad.astype(BF16)
                if to_key:
                    weights = weights.astype(BF16)
                    key_acc[k_blk, 0, k_rows, :] += dot(score_grad, query, ((1,), (0,)))
                    key_acc[k_blk, 1, k_rows, :] += dot(weights, grad, ((1,), (0,)))
                if to_query:
                    query_acc[q_blk, q_rows, :] += dot(score_grad, key, ((0,), (0,)))

            @pl.when(live & full)
            def _():
                work(False)

            @pl.when(live & jnp.logical_not(full))
            def _():
                work(True)

            return carry

        lax.fori_loop(0, q_count * per * k_tiles, body, 0)

    for entry in plan.entries:
        run(*entry)
    if last:
        for blk, out in enumerate(outs):
            out[0] = (query_acc[blk] * (SCALE / 2)).astype(BF16)
            out[1] = (key_acc[blk, 0] * (SCALE / 2)).astype(BF16)
            out[2] = key_acc[blk, 1].astype(BF16)
    else:
        done = [
            pltpu.make_async_copy(source, target, sems.at[n])
            for n, (source, target) in enumerate(zip((query_acc, key_acc), outs))
        ]
        for copy in done:
            copy.start()
        for copy in done:
            copy.wait()


class Plan:
    def __init__(self, shards):
        self.blocks, self.ids, self.entries = [], [], []
        self.shards = shards

    def add(self, blocks, ids):
        start = len(self.blocks)
        self.blocks += blocks
        self.ids += ids
        return start, len(blocks)


def attend(plan, first, last, segs, seg_rows, acc):
    rows = plan.blocks[0].shape[1]
    any_spec = pl.BlockSpec(memory_space=pl.ANY)
    vmem = pl.BlockSpec(memory_space=pltpu.VMEM)
    ids = jnp.stack(plan.ids).astype(jnp.int32)
    acc = [] if first else list(acc)
    query_shape, key_shape = (2, rows, HEAD_DIM), (2, 2, rows, HEAD_DIM)
    if last:
        out_shape = [jax.ShapeDtypeStruct((3, rows, HEAD_DIM), BF16)] * 2
    else:
        out_shape = [jax.ShapeDtypeStruct(query_shape, F32), jax.ShapeDtypeStruct(key_shape, F32)]
    return pl.pallas_call(
        functools.partial(attend_kernel, plan, first, last),
        grid_spec=pltpu.PrefetchScalarGridSpec(
            num_scalar_prefetch=2,
            grid=(),
            in_specs=[vmem] + [any_spec] * (len(plan.blocks) + len(acc)),
            out_specs=[vmem if last else any_spec] * 2,
            scratch_shapes=[
                pltpu.VMEM((len(plan.blocks), 2, rows, HEAD_DIM), BF16),
                pltpu.VMEM(query_shape, F32),
                pltpu.VMEM(key_shape, F32),
                pltpu.SemaphoreType.DMA((len(plan.blocks) + 2,)),
            ],
        ),
        out_shape=out_shape,
        compiler_params=pltpu.CompilerParams(vmem_limit_bytes=VMEM_BYTES),
        cost_estimate=pl.CostEstimate(
            flops=2 * rows * rows * HEAD_DIM, bytes_accessed=8 * rows * HEAD_DIM, transcendentals=0
        ),
        name="attend",
    )(ids, segs, seg_rows, *plan.blocks, *acc)


def project_early_kernel(place, own, gate_grad, weights, out):
    cols = pl.ds(pl.multiple_of(place[0] * HEAD_DIM, HEAD_DIM), HEAD_DIM)
    total = dot(gate_grad[...], weights[3], ((1,), (1,)))
    for part in range(3):
        total = total + dot(own[part], weights[part, :, cols], ((1,), (1,)))
    out[0] = total


def project_late_kernel(place, other, early, weights, out):
    cols = pl.ds(pl.multiple_of((1 - place[0]) * HEAD_DIM, HEAD_DIM), HEAD_DIM)
    total = early[0]
    for part in range(3):
        total = total + dot(other[part], weights[part, :, cols], ((1,), (1,)))
    out[0] = total.astype(out.dtype)


def project(place, skip, count, grads, early, projections, dtype):
    width = projections.shape[2]
    rows = grads[0].shape[-2]
    whole = lambda array: pl.BlockSpec(array.shape, lambda i, place: (0,) * array.ndim)
    partial = []
    if early is not None:
        partial = [pl.BlockSpec((1, rows, width), lambda i, place: (skip + i, 0, 0))]
    return pl.pallas_call(
        project_early_kernel if early is None else project_late_kernel,
        grid_spec=pltpu.PrefetchScalarGridSpec(
            num_scalar_prefetch=1,
            grid=(count,),
            in_specs=[whole(grad) for grad in grads]
            + partial
            + [pl.BlockSpec((4, width, width), lambda i, place: (0, place[1 + skip + i], 0))],
            out_specs=pl.BlockSpec((1, rows, width), lambda i, place: (i, 0, 0)),
        ),
        out_shape=jax.ShapeDtypeStruct((count, rows, width), dtype),
        compiler_params=pltpu.CompilerParams(vmem_limit_bytes=VMEM_BYTES),
        cost_estimate=pl.CostEstimate(
            flops=6 * count * rows * width * width,
            bytes_accessed=rows * width * (8 + 4 * count),
            transcendentals=0,
        ),
        name="project_early" if early is None else "project_late",
    )(place, *grads, *([] if early is None else [early]), projections)


def per_device(queries, key_rows, value_rows, attn_out, gate_pre, out_grad, segments, projections):
    rows = queries.shape[0]
    shards, groups = lax.axis_size("seq"), lax.axis_size("head")
    shard, group = lax.axis_index("seq"), lax.axis_index("head")
    pairs = shards // PAIR
    pair, lane = shard // PAIR, shard % PAIR

    def shift(block, distance, cross=0):
        route = [(i, (i + PAIR * distance) ^ cross) for i in range(shards)]
        return lax.ppermute(block, "seq", [hop for hop in route if 0 <= hop[1] < shards])

    query_own, key_own, other, gate_grad, seg_all = prepare(
        shards, queries, key_rows, value_rows, attn_out, gate_pre, out_grad,
        segments.reshape(-1, HEAD_DIM),
    )
    segs = seg_all.reshape(shards * rows)
    seg_rows = seg_all.reshape(shards, rows).astype(F32)
    reach = min((WINDOW + 1) // PAIR, pairs - 1)

    def travel(block, sign, relay):
        arrived = {0: block}
        for distance in range(1, reach + 1):
            if relay:
                arrived[distance] = shift(arrived[distance - 1], sign)
            else:
                arrived[distance] = shift(block, sign * distance)
        return arrived

    partner = shift(other, 0, 1)
    query_mine = [query_own, partner[:2]]
    key_mine = [key_own, partner[2:]]
    here = [shard, shard ^ 1]
    far_queries = [travel(block, -1, relay) for block, relay in zip(query_mine, (True, False))]
    far_keys = [travel(block, 1, relay) for block, relay in zip(key_mine, (True, False))]

    def far_ids(distance):
        far = pair + distance
        valid = (far >= 0) & (far < pairs)
        return [jnp.where(valid, PAIR * far + spot, -1) for spot in (lane, 1 - lane)]

    acc = None
    stages = [[0]] + [[distance] for distance in range(1, min(reach, 1) + 1)]
    if reach > 1:
        stages.append(list(range(2, reach + 1)))
    for number, stage in enumerate(stages):
        plan = Plan(shards)
        query_at = plan.add(query_mine, here)
        key_at = plan.add(key_mine, here)
        if number == 0:
            plan.entries.append((*query_at, *key_at, True, True))
        else:
            queries_in, keys_in, query_ids, key_ids = [], [], [], []
            for distance in stage:
                queries_in += [blocks[distance] for blocks in far_queries]
                keys_in += [blocks[distance] for blocks in far_keys]
                query_ids += far_ids(distance)
                key_ids += far_ids(-distance)
            plan.entries.append((*plan.add(queries_in, query_ids), *key_at, False, True))
            plan.entries.append((*query_at, *plan.add(keys_in, key_ids), True, False))
        acc = attend(plan, number == 0, number == len(stages) - 1, segs, seg_rows, acc)
    own_grads, other_grads = acc
    early = (own_grads, gate_grad)
    late = (shift(other_grads, 0, 1),)

    bits = []
    while (1 << len(bits)) < groups:
        bits.append(1 << len(bits))
    kept = list(range(groups))

    def across(block, bit):
        return lax.ppermute(block, "head", [(i, i ^ bit) for i in range(groups)])

    sent = [offset for offset in kept if offset & 1 == 1]
    near = [offset for offset in kept if offset & 1 == 0]
    place = jnp.stack([lane] + [group ^ offset for offset in sent + near]).astype(jnp.int32)
    base = project(place, 0, groups, early, None, projections, F32)
    away = project(place, 0, len(sent), late, base, projections, BF16)
    arrived = across(away, 1)
    total = project(place, len(sent), len(near), late, base, projections, F32)
    total = total + arrived.astype(F32)
    for bit in bits[1:]:
        sent = [n for n, offset in enumerate(near) if offset & bit]
        held = [n for n, offset in enumerate(near) if not offset & bit]
        arrived = across(jnp.stack([total[n] for n in sent]).astype(BF16), bit)
        total = jnp.stack([total[n] for n in held]) + arrived.astype(F32)
        near = [near[n] for n in held]
    return total[0].astype(BF16)


def solution(mesh):
    return jax.shard_map(
        per_device,
        mesh=mesh,
        in_specs=(
            P("seq", "head"),
            P("seq", "head"),
            P("seq", "head"),
            P("seq", "head"),
            P("seq", "head"),
            P("seq", "head"),
            P("seq"),
            P(None, None, "head"),
        ),
        out_specs=P("seq", "head"),
        check_vma=False,
    )
```

time: 177 us -> 192 us (1.085)
  the two profiles are of different devices: /device:TPU:0 before, /device:TPU:12 now
where the time goes in v3:
time: 192 us; the launch traced here: 195 us
  Pallas kernels  92.9 us (48%)
  waiting for transfers between devices  62.2 us (32%)
  starting transfers between devices  31.6 us (16%)
  local copies, waits for them, and re-layouts  4.44 us (2%)
  other arithmetic  3.34 us (2%)
    pallas_call x3, Pallas kernels, attend(): pl.pallas_call(functools.partial(attend_kernel, plan, first, last), grid_...  68.3 us
    ppermute x14, waiting for transfers between devices, shift(): lax.ppermute(block, 'seq', [hop for hop in route if 0 <= hop[1] < shards])  49.4 us
    ppermute x14, starting transfers between devices, shift(): lax.ppermute(block, 'seq', [hop for hop in route if 0 <= hop[1] < shards])  30 us
    pallas_call x3, Pallas kernels, project(): pl.pallas_call(project_early_kernel if early is None else project_late_ke...  15.5 us
    ppermute x2, waiting for transfers between devices, across(): return lax.ppermute(block, 'head', [(i, i ^ bit) for i in range(groups)])  12.8 us
    pallas_call x1, Pallas kernels, prepare(): pl.pallas_call(functools.partial(prepare_kernel, shards), grid=(rows // s...  9.14 us
  transfers between devices with their start and end apart: 16, of which 7 were waited for; matrix products, arithmetic and copies ran while one was open for 2% of the time, Pallas kernels for 28%

profile of v3, /device:TPU:12, one launch (start us, length us, event | category | flops | bytes accessed | tf_op | source)
XLA Modules:
  0.0 194.8 jit_solution(10237497795191737654)
XLA Ops:
  0.0 9.1 %prepare.1 = (bf16[2,1024,128]{2,1,0:T(8,128)(2,1)}, bf16[2,1024,128]{2,1,0:T(8,128)(2,1)}, bf16[4,1024,128]{2,1,0:T(8,128)(2,1)}, bf16[1024,256]{1,0:T(8,128)(2,1)}, s32[8,8,128]{2,1,0:T(8,128)}) custom-call(bf16[1024,256]{1,0:T(8,128)(2,1)} %queries.1, bf16[1024,256]{1,0:T(8,128)(2,1)} %keys.1, bf16[1024,256]{1,0:T(8,128)(2,1)} %values.1, ...), custom_call_target="tpu_custom_call" | custom-call | flops 10485760 | bytes 5767168 | tf_op jit(solution)/shard_map/prepare/pallas_call | solution.py:106
  9.2 1.1 collective-permute-start
  10.2 3.4 %collective-permute-start.1 = (bf16[2,1024,128]{2,1,0:T(8,128)(2,1)}, bf16[2,1024,128]{2,1,0:T(8,128)(2,1)S(1)}, u32[]{:S(2)}, u32[]{:S(2)}) collective-permute-start(bf16[2,1024,128]{2,1,0:T(8,128)(2,1)} %get-tuple-element.17.refs_0_), channel_id=1, source_target_pairs={{8,0},{12,4},{16,8},{20,12},{24,16},{28,20},{9,1},{13,5},{17,9},{2... | collective-permute-start | bytes 1572872 | tf_op jit(solution)/shard_map/ppermute | solution.py:330
  13.6 2.5 %collective-permute-start.6 = (bf16[2,1024,128]{2,1,0:T(8,128)(2,1)}, bf16[2,1024,128]{2,1,0:T(8,128)(2,1)S(1)}, u32[]{:S(2)}, u32[]{:S(2)}) collective-permute-start(bf16[2,1024,128]{2,1,0:T(8,128)(2,1)} %get-tuple-element.19.refs_2_), channel_id=1, source_target_pairs={{0,8},{4,12},{8,16},{12,20},{16,24},{20,28},{1,9},{5,13},{9,17},{1... | collective-permute-start | bytes 1572872 | tf_op jit(solution)/shard_map/ppermute | solution.py:330
  16.1 9.3 %collective-permute-done.1.refs_4_ = bf16[2,1024,128]{2,1,0:T(8,128)(2,1)S(1)} collective-permute-done((bf16[2,1024,128]{2,1,0:T(8,128)(2,1)}, bf16[2,1024,128]{2,1,0:T(8,128)(2,1)S(1)}, u32[]{:S(2)}, u32[]{:S(2)}) %collective-permute-start.1) | collective-permute-done | bytes 524320 | tf_op jit(solution)/shard_map/ppermute | solution.py:330
  25.4 3.4 %collective-permute-start.2 = (bf16[2,1024,128]{2,1,0:T(8,128)(2,1)S(1)}, bf16[2,1024,128]{2,1,0:T(8,128)(2,1)S(1)}, u32[]{:S(2)}, u32[]{:S(2)}) collective-permute-start(bf16[2,1024,128]{2,1,0:T(8,128)(2,1)S(1)} %collective-permute-done.1.refs_4_), channel_id=1, source_target_pairs={{8,0},{12,4},{16,8},{20,12},{24,16},{28,20},{9,1},{13,5},{17,9},{2... | collective-permute-start | bytes 1572872 | tf_op jit(solution)/shard_map/ppermute | solution.py:330
  28.8 0.0 collective-permute-done.6.refs_6_
  28.8 2.5 %collective-permute-start.7 = (bf16[2,1024,128]{2,1,0:T(8,128)(2,1)S(1)}, bf16[2,1024,128]{2,1,0:T(8,128)(2,1)S(1)}, u32[]{:S(2)}, u32[]{:S(2)}) collective-permute-start(bf16[2,1024,128]{2,1,0:T(8,128)(2,1)S(1)} %collective-permute-done.6.refs_6_), channel_id=1, source_target_pairs={{0,8},{4,12},{8,16},{12,20},{16,24},{20,28},{1,9},{5,13},{9,17},{1... | collective-permute-start | bytes 1572872 | tf_op jit(solution)/shard_map/ppermute | solution.py:330
  31.3 2.3 %collective-permute-done = bf16[4,1024,128]{2,1,0:T(8,128)(2,1)S(1)} collective-permute-done((bf16[4,1024,128]{2,1,0:T(8,128)(2,1)}, bf16[4,1024,128]{2,1,0:T(8,128)(2,1)S(1)}, u32[]{:S(2)}, u32[]{:S(2)}) %collective-permute-start) | collective-permute-done | bytes 1048608 | tf_op jit(solution)/shard_map/ppermute | solution.py:330
  33.6 0.1 fusion.2
  33.7 0.0 copy-start.1
  33.7 3.4 %collective-permute-start.11 = (bf16[2,1024,128]{2,1,0:T(8,128)(2,1)S(1)}, bf16[2,1024,128]{2,1,0:T(8,128)(2,1)S(1)}, u32[]{:S(2)}, u32[]{:S(2)}) collective-permute-start(bf16[2,1024,128]{2,1,0:T(8,128)(2,1)S(1)} %get-tuple-element.28.refs_1_), channel_id=1, source_target_pairs={{8,0},{12,4},{16,8},{20,12},{24,16},{28,20},{9,1},{13,5},{17,9},{2... | collective-permute-start | bytes 1572872 | tf_op jit(solution)/shard_map/ppermute | solution.py:330
  37.1 2.5 %collective-permute-start.12 = (bf16[2,1024,128]{2,1,0:T(8,128)(2,1)S(1)}, bf16[2,1024,128]{2,1,0:T(8,128)(2,1)S(1)}, u32[]{:S(2)}, u32[]{:S(2)}) collective-permute-start(bf16[2,1024,128]{2,1,0:T(8,128)(2,1)S(1)} %get-tuple-element.27.refs_3_), channel_id=1, source_target_pairs={{0,8},{4,12},{8,16},{12,20},{16,24},{20,28},{1,9},{5,13},{9,17},{1... | collective-permute-start | bytes 1572872 | tf_op jit(solution)/shard_map/ppermute | solution.py:330
  39.5 0.7 collective-permute-start.10
  40.2 1.9 collective-permute-done.2.refs_4_
  42.2 1.3 collective-permute-start.3
  43.5 1.8 collective-permute-done.7.refs_8_
  45.2 1.5 collective-permute-start.5
  46.7 29.2 %collective-permute-done.11.refs_5_ = bf16[2,1024,128]{2,1,0:T(8,128)(2,1)S(1)} collective-permute-done((bf16[2,1024,128]{2,1,0:T(8,128)(2,1)S(1)}, bf16[2,1024,128]{2,1,0:T(8,128)(2,1)S(1)}, u32[]{:S(2)}, u32[]{:S(2)}) %collective-permute-start.11) | collective-permute-done | bytes 524320 | tf_op jit(solution)/shard_map/ppermute | solution.py:330
  75.9 2.1 %collective-permute-start.8 = (bf16[2,1024,128]{2,1,0:T(8,128)(2,1)S(1)}, bf16[2,1024,128]{2,1,0:T(8,128)(2,1)}, u32[]{:S(2)}, u32[]{:S(2)}) collective-permute-start(bf16[2,1024,128]{2,1,0:T(8,128)(2,1)S(1)} %get-tuple-element.27.refs_3_), channel_id=1, source_target_pairs={{0,16},{4,20},{8,24},{12,28},{1,17},{5,21},{9,25},{13,29},{2,18},{... | collective-permute-start | bytes 1572872 | tf_op jit(solution)/shard_map/ppermute | solution.py:330
  78.0 3.4 %collective-permute-start.4 = (bf16[2,1024,128]{2,1,0:T(8,128)(2,1)S(1)}, bf16[2,1024,128]{2,1,0:T(8,128)(2,1)}, u32[]{:S(2)}, u32[]{:S(2)}) collective-permute-start(bf16[2,1024,128]{2,1,0:T(8,128)(2,1)S(1)} %collective-permute-done.2.refs_4_), channel_id=1, source_target_pairs={{8,0},{12,4},{16,8},{20,12},{24,16},{28,20},{9,1},{13,5},{17,9},{2... | collective-permute-start | bytes 1572872 | tf_op jit(solution)/shard_map/ppermute | solution.py:330
  81.3 0.0 collective-permute-done.10.refs_11_
  81.4 0.8 copy-done.8
  82.2 2.4 %collective-permute-start.9 = (bf16[2,1024,128]{2,1,0:T(8,128)(2,1)S(1)}, bf16[2,1024,128]{2,1,0:T(8,128)(2,1)}, u32[]{:S(2)}, u32[]{:S(2)}) collective-permute-start(bf16[2,1024,128]{2,1,0:T(8,128)(2,1)S(1)} %collective-permute-done.7.refs_8_), channel_id=1, source_target_pairs={{0,8},{4,12},{8,16},{12,20},{16,24},{20,28},{1,9},{5,13},{9,17},{1... | collective-permute-start | bytes 1572872 | tf_op jit(solution)/shard_map/ppermute | solution.py:330
  84.8 0.6 copy.11
  85.4 0.6 stack.100.ids
  86.0 0.7 stack.95.ids
  86.7 0.6 pad_add_fusion.ids
  87.2 17.4 %attend.3 = (f32[2,1024,128]{2,1,0:T(8,128)}, f32[2,2,1024,128]{3,2,1,0:T(8,128)}) custom-call(s32[4]{0:T(128)} %pad_add_fusion.ids, s32[8192]{0:T(1024)} %bitcast.28, f32[8,1024]{1,0:T(8,128)} %bitcast.31, bf16[2,1024,128]{2,1,0:T(8,128)(2,1)} %get-tuple-element.17.refs_0_, bf16[2,1024,128]{2,1,0:T(8,128)(2,1)} %copy-done.1, ...), custom_call_target="tpu_custom_call" | custom-call | flops 268435456 | bytes 1048576 | tf_op jit(solution)/shard_map/attend/pallas_call | solution.py:254
  104.7 26.5 %attend.4 = (f32[2,1024,128]{2,1,0:T(8,128)}, f32[2,2,1024,128]{3,2,1,0:T(8,128)}) custom-call(s32[8]{0:T(128)} %stack.100.ids, s32[8192]{0:T(1024)} %bitcast.29, f32[8,1024]{1,0:T(8,128)} %bitcast.32, bf16[2,1024,128]{2,1,0:T(8,128)(2,1)} %get-tuple-element.17.refs_0_, bf16[2,1024,128]{2,1,0:T(8,128)(2,1)} %copy-done.1, ...), custom_call_target="tpu_custom_call" | custom-call | flops 268435456 | bytes 1048576 | tf_op jit(solution)/shard_map/attend/pallas_call | solution.py:254
  131.2 0.0 collective-permute-done.3.refs_5_
  131.3 0.0 collective-permute-done.5.refs_7_
  131.3 0.0 collective-permute-done.4.refs_6_
  131.3 0.0 collective-permute-done.9.refs_10_
  131.3 24.3 %attend.5 = (bf16[3,1024,128]{2,1,0:T(8,128)(2,1)}, bf16[3,1024,128]{2,1,0:T(8,128)(2,1)}) custom-call(s32[12]{0:T(128)} %stack.95.ids, s32[8192]{0:T(1024)} %bitcast.30, f32[8,1024]{1,0:T(8,128)} %bitcast.33, bf16[2,1024,128]{2,1,0:T(8,128)(2,1)} %get-tuple-element.17.refs_0_, bf16[2,1024,128]{2,1,0:T(8,128)(2,1)} %copy-done.1, ...), custom_call_target="tpu_custom_call" | custom-call | flops 268435456 | bytes 1048576 | tf_op jit(solution)/shard_map/attend/pallas_call | solution.py:254
  155.6 0.1 collective-permute-start.13
  155.7 0.6 stack.84.place
  156.3 6.7 %project_early.1.early = f32[4,1024,256]{2,1,0:T(8,128)} custom-call(s32[5]{0:T(128)} %stack.84.place, bf16[3,1024,128]{2,1,0:T(8,128)(2,1)} %get-tuple-element.25.own, bf16[1024,256]{1,0:T(8,128)(2,1)} %get-tuple-element.26.gate_grad, bf16[4,1024,256]{2,1,0:T(8,128)(2,1)} %weights.5), custom_call_target="tpu_custom_call" | custom-call | flops 1610612736 | bytes 6291456 | tf_op jit(solution)/shard_map/project_early/pallas_call | solution.py:300
  163.0 4.8 %collective-permute-done.13.other = bf16[3,1024,128]{2,1,0:T(8,128)(2,1)S(1)} collective-permute-done((bf16[3,1024,128]{2,1,0:T(8,128)(2,1)}, bf16[3,1024,128]{2,1,0:T(8,128)(2,1)S(1)}, u32[]{:S(2)}, u32[]{:S(2)}) %collective-permute-start.13) | collective-permute-done | bytes 786464 | tf_op jit(solution)/shard_map/ppermute | solution.py:330
  167.9 0.9 copy-done.2
  168.8 4.3 %project_late.3 = bf16[2,1024,256]{2,1,0:T(8,128)(2,1)} custom-call(s32[5]{0:T(128)} %stack.84.place, bf16[3,1024,128]{2,1,0:T(8,128)(2,1)} %copy-done.2, f32[4,1024,256]{2,1,0:T(8,128)} %project_early.1.early, bf16[4,1024,256]{2,1,0:T(8,128)(2,1)} %weights.5), custom_call_target="tpu_custom_call" | custom-call | flops 805306368 | bytes 4194304 | tf_op jit(solution)/shard_map/project_late/pallas_call | solution.py:300
  173.1 0.0 collective-permute-start.14
  173.1 4.5 %project_late.2 = f32[2,1024,256]{2,1,0:T(8,128)} custom-call(s32[5]{0:T(128)} %stack.84.place, bf16[3,1024,128]{2,1,0:T(8,128)(2,1)} %copy-done.2, f32[4,1024,256]{2,1,0:T(8,128)} %project_early.1.early, bf16[4,1024,256]{2,1,0:T(8,128)(2,1)} %weights.5), custom_call_target="tpu_custom_call" | custom-call | flops 805306368 | bytes 4194304 | tf_op jit(solution)/shard_map/project_late/pallas_call | solution.py:300
  177.6 1.8 convert_add_fusion
  179.4 0.1 slice.27
  179.4 1.6 collective-permute-start.15
  181.0 12.8 %collective-permute-done.15 = bf16[1,1024,256]{2,1,0:T(8,128)(2,1)S(1)} collective-permute-done((bf16[1,1024,256]{2,1,0:T(8,128)(2,1)S(1)}, bf16[1,1024,256]{2,1,0:T(8,128)(2,1)S(1)}, u32[]{:S(2)}, u32[]{:S(2)}) %collective-permute-start.15) | collective-permute-done | bytes 524320 | tf_op jit(solution)/shard_map/ppermute | solution.py:391
  193.8 1.0 fusion.1
  (23 shorter events, 0.0 us)
Async XLA Ops:
  9.1 75.6 %copy-start.3 = (s32[8,8,128]{2,1,0:T(8,128)S(1)}, s32[8,8,128]{2,1,0:T(8,128)}, u32[]{:S(2)}) copy-start(s32[8,8,128]{2,1,0:T(8,128)} %get-tuple-element.16) | copy-start | bytes 98308
  9.2 24.4 %collective-permute-start = (bf16[4,1024,128]{2,1,0:T(8,128)(2,1)}, bf16[4,1024,128]{2,1,0:T(8,128)(2,1)S(1)}, u32[]{:S(2)}, u32[]{:S(2)}) collective-permute-start(bf16[4,1024,128]{2,1,0:T(8,128)(2,1)} %get-tuple-element.18), channel_id=1, source_target_pairs={{0,4},{4,0},{8,12},{12,8},{16,20},{20,16},{24,28},{28,24},{1,5},{5... | collective-permute-start | bytes 3145736 | tf_op jit(solution)/shard_map/ppermute | solution.py:330
  10.2 15.2 %collective-permute-start.1 = (bf16[2,1024,128]{2,1,0:T(8,128)(2,1)}, bf16[2,1024,128]{2,1,0:T(8,128)(2,1)S(1)}, u32[]{:S(2)}, u32[]{:S(2)}) collective-permute-start(bf16[2,1024,128]{2,1,0:T(8,128)(2,1)} %get-tuple-element.17.refs_0_), channel_id=1, source_target_pairs={{8,0},{12,4},{16,8},{20,12},{24,16},{28,20},{9,1},{13,5},{17,9},{2... | collective-permute-start | bytes 1572872 | tf_op jit(solution)/shard_map/ppermute | solution.py:330
  13.6 15.2 %collective-permute-start.6 = (bf16[2,1024,128]{2,1,0:T(8,128)(2,1)}, bf16[2,1024,128]{2,1,0:T(8,128)(2,1)S(1)}, u32[]{:S(2)}, u32[]{:S(2)}) collective-permute-start(bf16[2,1024,128]{2,1,0:T(8,128)(2,1)} %get-tuple-element.19.refs_2_), channel_id=1, source_target_pairs={{0,8},{4,12},{8,16},{12,20},{16,24},{20,28},{1,9},{5,13},{9,17},{1... | collective-permute-start | bytes 1572872 | tf_op jit(solution)/shard_map/ppermute | solution.py:330
  25.4 79.2 %copy-start.6 = (bf16[2,1024,128]{2,1,0:T(8,128)(2,1)}, bf16[2,1024,128]{2,1,0:T(8,128)(2,1)S(1)}, u32[]{:S(2)}) copy-start(bf16[2,1024,128]{2,1,0:T(8,128)(2,1)S(1)} %collective-permute-done.1.refs_4_) | copy-start | bytes 1572868
  25.4 16.7 %collective-permute-start.2 = (bf16[2,1024,128]{2,1,0:T(8,128)(2,1)S(1)}, bf16[2,1024,128]{2,1,0:T(8,128)(2,1)S(1)}, u32[]{:S(2)}, u32[]{:S(2)}) collective-permute-start(bf16[2,1024,128]{2,1,0:T(8,128)(2,1)S(1)} %collective-permute-done.1.refs_4_), channel_id=1, source_target_pairs={{8,0},{12,4},{16,8},{20,12},{24,16},{28,20},{9,1},{13,5},{17,9},{2... | collective-permute-start | bytes 1572872 | tf_op jit(solution)/shard_map/ppermute | solution.py:330
  28.8 75.9 %copy-start.7 = (bf16[2,1024,128]{2,1,0:T(8,128)(2,1)}, bf16[2,1024,128]{2,1,0:T(8,128)(2,1)S(1)}, u32[]{:S(2)}) copy-start(bf16[2,1024,128]{2,1,0:T(8,128)(2,1)S(1)} %collective-permute-done.6.refs_6_) | copy-start | bytes 1572868
  28.8 16.4 %collective-permute-start.7 = (bf16[2,1024,128]{2,1,0:T(8,128)(2,1)S(1)}, bf16[2,1024,128]{2,1,0:T(8,128)(2,1)S(1)}, u32[]{:S(2)}, u32[]{:S(2)}) collective-permute-start(bf16[2,1024,128]{2,1,0:T(8,128)(2,1)S(1)} %collective-permute-done.6.refs_6_), channel_id=1, source_target_pairs={{0,8},{4,12},{8,16},{12,20},{16,24},{20,28},{1,9},{5,13},{9,17},{1... | collective-permute-start | bytes 1572872 | tf_op jit(solution)/shard_map/ppermute | solution.py:330
  33.7 53.6 %copy-start = (bf16[2,1024,128]{2,1,0:T(8,128)(2,1)}, bf16[2,1024,128]{2,1,0:T(8,128)(2,1)S(1)}, u32[]{:S(2)}) copy-start(bf16[2,1024,128]{2,1,0:T(8,128)(2,1)S(1)} %get-tuple-element.27.refs_3_) | copy-start | bytes 1572868
  33.7 53.6 %copy-start.1 = (bf16[2,1024,128]{2,1,0:T(8,128)(2,1)}, bf16[2,1024,128]{2,1,0:T(8,128)(2,1)S(1)}, u32[]{:S(2)}) copy-start(bf16[2,1024,128]{2,1,0:T(8,128)(2,1)S(1)} %get-tuple-element.28.refs_1_) | copy-start | bytes 1572868
  33.7 42.2 %collective-permute-start.11 = (bf16[2,1024,128]{2,1,0:T(8,128)(2,1)S(1)}, bf16[2,1024,128]{2,1,0:T(8,128)(2,1)S(1)}, u32[]{:S(2)}, u32[]{:S(2)}) collective-permute-start(bf16[2,1024,128]{2,1,0:T(8,128)(2,1)S(1)} %get-tuple-element.28.refs_1_), channel_id=1, source_target_pairs={{8,0},{12,4},{16,8},{20,12},{24,16},{28,20},{9,1},{13,5},{17,9},{2... | collective-permute-start | bytes 1572872 | tf_op jit(solution)/shard_map/ppermute | solution.py:330
  37.1 40.9 %collective-permute-start.12 = (bf16[2,1024,128]{2,1,0:T(8,128)(2,1)S(1)}, bf16[2,1024,128]{2,1,0:T(8,128)(2,1)S(1)}, u32[]{:S(2)}, u32[]{:S(2)}) collective-permute-start(bf16[2,1024,128]{2,1,0:T(8,128)(2,1)S(1)} %get-tuple-element.27.refs_3_), channel_id=1, source_target_pairs={{0,8},{4,12},{8,16},{12,20},{16,24},{20,28},{1,9},{5,13},{9,17},{1... | collective-permute-start | bytes 1572872 | tf_op jit(solution)/shard_map/ppermute | solution.py:330
  39.5 41.8 %collective-permute-start.10 = (bf16[2,1024,128]{2,1,0:T(8,128)(2,1)S(1)}, bf16[2,1024,128]{2,1,0:T(8,128)(2,1)S(1)}, u32[]{:S(2)}, u32[]{:S(2)}) collective-permute-start(bf16[2,1024,128]{2,1,0:T(8,128)(2,1)S(1)} %get-tuple-element.27.refs_3_), channel_id=1, source_target_pairs={{0,24},{4,28},{1,25},{5,29},{2,26},{6,30},{3,27},{7,31}} | collective-permute-start | bytes 1572872 | tf_op jit(solution)/shard_map/ppermute | solution.py:330
  42.2 89.1 %copy-start.4 = (bf16[2,1024,128]{2,1,0:T(8,128)(2,1)}, bf16[2,1024,128]{2,1,0:T(8,128)(2,1)S(1)}, u32[]{:S(2)}) copy-start(bf16[2,1024,128]{2,1,0:T(8,128)(2,1)S(1)} %collective-permute-done.2.refs_4_) | copy-start | bytes 1572868
  42.2 89.1 %collective-permute-start.3 = (bf16[2,1024,128]{2,1,0:T(8,128)(2,1)S(1)}, bf16[2,1024,128]{2,1,0:T(8,128)(2,1)}, u32[]{:S(2)}, u32[]{:S(2)}) collective-permute-start(bf16[2,1024,128]{2,1,0:T(8,128)(2,1)S(1)} %get-tuple-element.28.refs_1_), channel_id=1, source_target_pairs={{16,0},{20,4},{24,8},{28,12},{17,1},{21,5},{25,9},{29,13},{18,2},{... | collective-permute-start | bytes 1572872 | tf_op jit(solution)/shard_map/ppermute | solution.py:330
  45.2 86.0 %copy-start.5 = (bf16[2,1024,128]{2,1,0:T(8,128)(2,1)}, bf16[2,1024,128]{2,1,0:T(8,128)(2,1)S(1)}, u32[]{:S(2)}) copy-start(bf16[2,1024,128]{2,1,0:T(8,128)(2,1)S(1)} %collective-permute-done.7.refs_8_) | copy-start | bytes 1572868
  45.2 86.0 %collective-permute-start.5 = (bf16[2,1024,128]{2,1,0:T(8,128)(2,1)S(1)}, bf16[2,1024,128]{2,1,0:T(8,128)(2,1)}, u32[]{:S(2)}, u32[]{:S(2)}) collective-permute-start(bf16[2,1024,128]{2,1,0:T(8,128)(2,1)S(1)} %get-tuple-element.28.refs_1_), channel_id=1, source_target_pairs={{24,0},{28,4},{25,1},{29,5},{26,2},{30,6},{27,3},{31,7}} | collective-permute-start | bytes 1572872 | tf_op jit(solution)/shard_map/ppermute | solution.py:330
  75.9 8.8 %copy-start.9 = (bf16[2,1024,128]{2,1,0:T(8,128)(2,1)}, bf16[2,1024,128]{2,1,0:T(8,128)(2,1)S(1)}, u32[]{:S(2)}) copy-start(bf16[2,1024,128]{2,1,0:T(8,128)(2,1)S(1)} %collective-permute-done.11.refs_5_) | copy-start | bytes 1572868
  75.9 55.4 %collective-permute-start.8 = (bf16[2,1024,128]{2,1,0:T(8,128)(2,1)S(1)}, bf16[2,1024,128]{2,1,0:T(8,128)(2,1)}, u32[]{:S(2)}, u32[]{:S(2)}) collective-permute-start(bf16[2,1024,128]{2,1,0:T(8,128)(2,1)S(1)} %get-tuple-element.27.refs_3_), channel_id=1, source_target_pairs={{0,16},{4,20},{8,24},{12,28},{1,17},{5,21},{9,25},{13,29},{2,18},{... | collective-permute-start | bytes 1572872 | tf_op jit(solution)/shard_map/ppermute | solution.py:330
  78.0 6.7 %copy-start.10 = (bf16[2,1024,128]{2,1,0:T(8,128)(2,1)}, bf16[2,1024,128]{2,1,0:T(8,128)(2,1)S(1)}, u32[]{:S(2)}) copy-start(bf16[2,1024,128]{2,1,0:T(8,128)(2,1)S(1)} %collective-permute-done.12.refs_7_) | copy-start | bytes 1572868
  78.0 53.3 %collective-permute-start.4 = (bf16[2,1024,128]{2,1,0:T(8,128)(2,1)S(1)}, bf16[2,1024,128]{2,1,0:T(8,128)(2,1)}, u32[]{:S(2)}, u32[]{:S(2)}) collective-permute-start(bf16[2,1024,128]{2,1,0:T(8,128)(2,1)S(1)} %collective-permute-done.2.refs_4_), channel_id=1, source_target_pairs={{8,0},{12,4},{16,8},{20,12},{24,16},{28,20},{9,1},{13,5},{17,9},{2... | collective-permute-start | bytes 1572872 | tf_op jit(solution)/shard_map/ppermute | solution.py:330
  81.4 0.8 copy-start.8
  82.2 49.1 %collective-permute-start.9 = (bf16[2,1024,128]{2,1,0:T(8,128)(2,1)S(1)}, bf16[2,1024,128]{2,1,0:T(8,128)(2,1)}, u32[]{:S(2)}, u32[]{:S(2)}) collective-permute-start(bf16[2,1024,128]{2,1,0:T(8,128)(2,1)S(1)} %collective-permute-done.7.refs_8_), channel_id=1, source_target_pairs={{0,8},{4,12},{8,16},{12,20},{16,24},{20,28},{1,9},{5,13},{9,17},{1... | collective-permute-start | bytes 1572872 | tf_op jit(solution)/shard_map/ppermute | solution.py:330
  155.6 12.3 %collective-permute-start.13 = (bf16[3,1024,128]{2,1,0:T(8,128)(2,1)}, bf16[3,1024,128]{2,1,0:T(8,128)(2,1)S(1)}, u32[]{:S(2)}, u32[]{:S(2)}) collective-permute-start(bf16[3,1024,128]{2,1,0:T(8,128)(2,1)} %get-tuple-element.24), channel_id=1, source_target_pairs={{0,4},{4,0},{8,12},{12,8},{16,20},{20,16},{24,28},{28,24},{1,5},{5... | collective-permute-start | bytes 2359304 | tf_op jit(solution)/shard_map/ppermute | solution.py:330
  167.9 0.9 copy-start.2
  173.1 4.5 %collective-permute-start.14 = (bf16[2,1024,256]{2,1,0:T(8,128)(2,1)}, bf16[2,1024,256]{2,1,0:T(8,128)(2,1)S(1)}, u32[]{:S(2)}, u32[]{:S(2)}) collective-permute-start(bf16[2,1024,256]{2,1,0:T(8,128)(2,1)} %project_late.3), channel_id=1, source_target_pairs={{0,1},{1,0},{2,3},{3,2},{4,5},{5,4},{6,7},{7,6},{8,9},{9,8},{10,11... | collective-permute-start | bytes 3145736 | tf_op jit(solution)/shard_map/ppermute | solution.py:391
  179.4 14.4 %collective-permute-start.15 = (bf16[1,1024,256]{2,1,0:T(8,128)(2,1)S(1)}, bf16[1,1024,256]{2,1,0:T(8,128)(2,1)S(1)}, u32[]{:S(2)}, u32[]{:S(2)}) collective-permute-start(bf16[1,1024,256]{2,1,0:T(8,128)(2,1)S(1)} %slice.27), channel_id=1, source_target_pairs={{0,2},{1,3},{2,0},{3,1},{4,6},{5,7},{6,4},{7,5},{8,10},{9,11},{10,... | collective-permute-start | bytes 1572872 | tf_op jit(solution)/shard_map/ppermute | solution.py:391

commit v4 on v3

--- a/solution.py
+++ b/solution.py
@@ -21,47 +21,58 @@
     return lax.dot_general(left, right, (dims, ((), ())), preferred_element_type=F32)
 
 
+def share_kernel(shards, segments, after, seg_all, send_sems, recv_sems):
+    me = lax.axis_index("seq")
+    to = [{"seq": lax.rem(me + offset, shards)} for offset in range(shards)]
+    barrier = pltpu.get_barrier_semaphore()
+    for offset in range(1, shards):
+        pl.semaphore_signal(
+            barrier, inc=1, device_id=to[offset], device_id_type=pl.DeviceIdType.MESH
+        )
+    pl.semaphore_wait(barrier, shards - 1)
+    copies = [
+        pltpu.make_async_remote_copy(
+            src_ref=segments,
+            dst_ref=seg_all.at[me],
+            send_sem=send_sems.at[offset],
+            recv_sem=recv_sems.at[offset],
+            device_id=to[offset],
+            device_id_type=pl.DeviceIdType.MESH,
+        )
+        for offset in range(1, shards)
+    ]
+    copies.append(pltpu.make_async_copy(segments, seg_all.at[me], send_sems.at[0]))
+    for copy in copies:
+        copy.start()
+    for copy in copies:
+        copy.wait()
+
+
+def share(shards, segments, after):
+    any_spec = pl.BlockSpec(memory_space=pl.ANY)
+    return pl.pallas_call(
+        functools.partial(share_kernel, shards),
+        in_specs=[any_spec] * 2,
+        out_specs=any_spec,
+        out_shape=jax.ShapeDtypeStruct((shards,) + segments.shape, segments.dtype),
+        scratch_shapes=[
+            pltpu.SemaphoreType.DMA((shards,)),
+            pltpu.SemaphoreType.DMA((shards,)),
+        ],
+        compiler_params=pltpu.CompilerParams(
+            vmem_limit_bytes=VMEM_BYTES, collective_id=0, has_side_effects=True
+        ),
+        cost_estimate=pl.CostEstimate(
+            flops=0, bytes_accessed=2 * shards * segments.size * 4, transcendentals=0
+        ),
+        name="share",
+    )(segments, after)
+
+
 def prepare_kernel(
-    shards, queries, keys, values, attn_out, gate_pre, out_grad, segments,
-    query_own, key_own, other, gate_grad, seg_all, send_sems, recv_sems,
+    queries, keys, values, attn_out, gate_pre, out_grad, query_own, key_own, other, gate_grad
 ):
-    me = lax.axis_index("seq")
-    lane = lax.rem(me, PAIR)
-    step = pl.program_id(0)
-
-    def seg_copies():
-        return [
-            pltpu.make_async_remote_copy(
-                src_ref=segments,
-                dst_ref=seg_all.at[me],
-                send_sem=send_sems.at[offset],
-                recv_sem=recv_sems.at[offset],
-                device_id={"seq": lax.rem(me + offset, shards)},
-                device_id_type=pl.DeviceIdType.MESH,
-            )
-            for offset in range(1, shards)
-        ]
-
-    @pl.when(step == 0)
-    def _():
-        barrier = pltpu.get_barrier_semaphore()
-        for offset in range(1, shards):
-            pl.semaphore_signal(
-                barrier,
-                inc=1,
-                device_id={"seq": lax.rem(me + offset, shards)},
-                device_id_type=pl.DeviceIdType.MESH,
-            )
-
-    @pl.when(step == 1)
-    def _():
-        pl.semaphore_wait(pltpu.get_barrier_semaphore(), shards - 1)
-        for copy in seg_copies():
-            copy.start()
-        own = pltpu.make_async_copy(segments, seg_all.at[me], send_sems.at[0])
-        own.start()
-        own.wait()
-
+    lane = lax.rem(lax.axis_index("seq"), PAIR)
     for slot, (to_query, to_key) in enumerate(
         ((query_own, key_own), (other.at[pl.ds(0, 2)], other.at[pl.ds(2, 2)]))
     ):
@@ -90,43 +101,30 @@
             )
         ).astype(BF16)
 
-    @pl.when(step == pl.num_programs(0) - 1)
-    def _():
-        for copy in seg_copies():
-            copy.wait()
-
-
-def prepare(shards, queries, keys, values, attn_out, gate_pre, out_grad, segments):
+
+def prepare(queries, keys, values, attn_out, gate_pre, out_grad):
     rows, width = queries.shape
     step = min(rows // 2, 256)
     wide = pl.BlockSpec((step, width), lambda i: (i, 0))
     heads = lambda deep: pl.BlockSpec((deep, step, HEAD_DIM), lambda i: (0, i, 0))
     head_shape = lambda deep: jax.ShapeDtypeStruct((deep, rows, HEAD_DIM), BF16)
-    any_spec = pl.BlockSpec(memory_space=pl.ANY)
     return pl.pallas_call(
-        functools.partial(prepare_kernel, shards),
+        prepare_kernel,
         grid=(rows // step,),
-        in_specs=[wide] * 6 + [any_spec],
-        out_specs=[heads(2), heads(2), heads(4), wide, any_spec],
+        in_specs=[wide] * 6,
+        out_specs=[heads(2), heads(2), heads(4), wide],
         out_shape=[
             head_shape(2),
             head_shape(2),
             head_shape(4),
             jax.ShapeDtypeStruct((rows, width), BF16),
-            jax.ShapeDtypeStruct((shards,) + segments.shape, segments.dtype),
         ],
-        scratch_shapes=[
-            pltpu.SemaphoreType.DMA((shards,)),
-            pltpu.SemaphoreType.DMA((shards,)),
-        ],
-        compiler_params=pltpu.CompilerParams(
-            vmem_limit_bytes=VMEM_BYTES, collective_id=0, has_side_effects=True
-        ),
+        compiler_params=pltpu.CompilerParams(vmem_limit_bytes=VMEM_BYTES),
         cost_estimate=pl.CostEstimate(
             flops=40 * rows * width, bytes_accessed=22 * rows * width, transcendentals=rows * width
         ),
         name="prepare",
-    )(queries, keys, values, attn_out, gate_pre, out_grad, segments)
+    )(queries, keys, values, attn_out, gate_pre, out_grad)
 
 
 def attend_kernel(plan, first, last, ids, segs, seg_rows, *refs):
@@ -150,23 +148,41 @@
         ]
     for copy in copies:
         copy.start()
-    for copy in copies:
-        copy.wait()
+    waiting = set(range(len(copies)))
+
+    def arrive(needed):
+        for n in sorted(waiting & set(needed)):
+            copies[n].wait()
+            waiting.discard(n)
+
+    arrive(range(len(blocks), len(copies)))
 
     def run(q_start, q_count, k_start, k_count, to_query, to_key):
-        k_tiles = k_count * per
-
-        def body(index, carry):
-            q_idx, k_idx = index // k_tiles, index % k_tiles
-            q_blk, k_blk = q_idx // per, k_idx // per
-            q_off = pl.multiple_of((q_idx % per) * TILE, TILE)
-            k_off = pl.multiple_of((k_idx % per) * TILE, TILE)
+        arrive(range(q_start, q_start + q_count))
+        arrive(range(k_start, k_start + k_count))
+
+        def pair_body(index, carry):
+            q_blk, k_blk = index // k_count, index % k_count
+            q_shard, k_shard = ids[q_start + q_blk], ids[k_start + k_blk]
+            valid = (q_shard >= 0) & (k_shard >= 0) & (k_shard <= q_shard)
+            q_shard, k_shard = jnp.maximum(q_shard, 0), jnp.maximum(k_shard, 0)
+            meet = segs[k_shard * rows + rows - 1] >= segs[q_shard * rows]
+
+            @pl.when(valid & meet)
+            def _():
+                lax.fori_loop(
+                    0, per * per, functools.partial(tile_body, q_blk, k_blk, q_shard, k_shard), 0
+                )
+
+            return carry
+
+        def tile_body(q_blk, k_blk, q_shard, k_shard, index, carry):
+            q_off = pl.multiple_of((index // per) * TILE, TILE)
+            k_off = pl.multiple_of((index % per) * TILE, TILE)
             q_held, k_held = q_start + q_blk, k_start + k_blk
-            valid = (ids[q_held] >= 0) & (ids[k_held] >= 0)
-            q_shard, k_shard = jnp.maximum(ids[q_held], 0), jnp.maximum(ids[k_held], 0)
             q_first, k_first = q_shard * rows + q_off, k_shard * rows + k_off
             q_last, k_last = q_first + TILE - 1, k_first + TILE - 1
-            live = valid & (k_first <= q_last) & (segs[k_last] >= segs[q_first])
+            live = (k_first <= q_last) & (segs[k_last] >= segs[q_first])
             full = (k_last <= q_first) & (segs[k_first] == segs[q_last])
             q_rows, k_rows = pl.ds(q_off, TILE), pl.ds(k_off, TILE)
 
@@ -208,7 +224,7 @@
 
             return carry
 
-        lax.fori_loop(0, q_count * per * k_tiles, body, 0)
+        lax.fori_loop(0, q_count * k_count, pair_body, 0)
 
     for entry in plan.entries:
         run(*entry)
@@ -268,7 +284,9 @@
         out_shape=out_shape,
         compiler_params=pltpu.CompilerParams(vmem_limit_bytes=VMEM_BYTES),
         cost_estimate=pl.CostEstimate(
-            flops=2 * rows * rows * HEAD_DIM, bytes_accessed=8 * rows * HEAD_DIM, transcendentals=0
+            flops=(1 if first else 2) * 2**7 * rows * rows * HEAD_DIM,
+            bytes_accessed=16 * rows * HEAD_DIM * len(plan.blocks),
+            transcendentals=4 * rows * rows,
         ),
         name="attend",
     )(ids, segs, seg_rows, *plan.blocks, *acc)
@@ -329,19 +347,19 @@
         route = [(i, (i + PAIR * distance) ^ cross) for i in range(shards)]
         return lax.ppermute(block, "seq", [hop for hop in route if 0 <= hop[1] < shards])
 
-    query_own, key_own, other, gate_grad, seg_all = prepare(
-        shards, queries, key_rows, value_rows, attn_out, gate_pre, out_grad,
-        segments.reshape(-1, HEAD_DIM),
+    query_own, key_own, other, gate_grad = prepare(
+        queries, key_rows, value_rows, attn_out, gate_pre, out_grad
     )
+    seg_all = share(shards, segments.reshape(-1, HEAD_DIM), gate_grad)
     segs = seg_all.reshape(shards * rows)
     seg_rows = seg_all.reshape(shards, rows).astype(F32)
     reach = min((WINDOW + 1) // PAIR, pairs - 1)
 
-    def travel(block, sign, relay):
+    def travel(block, sign):
         arrived = {0: block}
         for distance in range(1, reach + 1):
-            if relay:
-                arrived[distance] = shift(arrived[distance - 1], sign)
+            if distance == 2:
+                arrived[distance] = shift(arrived[1], sign)
             else:
                 arrived[distance] = shift(block, sign * distance)
         return arrived
@@ -350,8 +368,8 @@
     query_mine = [query_own, partner[:2]]
     key_mine = [key_own, partner[2:]]
     here = [shard, shard ^ 1]
-    far_queries = [travel(block, -1, relay) for block, relay in zip(query_mine, (True, False))]
-    far_keys = [travel(block, 1, relay) for block, relay in zip(key_mine, (True, False))]
+    far_queries = [travel(block, -1) for block in query_mine]
+    far_keys = [travel(block, 1) for block in key_mine]
 
     def far_ids(distance):
         far = pair + distance

time: 192 us -> 163 us (0.85); the launches traced: 195 us -> 162 us
  waiting for transfers between devices: 62.2 us -> 21.2 us
  Pallas kernels: 92.9 us -> 100 us
    ppermute x14, waiting for transfers between devices: 49.4 us -> 8.32 us  [shift(): lax.ppermute(block, 'seq', [hop for hop in route if 0 <= hop[1] < shards])]
    pallas_call x1 -> x2, Pallas kernels: 9.14 us -> 28.1 us  [the longest x1 23.1 us: share(): pl.pallas_call(functools.partial(share_kernel, shards), in_specs=[any_spe...]
    pallas_call x3, Pallas kernels: 68.3 us -> 56.5 us  [attend(): pl.pallas_call(functools.partial(attend_kernel, plan, first, last), grid_...]
  transfers between devices with their start and end apart: 16 -> 16, of which waited for: 7 -> 2; matrix products, arithmetic and copies ran while one was open for 2% -> 2% of each run, Pallas kernels for 28% -> 47%
where the time goes in v4:
time: 163 us; the launch traced here: 162 us
  Pallas kernels  100 us (61%)
  starting transfers between devices  31 us (19%)
  waiting for transfers between devices  21.2 us (13%)
  local copies, waits for them, and re-layouts  4.87 us (3%)
  other arithmetic  4.15 us (3%)
    pallas_call x3, Pallas kernels, attend(): pl.pallas_call(functools.partial(attend_kernel, plan, first, last), grid_...  56.5 us
    ppermute x14, starting transfers between devices, shift(): lax.ppermute(block, 'seq', [hop for hop in route if 0 <= hop[1] < shards])  29.5 us
    pallas_call x1, Pallas kernels, share(): pl.pallas_call(functools.partial(share_kernel, shards), in_specs=[any_spe...  23.1 us
    pallas_call x3, Pallas kernels, project(): pl.pallas_call(project_early_kernel if early is None else project_late_ke...  15.5 us
    ppermute x2, waiting for transfers between devices, across(): return lax.ppermute(block, 'head', [(i, i ^ bit) for i in range(groups)])  12.9 us
    ppermute x14, waiting for transfers between devices, shift(): lax.ppermute(block, 'seq', [hop for hop in route if 0 <= hop[1] < shards])  8.32 us
    pallas_call x1, Pallas kernels, prepare(): pl.pallas_call(prepare_kernel, grid=(rows // step,), in_specs=[wide] * 6,...  5.03 us
  transfers between devices with their start and end apart: 16, of which 2 were waited for; matrix products, arithmetic and copies ran while one was open for 2% of the time, Pallas kernels for 47%

profile of v4, /device:TPU:12, one launch (start us, length us, event | category | flops | bytes accessed | tf_op | source)
XLA Modules:
  0.0 161.7 jit_solution(323100026421036557)
XLA Ops:
  0.0 5.0 %prepare.1 = (bf16[2,1024,128]{2,1,0:T(8,128)(2,1)}, bf16[2,1024,128]{2,1,0:T(8,128)(2,1)}, bf16[4,1024,128]{2,1,0:T(8,128)(2,1)}, bf16[1024,256]{1,0:T(8,128)(2,1)}) custom-call(bf16[1024,256]{1,0:T(8,128)(2,1)} %queries.1, bf16[1024,256]{1,0:T(8,128)(2,1)} %keys.1, bf16[1024,256]{1,0:T(8,128)(2,1)} %values.1, bf16[1024,256]{1,0:T(8,128)(2,1)} %attn_out.1, ...), custom_call_target="tpu_custom_call" | custom-call | flops 10485760 | bytes 5767168 | tf_op jit(solution)/shard_map/prepare/pallas_call | solution.py:111
  5.0 0.5 collective-permute-start
  5.6 1.9 %collective-permute-start.1 = (bf16[2,1024,128]{2,1,0:T(8,128)(2,1)}, bf16[2,1024,128]{2,1,0:T(8,128)(2,1)S(1)}, u32[]{:S(2)}, u32[]{:S(2)}) collective-permute-start(bf16[2,1024,128]{2,1,0:T(8,128)(2,1)} %get-tuple-element.16.refs_0_), channel_id=1, source_target_pairs={{8,0},{12,4},{16,8},{20,12},{24,16},{28,20},{9,1},{13,5},{17,9},{2... | collective-permute-start | bytes 1572872 | tf_op jit(solution)/shard_map/ppermute | solution.py:348
  7.5 3.9 %collective-permute-start.7 = (bf16[2,1024,128]{2,1,0:T(8,128)(2,1)}, bf16[2,1024,128]{2,1,0:T(8,128)(2,1)}, u32[]{:S(2)}, u32[]{:S(2)}) collective-permute-start(bf16[2,1024,128]{2,1,0:T(8,128)(2,1)} %get-tuple-element.18.refs_2_), channel_id=1, source_target_pairs={{0,8},{4,12},{8,16},{12,20},{16,24},{20,28},{1,9},{5,13},{9,17},{1... | collective-permute-start | bytes 1572872 | tf_op jit(solution)/shard_map/ppermute | solution.py:348
  11.4 0.7 collective-permute-start.11
  12.1 0.7 collective-permute-start.5
  12.9 23.1 %share.1 = s32[8,8,128]{2,1,0:T(8,128)} custom-call(s32[8,128]{1,0:T(8,128)} %bitcast.34, bf16[1024,256]{1,0:T(8,128)(2,1)} %get-tuple-element.15.after.gate_grad), custom_call_target="tpu_custom_call" | custom-call | bytes 65536 | tf_op jit(solution)/shard_map/share/pallas_call | solution.py:53
  36.0 0.8 convert_bitcast_fusion
  36.8 0.6 copy.11
  37.4 0.7 stack.100.ids
  38.0 0.7 stack.95.ids
  38.7 0.6 pad_add_fusion.ids
  39.3 0.0 collective-permute-done.1.refs_4_
  39.3 2.2 %collective-permute-start.2 = (bf16[2,1024,128]{2,1,0:T(8,128)(2,1)S(1)}, bf16[2,1024,128]{2,1,0:T(8,128)(2,1)}, u32[]{:S(2)}, u32[]{:S(2)}) collective-permute-start(bf16[2,1024,128]{2,1,0:T(8,128)(2,1)S(1)} %collective-permute-done.1.refs_4_), channel_id=1, source_target_pairs={{8,0},{12,4},{16,8},{20,12},{24,16},{28,20},{9,1},{13,5},{17,9},{2... | collective-permute-start | bytes 1572872 | tf_op jit(solution)/shard_map/ppermute | solution.py:348
  41.6 0.0 collective-permute-done
  41.6 0.1 fusion.2
  41.7 1.9 %collective-permute-start.3 = (bf16[2,1024,128]{2,1,0:T(8,128)(2,1)S(1)}, bf16[2,1024,128]{2,1,0:T(8,128)(2,1)S(1)}, u32[]{:S(2)}, u32[]{:S(2)}) collective-permute-start(bf16[2,1024,128]{2,1,0:T(8,128)(2,1)S(1)} %get-tuple-element.26.refs_1_), channel_id=1, source_target_pairs={{8,0},{12,4},{16,8},{20,12},{24,16},{28,20},{9,1},{13,5},{17,9},{2... | collective-permute-start | bytes 1572872 | tf_op jit(solution)/shard_map/ppermute | solution.py:348
  43.6 3.9 %collective-permute-start.9 = (bf16[2,1024,128]{2,1,0:T(8,128)(2,1)S(1)}, bf16[2,1024,128]{2,1,0:T(8,128)(2,1)}, u32[]{:S(2)}, u32[]{:S(2)}) collective-permute-start(bf16[2,1024,128]{2,1,0:T(8,128)(2,1)S(1)} %get-tuple-element.25.refs_3_), channel_id=1, source_target_pairs={{0,8},{4,12},{8,16},{12,20},{16,24},{20,28},{1,9},{5,13},{9,17},{1... | collective-permute-start | bytes 1572872 | tf_op jit(solution)/shard_map/ppermute | solution.py:348
  47.6 15.2 %attend.3 = (f32[2,1024,128]{2,1,0:T(8,128)}, f32[2,2,1024,128]{3,2,1,0:T(8,128)}) custom-call(s32[4]{0:T(128)} %pad_add_fusion.ids, s32[8192]{0:T(1024)} %bitcast.28, f32[8,1024]{1,0:T(8,128)} %bitcast.31, bf16[2,1024,128]{2,1,0:T(8,128)(2,1)} %get-tuple-element.16.refs_0_, bf16[2,1024,128]{2,1,0:T(8,128)(2,1)} %copy-done.2, ...), custom_call_target="tpu_custom_call" | custom-call | flops 17179869184 | bytes 8388608 | tf_op jit(solution)/shard_map/attend/pallas_call | solution.py:270
  62.8 0.0 collective-permute-done.11.refs_10_
  62.8 4.8 %collective-permute-start.8 = (bf16[2,1024,128]{2,1,0:T(8,128)(2,1)}, bf16[2,1024,128]{2,1,0:T(8,128)(2,1)S(1)}, u32[]{:S(2)}, u32[]{:S(2)}) collective-permute-start(bf16[2,1024,128]{2,1,0:T(8,128)(2,1)} %collective-permute-done.7.refs_6_), channel_id=1, source_target_pairs={{0,8},{4,12},{8,16},{12,20},{16,24},{20,28},{1,9},{5,13},{9,17},{1... | collective-permute-start | bytes 1572872 | tf_op jit(solution)/shard_map/ppermute | solution.py:348
  67.7 1.5 collective-permute-start.12
  69.1 0.0 collective-permute-done.2.refs_4_
  69.1 0.7 collective-permute-start.6
  69.8 1.9 %collective-permute-start.10 = (bf16[2,1024,128]{2,1,0:T(8,128)(2,1)}, bf16[2,1024,128]{2,1,0:T(8,128)(2,1)S(1)}, u32[]{:S(2)}, u32[]{:S(2)}) collective-permute-start(bf16[2,1024,128]{2,1,0:T(8,128)(2,1)} %collective-permute-done.9.refs_7_), channel_id=1, source_target_pairs={{0,8},{4,12},{8,16},{12,20},{16,24},{20,28},{1,9},{5,13},{9,17},{1... | collective-permute-start | bytes 1572872 | tf_op jit(solution)/shard_map/ppermute | solution.py:348
  71.8 4.1 %collective-permute-start.4 = (bf16[2,1024,128]{2,1,0:T(8,128)(2,1)S(1)}, bf16[2,1024,128]{2,1,0:T(8,128)(2,1)S(1)}, u32[]{:S(2)}, u32[]{:S(2)}) collective-permute-start(bf16[2,1024,128]{2,1,0:T(8,128)(2,1)S(1)} %collective-permute-done.3.refs_5_), channel_id=1, source_target_pairs={{8,0},{12,4},{16,8},{20,12},{24,16},{28,20},{9,1},{13,5},{17,9},{2... | collective-permute-start | bytes 1572872 | tf_op jit(solution)/shard_map/ppermute | solution.py:348
  75.9 25.9 %attend.4 = (f32[2,1024,128]{2,1,0:T(8,128)}, f32[2,2,1024,128]{3,2,1,0:T(8,128)}) custom-call(s32[8]{0:T(128)} %stack.100.ids, s32[8192]{0:T(1024)} %bitcast.29, f32[8,1024]{1,0:T(8,128)} %bitcast.32, bf16[2,1024,128]{2,1,0:T(8,128)(2,1)} %get-tuple-element.16.refs_0_, bf16[2,1024,128]{2,1,0:T(8,128)(2,1)} %copy-done.2, ...), custom_call_target="tpu_custom_call" | custom-call | flops 34359738368 | bytes 16777216 | tf_op jit(solution)/shard_map/attend/pallas_call | solution.py:270
  101.9 0.0 collective-permute-done.12.refs_11_
  101.9 0.0 collective-permute-done.6.refs_7_
  101.9 0.0 collective-permute-done.4.refs_5_
  102.0 0.7 copy-done.7
  102.7 0.2 copy-done.8
  102.9 0.2 copy-done.9
  103.1 0.1 copy-done.10
  103.2 15.4 %attend.5 = (bf16[3,1024,128]{2,1,0:T(8,128)(2,1)}, bf16[3,1024,128]{2,1,0:T(8,128)(2,1)}) custom-call(s32[12]{0:T(128)} %stack.95.ids, s32[8192]{0:T(1024)} %bitcast.30, f32[8,1024]{1,0:T(8,128)} %bitcast.33, bf16[2,1024,128]{2,1,0:T(8,128)(2,1)} %get-tuple-element.16.refs_0_, bf16[2,1024,128]{2,1,0:T(8,128)(2,1)} %copy-done.2, ...), custom_call_target="tpu_custom_call" | custom-call | flops 34359738368 | bytes 25165824 | tf_op jit(solution)/shard_map/attend/pallas_call | solution.py:270
  118.6 0.5 collective-permute-start.13
  119.1 0.6 stack.84.place
  119.7 6.7 %project_early.1.early = f32[4,1024,256]{2,1,0:T(8,128)} custom-call(s32[5]{0:T(128)} %stack.84.place, bf16[3,1024,128]{2,1,0:T(8,128)(2,1)} %get-tuple-element.24.own, bf16[1024,256]{1,0:T(8,128)(2,1)} %get-tuple-element.15.after.gate_grad, bf16[4,1024,256]{2,1,0:T(8,128)(2,1)} %weights.5), custom_call_target="tpu_custom_call" | custom-call | flops 1610612736 | bytes 6291456 | tf_op jit(solution)/shard_map/project_early/pallas_call | solution.py:318
  126.5 8.3 %collective-permute-done.13.other = bf16[3,1024,128]{2,1,0:T(8,128)(2,1)S(1)} collective-permute-done((bf16[3,1024,128]{2,1,0:T(8,128)(2,1)}, bf16[3,1024,128]{2,1,0:T(8,128)(2,1)S(1)}, u32[]{:S(2)}, u32[]{:S(2)}) %collective-permute-start.13) | collective-permute-done | bytes 786464 | tf_op jit(solution)/shard_map/ppermute | solution.py:348
  134.7 0.9 copy-done
  135.7 4.3 %project_late.3 = bf16[2,1024,256]{2,1,0:T(8,128)(2,1)} custom-call(s32[5]{0:T(128)} %stack.84.place, bf16[3,1024,128]{2,1,0:T(8,128)(2,1)} %copy-done, f32[4,1024,256]{2,1,0:T(8,128)} %project_early.1.early, bf16[4,1024,256]{2,1,0:T(8,128)(2,1)} %weights.5), custom_call_target="tpu_custom_call" | custom-call | flops 805306368 | bytes 4194304 | tf_op jit(solution)/shard_map/project_late/pallas_call | solution.py:318
  140.0 4.5 %project_late.2 = f32[2,1024,256]{2,1,0:T(8,128)} custom-call(s32[5]{0:T(128)} %stack.84.place, bf16[3,1024,128]{2,1,0:T(8,128)(2,1)} %copy-done, f32[4,1024,256]{2,1,0:T(8,128)} %project_early.1.early, bf16[4,1024,256]{2,1,0:T(8,128)(2,1)} %weights.5), custom_call_target="tpu_custom_call" | custom-call | flops 805306368 | bytes 4194304 | tf_op jit(solution)/shard_map/project_late/pallas_call | solution.py:318
  144.4 0.0 collective-permute-done.14
  144.4 1.8 %convert_add_fusion = f32[2,1024,256]{2,1,0:T(8,128)S(1)} fusion(f32[2,1024,256]{2,1,0:T(8,128)} %project_late.2, bf16[2,1024,256]{2,1,0:T(8,128)(2,1)S(1)} %collective-permute-done.14), kind=kLoop, calls=%fused_computation | loop fusion | flops 1048576 | bytes 5242880 | tf_op jit(solution)/shard_map/add | solution.py:418
  146.3 0.1 slice.27
  146.3 1.5 collective-permute-start.15
  147.9 12.9 %collective-permute-done.15 = bf16[1,1024,256]{2,1,0:T(8,128)(2,1)S(1)} collective-permute-done((bf16[1,1024,256]{2,1,0:T(8,128)(2,1)S(1)}, bf16[1,1024,256]{2,1,0:T(8,128)(2,1)S(1)}, u32[]{:S(2)}, u32[]{:S(2)}) %collective-permute-start.15) | collective-permute-done | bytes 524320 | tf_op jit(solution)/shard_map/ppermute | solution.py:409
  160.7 1.0 fusion.1
  (24 shorter events, 0.1 us)
Async XLA Ops:
  5.0 36.5 %collective-permute-start = (bf16[4,1024,128]{2,1,0:T(8,128)(2,1)}, bf16[4,1024,128]{2,1,0:T(8,128)(2,1)S(1)}, u32[]{:S(2)}, u32[]{:S(2)}) collective-permute-start(bf16[4,1024,128]{2,1,0:T(8,128)(2,1)} %get-tuple-element.17), channel_id=1, source_target_pairs={{0,4},{4,0},{8,12},{12,8},{16,20},{20,16},{24,28},{28,24},{1,5},{5... | collective-permute-start | bytes 3145736 | tf_op jit(solution)/shard_map/ppermute | solution.py:348
  5.6 33.7 %collective-permute-start.1 = (bf16[2,1024,128]{2,1,0:T(8,128)(2,1)}, bf16[2,1024,128]{2,1,0:T(8,128)(2,1)S(1)}, u32[]{:S(2)}, u32[]{:S(2)}) collective-permute-start(bf16[2,1024,128]{2,1,0:T(8,128)(2,1)} %get-tuple-element.16.refs_0_), channel_id=1, source_target_pairs={{8,0},{12,4},{16,8},{20,12},{24,16},{28,20},{9,1},{13,5},{17,9},{2... | collective-permute-start | bytes 1572872 | tf_op jit(solution)/shard_map/ppermute | solution.py:348
  7.5 36.1 %collective-permute-start.7 = (bf16[2,1024,128]{2,1,0:T(8,128)(2,1)}, bf16[2,1024,128]{2,1,0:T(8,128)(2,1)}, u32[]{:S(2)}, u32[]{:S(2)}) collective-permute-start(bf16[2,1024,128]{2,1,0:T(8,128)(2,1)} %get-tuple-element.18.refs_2_), channel_id=1, source_target_pairs={{0,8},{4,12},{8,16},{12,20},{16,24},{20,28},{1,9},{5,13},{9,17},{1... | collective-permute-start | bytes 1572872 | tf_op jit(solution)/shard_map/ppermute | solution.py:348
  11.4 51.3 %collective-permute-start.11 = (bf16[2,1024,128]{2,1,0:T(8,128)(2,1)}, bf16[2,1024,128]{2,1,0:T(8,128)(2,1)S(1)}, u32[]{:S(2)}, u32[]{:S(2)}) collective-permute-start(bf16[2,1024,128]{2,1,0:T(8,128)(2,1)} %get-tuple-element.18.refs_2_), channel_id=1, source_target_pairs={{0,24},{4,28},{1,25},{5,29},{2,26},{6,30},{3,27},{7,31}} | collective-permute-start | bytes 1572872 | tf_op jit(solution)/shard_map/ppermute | solution.py:348
  12.1 55.5 %collective-permute-start.5 = (bf16[2,1024,128]{2,1,0:T(8,128)(2,1)}, bf16[2,1024,128]{2,1,0:T(8,128)(2,1)S(1)}, u32[]{:S(2)}, u32[]{:S(2)}) collective-permute-start(bf16[2,1024,128]{2,1,0:T(8,128)(2,1)} %get-tuple-element.16.refs_0_), channel_id=1, source_target_pairs={{24,0},{28,4},{25,1},{29,5},{26,2},{30,6},{27,3},{31,7}} | collective-permute-start | bytes 1572872 | tf_op jit(solution)/shard_map/ppermute | solution.py:348
  39.3 23.4 %copy-start.5 = (bf16[2,1024,128]{2,1,0:T(8,128)(2,1)}, bf16[2,1024,128]{2,1,0:T(8,128)(2,1)S(1)}, u32[]{:S(2)}) copy-start(bf16[2,1024,128]{2,1,0:T(8,128)(2,1)S(1)} %collective-permute-done.1.refs_4_) | copy-start | bytes 1572868
  39.3 29.8 %collective-permute-start.2 = (bf16[2,1024,128]{2,1,0:T(8,128)(2,1)S(1)}, bf16[2,1024,128]{2,1,0:T(8,128)(2,1)}, u32[]{:S(2)}, u32[]{:S(2)}) collective-permute-start(bf16[2,1024,128]{2,1,0:T(8,128)(2,1)S(1)} %collective-permute-done.1.refs_4_), channel_id=1, source_target_pairs={{8,0},{12,4},{16,8},{20,12},{24,16},{28,20},{9,1},{13,5},{17,9},{2... | collective-permute-start | bytes 1572872 | tf_op jit(solution)/shard_map/ppermute | solution.py:348
  41.7 5.9 %copy-start.1 = (bf16[2,1024,128]{2,1,0:T(8,128)(2,1)}, bf16[2,1024,128]{2,1,0:T(8,128)(2,1)S(1)}, u32[]{:S(2)}) copy-start(bf16[2,1024,128]{2,1,0:T(8,128)(2,1)S(1)} %get-tuple-element.25.refs_3_) | copy-start | bytes 1572868
  41.7 5.9 %copy-start.2 = (bf16[2,1024,128]{2,1,0:T(8,128)(2,1)}, bf16[2,1024,128]{2,1,0:T(8,128)(2,1)S(1)}, u32[]{:S(2)}) copy-start(bf16[2,1024,128]{2,1,0:T(8,128)(2,1)S(1)} %get-tuple-element.26.refs_1_) | copy-start | bytes 1572868
  41.7 30.1 %collective-permute-start.3 = (bf16[2,1024,128]{2,1,0:T(8,128)(2,1)S(1)}, bf16[2,1024,128]{2,1,0:T(8,128)(2,1)S(1)}, u32[]{:S(2)}, u32[]{:S(2)}) collective-permute-start(bf16[2,1024,128]{2,1,0:T(8,128)(2,1)S(1)} %get-tuple-element.26.refs_1_), channel_id=1, source_target_pairs={{8,0},{12,4},{16,8},{20,12},{24,16},{28,20},{9,1},{13,5},{17,9},{2... | collective-permute-start | bytes 1572872 | tf_op jit(solution)/shard_map/ppermute | solution.py:348
  43.6 26.2 %collective-permute-start.9 = (bf16[2,1024,128]{2,1,0:T(8,128)(2,1)S(1)}, bf16[2,1024,128]{2,1,0:T(8,128)(2,1)}, u32[]{:S(2)}, u32[]{:S(2)}) collective-permute-start(bf16[2,1024,128]{2,1,0:T(8,128)(2,1)S(1)} %get-tuple-element.25.refs_3_), channel_id=1, source_target_pairs={{0,8},{4,12},{8,16},{12,20},{16,24},{20,28},{1,9},{5,13},{9,17},{1... | collective-permute-start | bytes 1572872 | tf_op jit(solution)/shard_map/ppermute | solution.py:348
  62.8 39.1 %copy-start.3 = (bf16[2,1024,128]{2,1,0:T(8,128)(2,1)}, bf16[2,1024,128]{2,1,0:T(8,128)(2,1)S(1)}, u32[]{:S(2)}) copy-start(bf16[2,1024,128]{2,1,0:T(8,128)(2,1)S(1)} %collective-permute-done.11.refs_10_) | copy-start | bytes 1572868
  62.8 39.1 %collective-permute-start.8 = (bf16[2,1024,128]{2,1,0:T(8,128)(2,1)}, bf16[2,1024,128]{2,1,0:T(8,128)(2,1)S(1)}, u32[]{:S(2)}, u32[]{:S(2)}) collective-permute-start(bf16[2,1024,128]{2,1,0:T(8,128)(2,1)} %collective-permute-done.7.refs_6_), channel_id=1, source_target_pairs={{0,8},{4,12},{8,16},{12,20},{16,24},{20,28},{1,9},{5,13},{9,17},{1... | collective-permute-start | bytes 1572872 | tf_op jit(solution)/shard_map/ppermute | solution.py:348
  67.6 34.2 %copy-start.4 = (bf16[2,1024,128]{2,1,0:T(8,128)(2,1)}, bf16[2,1024,128]{2,1,0:T(8,128)(2,1)S(1)}, u32[]{:S(2)}) copy-start(bf16[2,1024,128]{2,1,0:T(8,128)(2,1)S(1)} %collective-permute-done.5.refs_6_) | copy-start | bytes 1572868
  67.7 34.2 %collective-permute-start.12 = (bf16[2,1024,128]{2,1,0:T(8,128)(2,1)}, bf16[2,1024,128]{2,1,0:T(8,128)(2,1)}, u32[]{:S(2)}, u32[]{:S(2)}) collective-permute-start(bf16[2,1024,128]{2,1,0:T(8,128)(2,1)} %copy-done.1), channel_id=1, source_target_pairs={{0,24},{4,28},{1,25},{5,29},{2,26},{6,30},{3,27},{7,31}} | collective-permute-start | bytes 1572872 | tf_op jit(solution)/shard_map/ppermute | solution.py:348
  69.1 32.8 %collective-permute-start.6 = (bf16[2,1024,128]{2,1,0:T(8,128)(2,1)}, bf16[2,1024,128]{2,1,0:T(8,128)(2,1)S(1)}, u32[]{:S(2)}, u32[]{:S(2)}) collective-permute-start(bf16[2,1024,128]{2,1,0:T(8,128)(2,1)} %copy-done.2), channel_id=1, source_target_pairs={{24,0},{28,4},{25,1},{29,5},{26,2},{30,6},{27,3},{31,7}} | collective-permute-start | bytes 1572872 | tf_op jit(solution)/shard_map/ppermute | solution.py:348
  69.8 32.1 %collective-permute-start.10 = (bf16[2,1024,128]{2,1,0:T(8,128)(2,1)}, bf16[2,1024,128]{2,1,0:T(8,128)(2,1)S(1)}, u32[]{:S(2)}, u32[]{:S(2)}) collective-permute-start(bf16[2,1024,128]{2,1,0:T(8,128)(2,1)} %collective-permute-done.9.refs_7_), channel_id=1, source_target_pairs={{0,8},{4,12},{8,16},{12,20},{16,24},{20,28},{1,9},{5,13},{9,17},{1... | collective-permute-start | bytes 1572872 | tf_op jit(solution)/shard_map/ppermute | solution.py:348
  71.8 4.2 %copy-start.6 = (bf16[2,1024,128]{2,1,0:T(8,128)(2,1)}, bf16[2,1024,128]{2,1,0:T(8,128)(2,1)S(1)}, u32[]{:S(2)}) copy-start(bf16[2,1024,128]{2,1,0:T(8,128)(2,1)S(1)} %collective-permute-done.3.refs_5_) | copy-start | bytes 1572868
  71.8 30.2 %collective-permute-start.4 = (bf16[2,1024,128]{2,1,0:T(8,128)(2,1)S(1)}, bf16[2,1024,128]{2,1,0:T(8,128)(2,1)S(1)}, u32[]{:S(2)}, u32[]{:S(2)}) collective-permute-start(bf16[2,1024,128]{2,1,0:T(8,128)(2,1)S(1)} %collective-permute-done.3.refs_5_), channel_id=1, source_target_pairs={{8,0},{12,4},{16,8},{20,12},{24,16},{28,20},{9,1},{13,5},{17,9},{2... | collective-permute-start | bytes 1572872 | tf_op jit(solution)/shard_map/ppermute | solution.py:348
  101.9 0.8 copy-start.7
  101.9 1.0 copy-start.8
  101.9 1.1 copy-start.9
  102.0 1.2 copy-start.10
  118.6 16.2 %collective-permute-start.13 = (bf16[3,1024,128]{2,1,0:T(8,128)(2,1)}, bf16[3,1024,128]{2,1,0:T(8,128)(2,1)S(1)}, u32[]{:S(2)}, u32[]{:S(2)}) collective-permute-start(bf16[3,1024,128]{2,1,0:T(8,128)(2,1)} %get-tuple-element.23), channel_id=1, source_target_pairs={{0,4},{4,0},{8,12},{12,8},{16,20},{20,16},{24,28},{28,24},{1,5},{5... | collective-permute-start | bytes 2359304 | tf_op jit(solution)/shard_map/ppermute | solution.py:348
  134.7 0.9 copy-start
  139.9 4.5 %collective-permute-start.14 = (bf16[2,1024,256]{2,1,0:T(8,128)(2,1)}, bf16[2,1024,256]{2,1,0:T(8,128)(2,1)S(1)}, u32[]{:S(2)}, u32[]{:S(2)}) collective-permute-start(bf16[2,1024,256]{2,1,0:T(8,128)(2,1)} %project_late.3), channel_id=1, source_target_pairs={{0,1},{1,0},{2,3},{3,2},{4,5},{5,4},{6,7},{7,6},{8,9},{9,8},{10,11... | collective-permute-start | bytes 3145736 | tf_op jit(solution)/shard_map/ppermute | solution.py:409
  146.3 14.4 %collective-permute-start.15 = (bf16[1,1024,256]{2,1,0:T(8,128)(2,1)S(1)}, bf16[1,1024,256]{2,1,0:T(8,128)(2,1)S(1)}, u32[]{:S(2)}, u32[]{:S(2)}) collective-permute-start(bf16[1,1024,256]{2,1,0:T(8,128)(2,1)S(1)} %slice.27), channel_id=1, source_target_pairs={{0,2},{1,3},{2,0},{3,1},{4,6},{5,7},{6,4},{7,5},{8,10},{9,11},{10,... | collective-permute-start | bytes 1572872 | tf_op jit(solution)/shard_map/ppermute | solution.py:409

commit v5 on v4

--- a/solution.py
+++ b/solution.py
@@ -21,7 +21,7 @@
     return lax.dot_general(left, right, (dims, ((), ())), preferred_element_type=F32)
 
 
-def share_kernel(shards, segments, after, seg_all, send_sems, recv_sems):
+def share_kernel(shards, segments, seg_all, send_sems, recv_sems):
     me = lax.axis_index("seq")
     to = [{"seq": lax.rem(me + offset, shards)} for offset in range(shards)]
     barrier = pltpu.get_barrier_semaphore()
@@ -48,11 +48,11 @@
         copy.wait()
 
 
-def share(shards, segments, after):
+def share(shards, segments):
     any_spec = pl.BlockSpec(memory_space=pl.ANY)
     return pl.pallas_call(
         functools.partial(share_kernel, shards),
-        in_specs=[any_spec] * 2,
+        in_specs=[any_spec],
         out_specs=any_spec,
         out_shape=jax.ShapeDtypeStruct((shards,) + segments.shape, segments.dtype),
         scratch_shapes=[
@@ -66,11 +66,12 @@
             flops=0, bytes_accessed=2 * shards * segments.size * 4, transcendentals=0
         ),
         name="share",
-    )(segments, after)
+    )(segments)
 
 
 def prepare_kernel(
-    queries, keys, values, attn_out, gate_pre, out_grad, query_own, key_own, other, gate_grad
+    queries, keys, values, attn_out, gate_pre, out_grad, after,
+    query_own, key_own, other, gate_grad,
 ):
     lane = lax.rem(lax.axis_index("seq"), PAIR)
     for slot, (to_query, to_key) in enumerate(
@@ -102,7 +103,7 @@
         ).astype(BF16)
 
 
-def prepare(queries, keys, values, attn_out, gate_pre, out_grad):
+def prepare(queries, keys, values, attn_out, gate_pre, out_grad, after):
     rows, width = queries.shape
     step = min(rows // 2, 256)
     wide = pl.BlockSpec((step, width), lambda i: (i, 0))
@@ -111,7 +112,7 @@
     return pl.pallas_call(
         prepare_kernel,
         grid=(rows // step,),
-        in_specs=[wide] * 6,
+        in_specs=[wide] * 6 + [pl.BlockSpec(memory_space=pl.ANY)],
         out_specs=[heads(2), heads(2), heads(4), wide],
         out_shape=[
             head_shape(2),
@@ -124,7 +125,7 @@
             flops=40 * rows * width, bytes_accessed=22 * rows * width, transcendentals=rows * width
         ),
         name="prepare",
-    )(queries, keys, values, attn_out, gate_pre, out_grad)
+    )(queries, keys, values, attn_out, gate_pre, out_grad, after)
 
 
 def attend_kernel(plan, first, last, ids, segs, seg_rows, *refs):
@@ -326,7 +327,7 @@
             out_specs=pl.BlockSpec((1, rows, width), lambda i, place: (i, 0, 0)),
         ),
         out_shape=jax.ShapeDtypeStruct((count, rows, width), dtype),
-        compiler_params=pltpu.CompilerParams(vmem_limit_bytes=VMEM_BYTES),
+        compiler_params=pltpu.CompilerParams(vmem_limit_bytes=24 * 2**20),
         cost_estimate=pl.CostEstimate(
             flops=6 * count * rows * width * width,
             bytes_accessed=rows * width * (8 + 4 * count),
@@ -347,10 +348,10 @@
         route = [(i, (i + PAIR * distance) ^ cross) for i in range(shards)]
         return lax.ppermute(block, "seq", [hop for hop in route if 0 <= hop[1] < shards])
 
+    seg_all = share(shards, segments.reshape(-1, HEAD_DIM))
     query_own, key_own, other, gate_grad = prepare(
-        queries, key_rows, value_rows, attn_out, gate_pre, out_grad
+        queries, key_rows, value_rows, attn_out, gate_pre, out_grad, seg_all
     )
-    seg_all = share(shards, segments.reshape(-1, HEAD_DIM), gate_grad)
     segs = seg_all.reshape(shards * rows)
     seg_rows = seg_all.reshape(shards, rows).astype(F32)
     reach = min((WINDOW + 1) // PAIR, pairs - 1)
@@ -403,26 +404,25 @@
     bits = []
     while (1 << len(bits)) < groups:
         bits.append(1 << len(bits))
-    kept = list(range(groups))
 
     def across(block, bit):
         return lax.ppermute(block, "head", [(i, i ^ bit) for i in range(groups)])
 
-    sent = [offset for offset in kept if offset & 1 == 1]
-    near = [offset for offset in kept if offset & 1 == 0]
-    place = jnp.stack([lane] + [group ^ offset for offset in sent + near]).astype(jnp.int32)
+    order = sorted(range(groups), key=lambda offset: (-(offset >> 1), -(offset & 1)))
+    place = jnp.stack([lane] + [group ^ offset for offset in order]).astype(jnp.int32)
     base = project(place, 0, groups, early, None, projections, F32)
-    away = project(place, 0, len(sent), late, base, projections, BF16)
-    arrived = across(away, 1)
-    total = project(place, len(sent), len(near), late, base, projections, F32)
-    total = total + arrived.astype(F32)
-    for bit in bits[1:]:
-        sent = [n for n, offset in enumerate(near) if offset & bit]
-        held = [n for n, offset in enumerate(near) if not offset & bit]
-        arrived = across(jnp.stack([total[n] for n in sent]).astype(BF16), bit)
-        total = jnp.stack([total[n] for n in held]) + arrived.astype(F32)
-        near = [near[n] for n in held]
-    return total[0].astype(BF16)
+    sums = {}
+    for number, offset in enumerate(order):
+        if offset & 1:
+            away = across(project(place, number, 1, late, base, projections, BF16)[0], 1)
+        else:
+            kept = project(place, number, 1, late, base, projections, F32)[0]
+            sums[offset] = kept if groups == 1 else kept + away.astype(F32)
+    for bit in reversed(bits[1:]):
+        for offset in [held for held in sums if held & bit]:
+            arrived = across(sums.pop(offset).astype(BF16), bit)
+            sums[offset ^ bit] = sums[offset ^ bit] + arrived.astype(F32)
+    return sums[0].astype(BF16)
 
 
 def solution(mesh):

time: 163 us -> 152 us (0.933)
  the two profiles are of different devices: /device:TPU:12 before, /device:TPU:20 now
where the time goes in v5:
time: 152 us; the launch traced here: 154 us
  Pallas kernels  80.1 us (53%)
  starting transfers between devices  36.7 us (24%)
  waiting for transfers between devices  31.2 us (21%)
  local copies, waits for them, and re-layouts  4.24 us (3%)
  other arithmetic  1.71 us (1%)
    pallas_call x3, Pallas kernels, attend(): pl.pallas_call(functools.partial(attend_kernel, plan, first, last), grid_...  59.7 us
    ppermute x14, starting transfers between devices, shift(): lax.ppermute(block, 'seq', [hop for hop in route if 0 <= hop[1] < shards])  34.5 us
    ppermute x14, waiting for transfers between devices, shift(): lax.ppermute(block, 'seq', [hop for hop in route if 0 <= hop[1] < shards])  20 us
    ppermute x3, waiting for transfers between devices, across(): return lax.ppermute(block, 'head', [(i, i ^ bit) for i in range(groups)])  11.2 us
    pallas_call x5, Pallas kernels, project(): pl.pallas_call(project_early_kernel if early is None else project_late_ke...  8.23 us
    pallas_call x1, Pallas kernels, share(): pl.pallas_call(functools.partial(share_kernel, shards), in_specs=[any_spe...  7.05 us
    pallas_call x1, Pallas kernels, prepare(): pl.pallas_call(prepare_kernel, grid=(rows // step,), in_specs=[wide] * 6...  5.05 us
  transfers between devices with their start and end apart: 17, of which 5 were waited for; matrix products, arithmetic and copies ran while one was open for 2% of the time, Pallas kernels for 31%

profile of v5, /device:TPU:20, one launch (start us, length us, event | category | flops | bytes accessed | tf_op | source)
XLA Modules:
  0.0 154.4 jit_solution(13547356028381975884)
XLA Ops:
  0.0 7.0 %share.1.after = s32[8,8,128]{2,1,0:T(8,128)} custom-call(s32[8,128]{1,0:T(8,128)} %bitcast.46), custom_call_target="tpu_custom_call" | custom-call | bytes 65536 | tf_op jit(solution)/shard_map/share/pallas_call | solution.py:53
  7.1 5.1 %prepare.1 = (bf16[2,1024,128]{2,1,0:T(8,128)(2,1)}, bf16[2,1024,128]{2,1,0:T(8,128)(2,1)}, bf16[4,1024,128]{2,1,0:T(8,128)(2,1)}, bf16[1024,256]{1,0:T(8,128)(2,1)}) custom-call(bf16[1024,256]{1,0:T(8,128)(2,1)} %queries.1, bf16[1024,256]{1,0:T(8,128)(2,1)} %keys.1, bf16[1024,256]{1,0:T(8,128)(2,1)} %values.1, bf16[1024,256]{1,0:T(8,128)(2,1)} %attn_out.1, ...), custom_call_target="tpu_custom_call" | custom-call | flops 10485760 | bytes 5767168 | tf_op jit(solution)/shard_map/prepare/pallas_call | solution.py:112
  12.1 0.6 collective-permute-start
  12.7 2.4 %collective-permute-start.1 = (bf16[2,1024,128]{2,1,0:T(8,128)(2,1)}, bf16[2,1024,128]{2,1,0:T(8,128)(2,1)}, u32[]{:S(2)}, u32[]{:S(2)}) collective-permute-start(bf16[2,1024,128]{2,1,0:T(8,128)(2,1)} %get-tuple-element.15.refs_0_), channel_id=1, source_target_pairs={{8,0},{12,4},{16,8},{20,12},{24,16},{28,20},{9,1},{13,5},{17,9},{2... | collective-permute-start | bytes 1572872 | tf_op jit(solution)/shard_map/ppermute | solution.py:349
  15.1 4.3 %collective-permute-start.7 = (bf16[2,1024,128]{2,1,0:T(8,128)(2,1)}, bf16[2,1024,128]{2,1,0:T(8,128)(2,1)}, u32[]{:S(2)}, u32[]{:S(2)}) collective-permute-start(bf16[2,1024,128]{2,1,0:T(8,128)(2,1)} %get-tuple-element.17.refs_2_), channel_id=1, source_target_pairs={{0,8},{4,12},{8,16},{12,20},{16,24},{20,28},{1,9},{5,13},{9,17},{1... | collective-permute-start | bytes 1572872 | tf_op jit(solution)/shard_map/ppermute | solution.py:349
  19.4 0.7 collective-permute-start.11
  20.1 0.7 collective-permute-start.5
  20.9 0.6 copy.11
  21.5 0.6 stack.100.ids
  22.1 0.6 stack.95.ids
  22.7 0.6 pad_add_fusion.ids
  23.3 5.7 %collective-permute-done.1.refs_4_ = bf16[2,1024,128]{2,1,0:T(8,128)(2,1)} collective-permute-done((bf16[2,1024,128]{2,1,0:T(8,128)(2,1)}, bf16[2,1024,128]{2,1,0:T(8,128)(2,1)}, u32[]{:S(2)}, u32[]{:S(2)}) %collective-permute-start.1) | collective-permute-done | bytes 524320 | tf_op jit(solution)/shard_map/ppermute | solution.py:349
  29.0 2.0 %collective-permute-start.2 = (bf16[2,1024,128]{2,1,0:T(8,128)(2,1)}, bf16[2,1024,128]{2,1,0:T(8,128)(2,1)}, u32[]{:S(2)}, u32[]{:S(2)}) collective-permute-start(bf16[2,1024,128]{2,1,0:T(8,128)(2,1)} %collective-permute-done.1.refs_4_), channel_id=1, source_target_pairs={{8,0},{12,4},{16,8},{20,12},{24,16},{28,20},{9,1},{13,5},{17,9},{2... | collective-permute-start | bytes 1572872 | tf_op jit(solution)/shard_map/ppermute | solution.py:349
  31.0 5.1 %collective-permute-done = bf16[4,1024,128]{2,1,0:T(8,128)(2,1)S(1)} collective-permute-done((bf16[4,1024,128]{2,1,0:T(8,128)(2,1)}, bf16[4,1024,128]{2,1,0:T(8,128)(2,1)S(1)}, u32[]{:S(2)}, u32[]{:S(2)}) %collective-permute-start) | collective-permute-done | bytes 1048608 | tf_op jit(solution)/shard_map/ppermute | solution.py:349
  36.1 0.1 fusion.3
  36.2 2.7 %collective-permute-start.3 = (bf16[2,1024,128]{2,1,0:T(8,128)(2,1)S(1)}, bf16[2,1024,128]{2,1,0:T(8,128)(2,1)S(1)}, u32[]{:S(2)}, u32[]{:S(2)}) collective-permute-start(bf16[2,1024,128]{2,1,0:T(8,128)(2,1)S(1)} %get-tuple-element.26.refs_1_), channel_id=1, source_target_pairs={{8,0},{12,4},{16,8},{20,12},{24,16},{28,20},{9,1},{13,5},{17,9},{2... | collective-permute-start | bytes 1572872 | tf_op jit(solution)/shard_map/ppermute | solution.py:349
  38.9 1.6 %collective-permute-done.7.refs_6_ = bf16[2,1024,128]{2,1,0:T(8,128)(2,1)} collective-permute-done((bf16[2,1024,128]{2,1,0:T(8,128)(2,1)}, bf16[2,1024,128]{2,1,0:T(8,128)(2,1)}, u32[]{:S(2)}, u32[]{:S(2)}) %collective-permute-start.7) | collective-permute-done | bytes 524320 | tf_op jit(solution)/shard_map/ppermute | solution.py:349
  40.5 4.5 %collective-permute-start.9 = (bf16[2,1024,128]{2,1,0:T(8,128)(2,1)S(1)}, bf16[2,1024,128]{2,1,0:T(8,128)(2,1)}, u32[]{:S(2)}, u32[]{:S(2)}) collective-permute-start(bf16[2,1024,128]{2,1,0:T(8,128)(2,1)S(1)} %get-tuple-element.25.refs_3_), channel_id=1, source_target_pairs={{0,8},{4,12},{8,16},{12,20},{16,24},{20,28},{1,9},{5,13},{9,17},{1... | collective-permute-start | bytes 1572872 | tf_op jit(solution)/shard_map/ppermute | solution.py:349
  45.1 15.2 %attend.3 = (f32[2,1024,128]{2,1,0:T(8,128)}, f32[2,2,1024,128]{3,2,1,0:T(8,128)}) custom-call(s32[4]{0:T(128)} %pad_add_fusion.ids, s32[8192]{0:T(1024)} %bitcast.40, f32[8,1024]{1,0:T(8,128)} %bitcast.43, bf16[2,1024,128]{2,1,0:T(8,128)(2,1)} %get-tuple-element.15.refs_0_, bf16[2,1024,128]{2,1,0:T(8,128)(2,1)} %copy-done.4, ...), custom_call_target="tpu_custom_call" | custom-call | flops 17179869184 | bytes 8388608 | tf_op jit(solution)/shard_map/attend/pallas_call | solution.py:271
  60.3 0.0 collective-permute-done.11.refs_10_
  60.3 2.5 %collective-permute-start.8 = (bf16[2,1024,128]{2,1,0:T(8,128)(2,1)}, bf16[2,1024,128]{2,1,0:T(8,128)(2,1)S(1)}, u32[]{:S(2)}, u32[]{:S(2)}) collective-permute-start(bf16[2,1024,128]{2,1,0:T(8,128)(2,1)} %collective-permute-done.7.refs_6_), channel_id=1, source_target_pairs={{0,8},{4,12},{8,16},{12,20},{16,24},{20,28},{1,9},{5,13},{9,17},{1... | collective-permute-start | bytes 1572872 | tf_op jit(solution)/shard_map/ppermute | solution.py:349
  62.8 0.0 collective-permute-done.5.refs_6_
  62.8 1.5 collective-permute-start.12
  64.3 1.5 collective-permute-start.6
  65.8 7.6 %collective-permute-start.10 = (bf16[2,1024,128]{2,1,0:T(8,128)(2,1)}, bf16[2,1024,128]{2,1,0:T(8,128)(2,1)S(1)}, u32[]{:S(2)}, u32[]{:S(2)}) collective-permute-start(bf16[2,1024,128]{2,1,0:T(8,128)(2,1)} %collective-permute-done.9.refs_7_), channel_id=1, source_target_pairs={{0,8},{4,12},{8,16},{12,20},{16,24},{20,28},{1,9},{5,13},{9,17},{1... | collective-permute-start | bytes 1572872 | tf_op jit(solution)/shard_map/ppermute | solution.py:349
  73.3 0.0 collective-permute-done.3.refs_5_
  73.4 2.1 %collective-permute-start.4 = (bf16[2,1024,128]{2,1,0:T(8,128)(2,1)S(1)}, bf16[2,1024,128]{2,1,0:T(8,128)(2,1)S(1)}, u32[]{:S(2)}, u32[]{:S(2)}) collective-permute-start(bf16[2,1024,128]{2,1,0:T(8,128)(2,1)S(1)} %collective-permute-done.3.refs_5_), channel_id=1, source_target_pairs={{8,0},{12,4},{16,8},{20,12},{24,16},{28,20},{9,1},{13,5},{17,9},{2... | collective-permute-start | bytes 1572872 | tf_op jit(solution)/shard_map/ppermute | solution.py:349
  75.5 25.9 %attend.4 = (f32[2,1024,128]{2,1,0:T(8,128)}, f32[2,2,1024,128]{3,2,1,0:T(8,128)}) custom-call(s32[8]{0:T(128)} %stack.100.ids, s32[8192]{0:T(1024)} %bitcast.41, f32[8,1024]{1,0:T(8,128)} %bitcast.44, bf16[2,1024,128]{2,1,0:T(8,128)(2,1)} %get-tuple-element.15.refs_0_, bf16[2,1024,128]{2,1,0:T(8,128)(2,1)} %copy-done.4, ...), custom_call_target="tpu_custom_call" | custom-call | flops 34359738368 | bytes 16777216 | tf_op jit(solution)/shard_map/attend/pallas_call | solution.py:271
  101.5 0.0 collective-permute-done.6.refs_7_
  101.5 0.7 copy-done.9
  102.2 0.2 copy-done.10
  102.4 0.2 copy-done.11
  102.6 18.6 %attend.5 = (bf16[3,1024,128]{2,1,0:T(8,128)(2,1)}, bf16[3,1024,128]{2,1,0:T(8,128)(2,1)}) custom-call(s32[12]{0:T(128)} %stack.95.ids, s32[8192]{0:T(1024)} %bitcast.42, f32[8,1024]{1,0:T(8,128)} %bitcast.45, bf16[2,1024,128]{2,1,0:T(8,128)(2,1)} %get-tuple-element.15.refs_0_, bf16[2,1024,128]{2,1,0:T(8,128)(2,1)} %copy-done.4, ...), custom_call_target="tpu_custom_call" | custom-call | flops 34359738368 | bytes 25165824 | tf_op jit(solution)/shard_map/attend/pallas_call | solution.py:271
  121.3 1.6 %collective-permute-start.13 = (bf16[3,1024,128]{2,1,0:T(8,128)(2,1)}, bf16[3,1024,128]{2,1,0:T(8,128)(2,1)S(1)}, u32[]{:S(2)}, u32[]{:S(2)}) collective-permute-start(bf16[3,1024,128]{2,1,0:T(8,128)(2,1)} %get-tuple-element.22), channel_id=1, source_target_pairs={{0,4},{4,0},{8,12},{12,8},{16,20},{20,16},{24,28},{28,24},{1,5},{5... | collective-permute-start | bytes 2359304 | tf_op jit(solution)/shard_map/ppermute | solution.py:349
  122.9 0.1 stack.84.place
  123.0 1.1 copy-done.1
  124.1 3.6 %project_early.1.early = f32[4,1024,256]{2,1,0:T(8,128)S(1)} custom-call(s32[5]{0:T(128)S(1)} %stack.84.place, bf16[3,1024,128]{2,1,0:T(8,128)(2,1)S(1)} %copy-done.1, bf16[1024,256]{1,0:T(8,128)(2,1)S(1)} %copy-done.2, bf16[4,1024,256]{2,1,0:T(8,128)(2,1)S(1)} %copy-done), custom_call_target="tpu_custom_call" | custom-call | flops 1610612736 | bytes 6291456 | tf_op jit(solution)/shard_map/project_early/pallas_call | solution.py:319
  127.7 7.5 %collective-permute-done.13.other = bf16[3,1024,128]{2,1,0:T(8,128)(2,1)S(1)} collective-permute-done((bf16[3,1024,128]{2,1,0:T(8,128)(2,1)}, bf16[3,1024,128]{2,1,0:T(8,128)(2,1)S(1)}, u32[]{:S(2)}, u32[]{:S(2)}) %collective-permute-start.13) | collective-permute-done | bytes 786464 | tf_op jit(solution)/shard_map/ppermute | solution.py:349
  135.2 1.2 project_late.7
  136.4 0.1 collective-permute-start.15
  136.5 1.2 project_late.5
  137.6 0.6 collective-permute-start.14
  138.2 1.1 project_late.6
  139.4 0.1 fusion
  139.5 1.5 collective-permute-start.16
  141.0 1.2 project_late.4
  142.2 11.2 %collective-permute-done.16 = bf16[1024,256]{1,0:T(8,128)(2,1)S(1)} collective-permute-done((bf16[1024,256]{1,0:T(8,128)(2,1)S(1)}, bf16[1024,256]{1,0:T(8,128)(2,1)S(1)}, u32[]{:S(2)}, u32[]{:S(2)}) %collective-permute-start.16) | collective-permute-done | bytes 524320 | tf_op jit(solution)/shard_map/ppermute | solution.py:409
  153.4 1.0 fusion.2
  (29 shorter events, 0.1 us)
Async XLA Ops:
  7.1 13.8 %copy-start.5 = (s32[8,8,128]{2,1,0:T(8,128)S(1)}, s32[8,8,128]{2,1,0:T(8,128)}, u32[]{:S(2)}) copy-start(s32[8,8,128]{2,1,0:T(8,128)} %share.1.after) | copy-start | bytes 98308
  12.1 24.0 %collective-permute-start = (bf16[4,1024,128]{2,1,0:T(8,128)(2,1)}, bf16[4,1024,128]{2,1,0:T(8,128)(2,1)S(1)}, u32[]{:S(2)}, u32[]{:S(2)}) collective-permute-start(bf16[4,1024,128]{2,1,0:T(8,128)(2,1)} %get-tuple-element.16), channel_id=1, source_target_pairs={{0,4},{4,0},{8,12},{12,8},{16,20},{20,16},{24,28},{28,24},{1,5},{5... | collective-permute-start | bytes 3145736 | tf_op jit(solution)/shard_map/ppermute | solution.py:349
  12.7 16.3 %collective-permute-start.1 = (bf16[2,1024,128]{2,1,0:T(8,128)(2,1)}, bf16[2,1024,128]{2,1,0:T(8,128)(2,1)}, u32[]{:S(2)}, u32[]{:S(2)}) collective-permute-start(bf16[2,1024,128]{2,1,0:T(8,128)(2,1)} %get-tuple-element.15.refs_0_), channel_id=1, source_target_pairs={{8,0},{12,4},{16,8},{20,12},{24,16},{28,20},{9,1},{13,5},{17,9},{2... | collective-permute-start | bytes 1572872 | tf_op jit(solution)/shard_map/ppermute | solution.py:349
  15.1 25.5 %collective-permute-start.7 = (bf16[2,1024,128]{2,1,0:T(8,128)(2,1)}, bf16[2,1024,128]{2,1,0:T(8,128)(2,1)}, u32[]{:S(2)}, u32[]{:S(2)}) collective-permute-start(bf16[2,1024,128]{2,1,0:T(8,128)(2,1)} %get-tuple-element.17.refs_2_), channel_id=1, source_target_pairs={{0,8},{4,12},{8,16},{12,20},{16,24},{20,28},{1,9},{5,13},{9,17},{1... | collective-permute-start | bytes 1572872 | tf_op jit(solution)/shard_map/ppermute | solution.py:349
  19.4 40.9 %collective-permute-start.11 = (bf16[2,1024,128]{2,1,0:T(8,128)(2,1)}, bf16[2,1024,128]{2,1,0:T(8,128)(2,1)S(1)}, u32[]{:S(2)}, u32[]{:S(2)}) collective-permute-start(bf16[2,1024,128]{2,1,0:T(8,128)(2,1)} %get-tuple-element.17.refs_2_), channel_id=1, source_target_pairs={{0,24},{4,28},{1,25},{5,29},{2,26},{6,30},{3,27},{7,31}} | collective-permute-start | bytes 1572872 | tf_op jit(solution)/shard_map/ppermute | solution.py:349
  20.1 42.7 %collective-permute-start.5 = (bf16[2,1024,128]{2,1,0:T(8,128)(2,1)}, bf16[2,1024,128]{2,1,0:T(8,128)(2,1)S(1)}, u32[]{:S(2)}, u32[]{:S(2)}) collective-permute-start(bf16[2,1024,128]{2,1,0:T(8,128)(2,1)} %get-tuple-element.15.refs_0_), channel_id=1, source_target_pairs={{24,0},{28,4},{25,1},{29,5},{26,2},{30,6},{27,3},{31,7}} | collective-permute-start | bytes 1572872 | tf_op jit(solution)/shard_map/ppermute | solution.py:349
  29.0 35.3 %collective-permute-start.2 = (bf16[2,1024,128]{2,1,0:T(8,128)(2,1)}, bf16[2,1024,128]{2,1,0:T(8,128)(2,1)}, u32[]{:S(2)}, u32[]{:S(2)}) collective-permute-start(bf16[2,1024,128]{2,1,0:T(8,128)(2,1)} %collective-permute-done.1.refs_4_), channel_id=1, source_target_pairs={{8,0},{12,4},{16,8},{20,12},{24,16},{28,20},{9,1},{13,5},{17,9},{2... | collective-permute-start | bytes 1572872 | tf_op jit(solution)/shard_map/ppermute | solution.py:349
  36.2 8.9 %copy-start.3 = (bf16[2,1024,128]{2,1,0:T(8,128)(2,1)}, bf16[2,1024,128]{2,1,0:T(8,128)(2,1)S(1)}, u32[]{:S(2)}) copy-start(bf16[2,1024,128]{2,1,0:T(8,128)(2,1)S(1)} %get-tuple-element.25.refs_3_) | copy-start | bytes 1572868
  36.2 8.9 %copy-start.4 = (bf16[2,1024,128]{2,1,0:T(8,128)(2,1)}, bf16[2,1024,128]{2,1,0:T(8,128)(2,1)S(1)}, u32[]{:S(2)}) copy-start(bf16[2,1024,128]{2,1,0:T(8,128)(2,1)S(1)} %get-tuple-element.26.refs_1_) | copy-start | bytes 1572868
  36.2 37.1 %collective-permute-start.3 = (bf16[2,1024,128]{2,1,0:T(8,128)(2,1)S(1)}, bf16[2,1024,128]{2,1,0:T(8,128)(2,1)S(1)}, u32[]{:S(2)}, u32[]{:S(2)}) collective-permute-start(bf16[2,1024,128]{2,1,0:T(8,128)(2,1)S(1)} %get-tuple-element.26.refs_1_), channel_id=1, source_target_pairs={{8,0},{12,4},{16,8},{20,12},{24,16},{28,20},{9,1},{13,5},{17,9},{2... | collective-permute-start | bytes 1572872 | tf_op jit(solution)/shard_map/ppermute | solution.py:349
  40.5 25.2 %collective-permute-start.9 = (bf16[2,1024,128]{2,1,0:T(8,128)(2,1)S(1)}, bf16[2,1024,128]{2,1,0:T(8,128)(2,1)}, u32[]{:S(2)}, u32[]{:S(2)}) collective-permute-start(bf16[2,1024,128]{2,1,0:T(8,128)(2,1)S(1)} %get-tuple-element.25.refs_3_), channel_id=1, source_target_pairs={{0,8},{4,12},{8,16},{12,20},{16,24},{20,28},{1,9},{5,13},{9,17},{1... | collective-permute-start | bytes 1572872 | tf_op jit(solution)/shard_map/ppermute | solution.py:349
  60.3 41.1 %copy-start.6 = (bf16[2,1024,128]{2,1,0:T(8,128)(2,1)}, bf16[2,1024,128]{2,1,0:T(8,128)(2,1)S(1)}, u32[]{:S(2)}) copy-start(bf16[2,1024,128]{2,1,0:T(8,128)(2,1)S(1)} %collective-permute-done.11.refs_10_) | copy-start | bytes 1572868
  60.3 41.2 %collective-permute-start.8 = (bf16[2,1024,128]{2,1,0:T(8,128)(2,1)}, bf16[2,1024,128]{2,1,0:T(8,128)(2,1)S(1)}, u32[]{:S(2)}, u32[]{:S(2)}) collective-permute-start(bf16[2,1024,128]{2,1,0:T(8,128)(2,1)} %collective-permute-done.7.refs_6_), channel_id=1, source_target_pairs={{0,8},{4,12},{8,16},{12,20},{16,24},{20,28},{1,9},{5,13},{9,17},{1... | collective-permute-start | bytes 1572872 | tf_op jit(solution)/shard_map/ppermute | solution.py:349
  62.8 38.6 %copy-start.7 = (bf16[2,1024,128]{2,1,0:T(8,128)(2,1)}, bf16[2,1024,128]{2,1,0:T(8,128)(2,1)S(1)}, u32[]{:S(2)}) copy-start(bf16[2,1024,128]{2,1,0:T(8,128)(2,1)S(1)} %collective-permute-done.5.refs_6_) | copy-start | bytes 1572868
  62.8 38.6 %collective-permute-start.12 = (bf16[2,1024,128]{2,1,0:T(8,128)(2,1)}, bf16[2,1024,128]{2,1,0:T(8,128)(2,1)}, u32[]{:S(2)}, u32[]{:S(2)}) collective-permute-start(bf16[2,1024,128]{2,1,0:T(8,128)(2,1)} %copy-done.3), channel_id=1, source_target_pairs={{0,24},{4,28},{1,25},{5,29},{2,26},{6,30},{3,27},{7,31}} | collective-permute-start | bytes 1572872 | tf_op jit(solution)/shard_map/ppermute | solution.py:349
  64.3 37.2 %collective-permute-start.6 = (bf16[2,1024,128]{2,1,0:T(8,128)(2,1)}, bf16[2,1024,128]{2,1,0:T(8,128)(2,1)}, u32[]{:S(2)}, u32[]{:S(2)}) collective-permute-start(bf16[2,1024,128]{2,1,0:T(8,128)(2,1)} %copy-done.4), channel_id=1, source_target_pairs={{24,0},{28,4},{25,1},{29,5},{26,2},{30,6},{27,3},{31,7}} | collective-permute-start | bytes 1572872 | tf_op jit(solution)/shard_map/ppermute | solution.py:349
  65.8 35.7 %collective-permute-start.10 = (bf16[2,1024,128]{2,1,0:T(8,128)(2,1)}, bf16[2,1024,128]{2,1,0:T(8,128)(2,1)S(1)}, u32[]{:S(2)}, u32[]{:S(2)}) collective-permute-start(bf16[2,1024,128]{2,1,0:T(8,128)(2,1)} %collective-permute-done.9.refs_7_), channel_id=1, source_target_pairs={{0,8},{4,12},{8,16},{12,20},{16,24},{20,28},{1,9},{5,13},{9,17},{1... | collective-permute-start | bytes 1572872 | tf_op jit(solution)/shard_map/ppermute | solution.py:349
  73.4 2.1 %copy-start.8 = (bf16[2,1024,128]{2,1,0:T(8,128)(2,1)}, bf16[2,1024,128]{2,1,0:T(8,128)(2,1)S(1)}, u32[]{:S(2)}) copy-start(bf16[2,1024,128]{2,1,0:T(8,128)(2,1)S(1)} %collective-permute-done.3.refs_5_) | copy-start | bytes 1572868
  73.4 28.1 %collective-permute-start.4 = (bf16[2,1024,128]{2,1,0:T(8,128)(2,1)S(1)}, bf16[2,1024,128]{2,1,0:T(8,128)(2,1)S(1)}, u32[]{:S(2)}, u32[]{:S(2)}) collective-permute-start(bf16[2,1024,128]{2,1,0:T(8,128)(2,1)S(1)} %collective-permute-done.3.refs_5_), channel_id=1, source_target_pairs={{8,0},{12,4},{16,8},{20,12},{24,16},{28,20},{9,1},{13,5},{17,9},{2... | collective-permute-start | bytes 1572872 | tf_op jit(solution)/shard_map/ppermute | solution.py:349
  101.4 0.8 copy-start.9
  101.5 0.9 copy-start.10
  101.5 1.1 copy-start.11
  102.6 20.4 %copy-start = (bf16[4,1024,256]{2,1,0:T(8,128)(2,1)S(1)}, bf16[4,1024,256]{2,1,0:T(8,128)(2,1)}, u32[]{:S(2)}) copy-start(bf16[4,1024,256]{2,1,0:T(8,128)(2,1)} %weights.9) | copy-start | bytes 6291460
  102.6 20.4 %copy-start.2 = (bf16[1024,256]{1,0:T(8,128)(2,1)S(1)}, bf16[1024,256]{1,0:T(8,128)(2,1)}, u32[]{:S(2)}) copy-start(bf16[1024,256]{1,0:T(8,128)(2,1)} %get-tuple-element.24.gate_grad) | copy-start | bytes 1572868
  121.3 13.9 %collective-permute-start.13 = (bf16[3,1024,128]{2,1,0:T(8,128)(2,1)}, bf16[3,1024,128]{2,1,0:T(8,128)(2,1)S(1)}, u32[]{:S(2)}, u32[]{:S(2)}) collective-permute-start(bf16[3,1024,128]{2,1,0:T(8,128)(2,1)} %get-tuple-element.22), channel_id=1, source_target_pairs={{0,4},{4,0},{8,12},{12,8},{16,20},{20,16},{24,28},{28,24},{1,5},{5... | collective-permute-start | bytes 2359304 | tf_op jit(solution)/shard_map/ppermute | solution.py:349
  123.0 1.1 copy-start.1
  136.4 3.0 %collective-permute-start.15 = (bf16[1024,256]{1,0:T(8,128)(2,1)S(1)}, bf16[1024,256]{1,0:T(8,128)(2,1)S(1)}, u32[]{:S(2)}, u32[]{:S(2)}) collective-permute-start(bf16[1024,256]{1,0:T(8,128)(2,1)S(1)} %bitcast.39), channel_id=1, source_target_pairs={{0,1},{1,0},{2,3},{3,2},{4,5},{5,4},{6,7},{7,6},{8,9},{9,8},{10,11... | collective-permute-start | bytes 1572872 | tf_op jit(solution)/shard_map/ppermute | solution.py:409
  137.6 4.6 %collective-permute-start.14 = (bf16[1024,256]{1,0:T(8,128)(2,1)S(1)}, bf16[1024,256]{1,0:T(8,128)(2,1)S(1)}, u32[]{:S(2)}, u32[]{:S(2)}) collective-permute-start(bf16[1024,256]{1,0:T(8,128)(2,1)S(1)} %bitcast.38), channel_id=1, source_target_pairs={{0,1},{1,0},{2,3},{3,2},{4,5},{5,4},{6,7},{7,6},{8,9},{9,8},{10,11... | collective-permute-start | bytes 1572872 | tf_op jit(solution)/shard_map/ppermute | solution.py:409
  139.5 13.9 %collective-permute-start.16 = (bf16[1024,256]{1,0:T(8,128)(2,1)S(1)}, bf16[1024,256]{1,0:T(8,128)(2,1)S(1)}, u32[]{:S(2)}, u32[]{:S(2)}) collective-permute-start(bf16[1024,256]{1,0:T(8,128)(2,1)S(1)} %fusion), channel_id=1, source_target_pairs={{0,2},{1,3},{2,0},{3,1},{4,6},{5,7},{6,4},{7,5},{8,10},{9,11},{10,... | collective-permute-start | bytes 1572872 | tf_op jit(solution)/shard_map/ppermute | solution.py:409

commit v6 on v3

--- a/solution.py
+++ b/solution.py
@@ -102,12 +102,11 @@
     wide = pl.BlockSpec((step, width), lambda i: (i, 0))
     heads = lambda deep: pl.BlockSpec((deep, step, HEAD_DIM), lambda i: (0, i, 0))
     head_shape = lambda deep: jax.ShapeDtypeStruct((deep, rows, HEAD_DIM), BF16)
-    any_spec = pl.BlockSpec(memory_space=pl.ANY)
     return pl.pallas_call(
         functools.partial(prepare_kernel, shards),
         grid=(rows // step,),
-        in_specs=[wide] * 6 + [any_spec],
-        out_specs=[heads(2), heads(2), heads(4), wide, any_spec],
+        in_specs=[wide] * 6 + [pl.BlockSpec(memory_space=pl.ANY)],
+        out_specs=[heads(2), heads(2), heads(4), wide, pl.BlockSpec(memory_space=pl.ANY)],
         out_shape=[
             head_shape(2),
             head_shape(2),
@@ -150,23 +149,41 @@
         ]
     for copy in copies:
         copy.start()
-    for copy in copies:
-        copy.wait()
+    waiting = set(range(len(copies)))
+
+    def arrive(needed):
+        for n in sorted(waiting & set(needed)):
+            copies[n].wait()
+            waiting.discard(n)
+
+    arrive(range(len(blocks), len(copies)))
 
     def run(q_start, q_count, k_start, k_count, to_query, to_key):
-        k_tiles = k_count * per
-
-        def body(index, carry):
-            q_idx, k_idx = index // k_tiles, index % k_tiles
-            q_blk, k_blk = q_idx // per, k_idx // per
-            q_off = pl.multiple_of((q_idx % per) * TILE, TILE)
-            k_off = pl.multiple_of((k_idx % per) * TILE, TILE)
+        arrive(range(q_start, q_start + q_count))
+        arrive(range(k_start, k_start + k_count))
+
+        def pair_body(index, carry):
+            q_blk, k_blk = index // k_count, index % k_count
+            q_shard, k_shard = ids[q_start + q_blk], ids[k_start + k_blk]
+            valid = (q_shard >= 0) & (k_shard >= 0) & (k_shard <= q_shard)
+            q_shard, k_shard = jnp.maximum(q_shard, 0), jnp.maximum(k_shard, 0)
+            meet = segs[k_shard * rows + rows - 1] >= segs[q_shard * rows]
+
+            @pl.when(valid & meet)
+            def _():
+                lax.fori_loop(
+                    0, per * per, functools.partial(tile_body, q_blk, k_blk, q_shard, k_shard), 0
+                )
+
+            return carry
+
+        def tile_body(q_blk, k_blk, q_shard, k_shard, index, carry):
+            q_off = pl.multiple_of((index // per) * TILE, TILE)
+            k_off = pl.multiple_of((index % per) * TILE, TILE)
             q_held, k_held = q_start + q_blk, k_start + k_blk
-            valid = (ids[q_held] >= 0) & (ids[k_held] >= 0)
-            q_shard, k_shard = jnp.maximum(ids[q_held], 0), jnp.maximum(ids[k_held], 0)
             q_first, k_first = q_shard * rows + q_off, k_shard * rows + k_off
             q_last, k_last = q_first + TILE - 1, k_first + TILE - 1
-            live = valid & (k_first <= q_last) & (segs[k_last] >= segs[q_first])
+            live = (k_first <= q_last) & (segs[k_last] >= segs[q_first])
             full = (k_last <= q_first) & (segs[k_first] == segs[q_last])
             q_rows, k_rows = pl.ds(q_off, TILE), pl.ds(k_off, TILE)
 
@@ -208,7 +225,7 @@
 
             return carry
 
-        lax.fori_loop(0, q_count * per * k_tiles, body, 0)
+        lax.fori_loop(0, q_count * k_count, pair_body, 0)
 
     for entry in plan.entries:
         run(*entry)
@@ -266,9 +283,11 @@
             ],
         ),
         out_shape=out_shape,
-        compiler_params=pltpu.CompilerParams(vmem_limit_bytes=VMEM_BYTES),
+        compiler_params=pltpu.CompilerParams(vmem_limit_bytes=24 * 2**20),
         cost_estimate=pl.CostEstimate(
-            flops=2 * rows * rows * HEAD_DIM, bytes_accessed=8 * rows * HEAD_DIM, transcendentals=0
+            flops=(1 if first else 2) * 2**7 * rows * rows * HEAD_DIM,
+            bytes_accessed=16 * rows * HEAD_DIM * len(plan.blocks),
+            transcendentals=4 * rows * rows,
         ),
         name="attend",
     )(ids, segs, seg_rows, *plan.blocks, *acc)
@@ -308,7 +327,7 @@
             out_specs=pl.BlockSpec((1, rows, width), lambda i, place: (i, 0, 0)),
         ),
         out_shape=jax.ShapeDtypeStruct((count, rows, width), dtype),
-        compiler_params=pltpu.CompilerParams(vmem_limit_bytes=VMEM_BYTES),
+        compiler_params=pltpu.CompilerParams(vmem_limit_bytes=24 * 2**20),
         cost_estimate=pl.CostEstimate(
             flops=6 * count * rows * width * width,
             bytes_accessed=rows * width * (8 + 4 * count),
@@ -337,11 +356,11 @@
     seg_rows = seg_all.reshape(shards, rows).astype(F32)
     reach = min((WINDOW + 1) // PAIR, pairs - 1)
 
-    def travel(block, sign, relay):
+    def travel(block, sign):
         arrived = {0: block}
         for distance in range(1, reach + 1):
-            if relay:
-                arrived[distance] = shift(arrived[distance - 1], sign)
+            if distance == 2:
+                arrived[distance] = shift(arrived[1], sign)
             else:
                 arrived[distance] = shift(block, sign * distance)
         return arrived
@@ -350,8 +369,8 @@
     query_mine = [query_own, partner[:2]]
     key_mine = [key_own, partner[2:]]
     here = [shard, shard ^ 1]
-    far_queries = [travel(block, -1, relay) for block, relay in zip(query_mine, (True, False))]
-    far_keys = [travel(block, 1, relay) for block, relay in zip(key_mine, (True, False))]
+    far_queries = [travel(block, -1) for block in query_mine]
+    far_keys = [travel(block, 1) for block in key_mine]
 
     def far_ids(distance):
         far = pair + distance
@@ -385,26 +404,25 @@
     bits = []
     while (1 << len(bits)) < groups:
         bits.append(1 << len(bits))
-    kept = list(range(groups))
 
     def across(block, bit):
         return lax.ppermute(block, "head", [(i, i ^ bit) for i in range(groups)])
 
-    sent = [offset for offset in kept if offset & 1 == 1]
-    near = [offset for offset in kept if offset & 1 == 0]
-    place = jnp.stack([lane] + [group ^ offset for offset in sent + near]).astype(jnp.int32)
+    order = sorted(range(groups), key=lambda offset: (-(offset >> 1), -(offset & 1)))
+    place = jnp.stack([lane] + [group ^ offset for offset in order]).astype(jnp.int32)
     base = project(place, 0, groups, early, None, projections, F32)
-    away = project(place, 0, len(sent), late, base, projections, BF16)
-    arrived = across(away, 1)
-    total = project(place, len(sent), len(near), late, base, projections, F32)
-    total = total + arrived.astype(F32)
-    for bit in bits[1:]:
-        sent = [n for n, offset in enumerate(near) if offset & bit]
-        held = [n for n, offset in enumerate(near) if not offset & bit]
-        arrived = across(jnp.stack([total[n] for n in sent]).astype(BF16), bit)
-        total = jnp.stack([total[n] for n in held]) + arrived.astype(F32)
-        near = [near[n] for n in held]
-    return total[0].astype(BF16)
+    sums = {}
+    for number, offset in enumerate(order):
+        if offset & 1:
+            away = across(project(place, number, 1, late, base, projections, BF16)[0], 1)
+        else:
+            kept = project(place, number, 1, late, base, projections, F32)[0]
+            sums[offset] = kept if groups == 1 else kept + away.astype(F32)
+    for bit in reversed(bits[1:]):
+        for offset in [held for held in sums if held & bit]:
+            arrived = across(sums.pop(offset).astype(BF16), bit)
+            sums[offset ^ bit] = sums[offset ^ bit] + arrived.astype(F32)
+    return sums[0].astype(BF16)
 
 
 def solution(mesh):

time: 192 us -> 150 us (0.78)
  the two profiles are of different devices: /device:TPU:12 before, /device:TPU:0 now
where the time goes in v6:
time: 150 us; the launch traced here: 149 us
  Pallas kernels  67.3 us (45%)
  waiting for transfers between devices  44.8 us (30%)
  starting transfers between devices  28.7 us (19%)
  local copies, waits for them, and re-layouts  5.71 us (4%)
  other arithmetic  1.95 us (1%)
    pallas_call x3, Pallas kernels, attend(): pl.pallas_call(functools.partial(attend_kernel, plan, first, last), grid_...  46.9 us
    ppermute x14, waiting for transfers between devices, shift(): lax.ppermute(block, 'seq', [hop for hop in route if 0 <= hop[1] < shards])  33.6 us
    ppermute x14, starting transfers between devices, shift(): lax.ppermute(block, 'seq', [hop for hop in route if 0 <= hop[1] < shards])  26.5 us
    pallas_call x1, Pallas kernels, prepare(): pl.pallas_call(functools.partial(prepare_kernel, shards), grid=(rows // s...  12.1 us
    ppermute x3, waiting for transfers between devices, across(): return lax.ppermute(block, 'head', [(i, i ^ bit) for i in range(groups)])  11.2 us
    pallas_call x5, Pallas kernels, project(): pl.pallas_call(project_early_kernel if early is None else project_late_ke...  8.23 us
    unnamed x25, local copies, waits for them, and re-layouts  4.18 us
  transfers between devices with their start and end apart: 17, of which 6 were waited for; matrix products, arithmetic and copies ran while one was open for 2% of the time, Pallas kernels for 24%

profile of v6, /device:TPU:0, one launch (start us, length us, event | category | flops | bytes accessed | tf_op | source)
XLA Modules:
  0.0 149.0 jit_solution(5018301161095671949)
XLA Ops:
  0.0 12.1 %prepare.1 = (bf16[2,1024,128]{2,1,0:T(8,128)(2,1)}, bf16[2,1024,128]{2,1,0:T(8,128)(2,1)}, bf16[4,1024,128]{2,1,0:T(8,128)(2,1)}, bf16[1024,256]{1,0:T(8,128)(2,1)}, s32[8,8,128]{2,1,0:T(8,128)}) custom-call(bf16[1024,256]{1,0:T(8,128)(2,1)} %queries.1, bf16[1024,256]{1,0:T(8,128)(2,1)} %keys.1, bf16[1024,256]{1,0:T(8,128)(2,1)} %values.1, ...), custom_call_target="tpu_custom_call" | custom-call | flops 10485760 | bytes 5767168 | tf_op jit(solution)/shard_map/prepare/pallas_call | solution.py:105
  12.1 0.6 collective-permute-start
  12.8 1.3 collective-permute-start.1
  14.0 5.3 %collective-permute-start.7 = (bf16[2,1024,128]{2,1,0:T(8,128)(2,1)}, bf16[2,1024,128]{2,1,0:T(8,128)(2,1)}, u32[]{:S(2)}, u32[]{:S(2)}) collective-permute-start(bf16[2,1024,128]{2,1,0:T(8,128)(2,1)} %get-tuple-element.19.refs_2_), channel_id=1, source_target_pairs={{0,8},{4,12},{8,16},{12,20},{16,24},{20,28},{1,9},{5,13},{9,17},{1... | collective-permute-start | bytes 1572872 | tf_op jit(solution)/shard_map/ppermute | solution.py:349
  19.4 2.0 %collective-permute-start.11 = (bf16[2,1024,128]{2,1,0:T(8,128)(2,1)}, bf16[2,1024,128]{2,1,0:T(8,128)(2,1)S(1)}, u32[]{:S(2)}, u32[]{:S(2)}) collective-permute-start(bf16[2,1024,128]{2,1,0:T(8,128)(2,1)} %get-tuple-element.19.refs_2_), channel_id=1, source_target_pairs={{0,24},{4,28},{1,25},{5,29},{2,26},{6,30},{3,27},{7,31}} | collective-permute-start | bytes 1572872 | tf_op jit(solution)/shard_map/ppermute | solution.py:349
  21.4 1.3 collective-permute-start.5
  22.8 0.8 convert_bitcast_fusion
  23.6 0.1 stack.100.ids
  23.7 0.1 stack.95.ids
  23.8 0.1 pad_add_fusion.ids
  23.9 6.0 %collective-permute-done.1.refs_4_ = bf16[2,1024,128]{2,1,0:T(8,128)(2,1)S(1)} collective-permute-done((bf16[2,1024,128]{2,1,0:T(8,128)(2,1)}, bf16[2,1024,128]{2,1,0:T(8,128)(2,1)S(1)}, u32[]{:S(2)}, u32[]{:S(2)}) %collective-permute-start.1) | collective-permute-done | bytes 524320 | tf_op jit(solution)/shard_map/ppermute | solution.py:349
  29.9 1.3 collective-permute-start.2
  31.2 5.9 %collective-permute-done = bf16[4,1024,128]{2,1,0:T(8,128)(2,1)} collective-permute-done((bf16[4,1024,128]{2,1,0:T(8,128)(2,1)}, bf16[4,1024,128]{2,1,0:T(8,128)(2,1)}, u32[]{:S(2)}, u32[]{:S(2)}) %collective-permute-start) | collective-permute-done | bytes 1048608 | tf_op jit(solution)/shard_map/ppermute | solution.py:349
  37.1 1.3 fusion.3
  38.4 1.3 collective-permute-start.3
  39.7 0.0 collective-permute-done.7.refs_6_
  39.7 4.6 %collective-permute-start.9 = (bf16[2,1024,128]{2,1,0:T(8,128)(2,1)S(1)}, bf16[2,1024,128]{2,1,0:T(8,128)(2,1)S(1)}, u32[]{:S(2)}, u32[]{:S(2)}) collective-permute-start(bf16[2,1024,128]{2,1,0:T(8,128)(2,1)S(1)} %get-tuple-element.27.refs_3_), channel_id=1, source_target_pairs={{0,8},{4,12},{8,16},{12,20},{16,24},{20,28},{1,9},{5,13},{9,17},{1... | collective-permute-start | bytes 1572872 | tf_op jit(solution)/shard_map/ppermute | solution.py:349
  44.3 13.0 %attend.3 = (f32[2,1024,128]{2,1,0:T(8,128)S(1)}, f32[2,2,1024,128]{3,2,1,0:T(8,128)S(1)}) custom-call(s32[4]{0:T(128)S(1)} %pad_add_fusion.ids, s32[8192]{0:T(1024)S(1)} %bitcast.40, f32[8,1024]{1,0:T(8,128)S(1)} %bitcast.43, bf16[2,1024,128]{2,1,0:T(8,128)(2,1)S(1)} %copy-done.5, bf16[2,1024,128]{2,1,0:T(8,128)(2,1)S(1)} %get-tuple-element.28.refs_1_, ...), custom_call_target="tpu_custom_call" | custom-call | flops 17179869184 | bytes 8388608 | tf_op jit(solution)/shard_map/attend/pallas_call | solution.py:271
  57.3 0.0 collective-permute-done.11.refs_10_
  57.3 2.5 %collective-permute-start.8 = (bf16[2,1024,128]{2,1,0:T(8,128)(2,1)}, bf16[2,1024,128]{2,1,0:T(8,128)(2,1)S(1)}, u32[]{:S(2)}, u32[]{:S(2)}) collective-permute-start(bf16[2,1024,128]{2,1,0:T(8,128)(2,1)} %collective-permute-done.7.refs_6_), channel_id=1, source_target_pairs={{0,8},{4,12},{8,16},{12,20},{16,24},{20,28},{1,9},{5,13},{9,17},{1... | collective-permute-start | bytes 1572872 | tf_op jit(solution)/shard_map/ppermute | solution.py:349
  59.8 0.0 copy-start.10
  59.8 1.3 collective-permute-start.12
  61.2 1.3 collective-permute-start.6
  62.5 0.0 collective-permute-done.9.refs_7_
  62.5 2.0 %collective-permute-start.10 = (bf16[2,1024,128]{2,1,0:T(8,128)(2,1)S(1)}, bf16[2,1024,128]{2,1,0:T(8,128)(2,1)S(1)}, u32[]{:S(2)}, u32[]{:S(2)}) collective-permute-start(bf16[2,1024,128]{2,1,0:T(8,128)(2,1)S(1)} %collective-permute-done.9.refs_7_), channel_id=1, source_target_pairs={{0,8},{4,12},{8,16},{12,20},{16,24},{20,28},{1,9},{5,13},{9,17},{1... | collective-permute-start | bytes 1572872 | tf_op jit(solution)/shard_map/ppermute | solution.py:349
  64.5 1.5 collective-permute-start.4
  66.0 15.9 %attend.4 = (f32[2,1024,128]{2,1,0:T(8,128)S(1)}, f32[2,2,1024,128]{3,2,1,0:T(8,128)S(1)}) custom-call(s32[8]{0:T(128)S(1)} %stack.100.ids, s32[8192]{0:T(1024)S(1)} %bitcast.41, f32[8,1024]{1,0:T(8,128)S(1)} %bitcast.44, bf16[2,1024,128]{2,1,0:T(8,128)(2,1)S(1)} %copy-done.5, bf16[2,1024,128]{2,1,0:T(8,128)(2,1)S(1)} %get-tuple-element.28.refs_1_, ...), custom_call_target="tpu_custom_call" | custom-call | flops 34359738368 | bytes 16777216 | tf_op jit(solution)/shard_map/attend/pallas_call | solution.py:271
  82.0 1.6 %collective-permute-done.12.refs_11_ = bf16[2,1024,128]{2,1,0:T(8,128)(2,1)S(1)} collective-permute-done((bf16[2,1024,128]{2,1,0:T(8,128)(2,1)S(1)}, bf16[2,1024,128]{2,1,0:T(8,128)(2,1)S(1)}, u32[]{:S(2)}, u32[]{:S(2)}) %collective-permute-start.12) | collective-permute-done | bytes 524320 | tf_op jit(solution)/shard_map/ppermute | solution.py:349
  83.6 8.3 %collective-permute-done.10.refs_9_ = bf16[2,1024,128]{2,1,0:T(8,128)(2,1)S(1)} collective-permute-done((bf16[2,1024,128]{2,1,0:T(8,128)(2,1)S(1)}, bf16[2,1024,128]{2,1,0:T(8,128)(2,1)S(1)}, u32[]{:S(2)}, u32[]{:S(2)}) %collective-permute-start.10) | collective-permute-done | bytes 524320 | tf_op jit(solution)/shard_map/ppermute | solution.py:349
  91.9 1.0 copy-done.9
  93.0 1.0 copy-done.11
  94.0 18.0 %attend.5 = (bf16[3,1024,128]{2,1,0:T(8,128)(2,1)S(1)}, bf16[3,1024,128]{2,1,0:T(8,128)(2,1)}) custom-call(s32[12]{0:T(128)S(1)} %stack.95.ids, s32[8192]{0:T(1024)S(1)} %bitcast.42, f32[8,1024]{1,0:T(8,128)S(1)} %bitcast.45, bf16[2,1024,128]{2,1,0:T(8,128)(2,1)S(1)} %copy-done.5, bf16[2,1024,128]{2,1,0:T(8,128)(2,1)S(1)} %get-tuple-element.28.refs_1_, ...), custom_call_target="tpu_custom_call" | custom-call | flops 34359738368 | bytes 25165824 | tf_op jit(solution)/shard_map/attend/pallas_call | solution.py:271
  112.1 0.9 copy-done.1
  113.0 0.3 collective-permute-start.13
  113.3 0.1 stack.84.place
  113.3 1.1 copy-done.2
  114.5 3.6 %project_early.1.early = f32[4,1024,256]{2,1,0:T(8,128)S(1)} custom-call(s32[5]{0:T(128)S(1)} %stack.84.place, bf16[3,1024,128]{2,1,0:T(8,128)(2,1)S(1)} %copy-done.2, bf16[1024,256]{1,0:T(8,128)(2,1)S(1)} %copy-done.3, bf16[4,1024,256]{2,1,0:T(8,128)(2,1)S(1)} %copy-done), custom_call_target="tpu_custom_call" | custom-call | flops 1610612736 | bytes 6291456 | tf_op jit(solution)/shard_map/project_early/pallas_call | solution.py:319
  118.1 11.7 %collective-permute-done.13.other = bf16[3,1024,128]{2,1,0:T(8,128)(2,1)S(1)} collective-permute-done((bf16[3,1024,128]{2,1,0:T(8,128)(2,1)}, bf16[3,1024,128]{2,1,0:T(8,128)(2,1)S(1)}, u32[]{:S(2)}, u32[]{:S(2)}) %collective-permute-start.13) | collective-permute-done | bytes 786464 | tf_op jit(solution)/shard_map/ppermute | solution.py:349
  129.8 1.2 project_late.7
  131.0 0.1 collective-permute-start.15
  131.1 1.2 project_late.5
  132.2 0.6 collective-permute-start.14
  132.8 1.1 project_late.6
  133.9 0.1 fusion
  134.1 1.6 %collective-permute-start.16 = (bf16[1024,256]{1,0:T(8,128)(2,1)S(1)}, bf16[1024,256]{1,0:T(8,128)(2,1)S(1)}, u32[]{:S(2)}, u32[]{:S(2)}) collective-permute-start(bf16[1024,256]{1,0:T(8,128)(2,1)S(1)} %fusion), channel_id=1, source_target_pairs={{0,2},{1,3},{2,0},{3,1},{4,6},{5,7},{6,4},{7,5},{8,10},{9,11},{10,... | collective-permute-start | bytes 1572872 | tf_op jit(solution)/shard_map/ppermute | solution.py:409
  135.6 1.2 project_late.4
  136.8 11.2 %collective-permute-done.16 = bf16[1024,256]{1,0:T(8,128)(2,1)S(1)} collective-permute-done((bf16[1024,256]{1,0:T(8,128)(2,1)S(1)}, bf16[1024,256]{1,0:T(8,128)(2,1)S(1)}, u32[]{:S(2)}, u32[]{:S(2)}) %collective-permute-start.16) | collective-permute-done | bytes 524320 | tf_op jit(solution)/shard_map/ppermute | solution.py:409
  148.0 1.0 fusion.2
  (28 shorter events, 0.1 us)
Async XLA Ops:
  12.1 32.2 %copy-start.4 = (s32[8,8,128]{2,1,0:T(8,128)S(1)}, s32[8,8,128]{2,1,0:T(8,128)}, u32[]{:S(2)}) copy-start(s32[8,8,128]{2,1,0:T(8,128)} %get-tuple-element.16) | copy-start | bytes 98308
  12.1 32.2 %copy-start.5 = (bf16[2,1024,128]{2,1,0:T(8,128)(2,1)S(1)}, bf16[2,1024,128]{2,1,0:T(8,128)(2,1)}, u32[]{:S(2)}) copy-start(bf16[2,1024,128]{2,1,0:T(8,128)(2,1)} %get-tuple-element.17.refs_0_) | copy-start | bytes 1572868
  12.1 32.2 %copy-start.6 = (bf16[2,1024,128]{2,1,0:T(8,128)(2,1)S(1)}, bf16[2,1024,128]{2,1,0:T(8,128)(2,1)}, u32[]{:S(2)}) copy-start(bf16[2,1024,128]{2,1,0:T(8,128)(2,1)} %get-tuple-element.19.refs_2_) | copy-start | bytes 1572868
  12.1 25.0 %collective-permute-start = (bf16[4,1024,128]{2,1,0:T(8,128)(2,1)}, bf16[4,1024,128]{2,1,0:T(8,128)(2,1)}, u32[]{:S(2)}, u32[]{:S(2)}) collective-permute-start(bf16[4,1024,128]{2,1,0:T(8,128)(2,1)} %get-tuple-element.18), channel_id=1, source_target_pairs={{0,4},{4,0},{8,12},{12,8},{16,20},{20,16},{24,28},{28,24},{1,5},{5... | collective-permute-start | bytes 3145736 | tf_op jit(solution)/shard_map/ppermute | solution.py:349
  12.8 17.1 %collective-permute-start.1 = (bf16[2,1024,128]{2,1,0:T(8,128)(2,1)}, bf16[2,1024,128]{2,1,0:T(8,128)(2,1)S(1)}, u32[]{:S(2)}, u32[]{:S(2)}) collective-permute-start(bf16[2,1024,128]{2,1,0:T(8,128)(2,1)} %get-tuple-element.17.refs_0_), channel_id=1, source_target_pairs={{8,0},{12,4},{16,8},{20,12},{24,16},{28,20},{9,1},{13,5},{17,9},{2... | collective-permute-start | bytes 1572872 | tf_op jit(solution)/shard_map/ppermute | solution.py:349
  14.0 25.7 %collective-permute-start.7 = (bf16[2,1024,128]{2,1,0:T(8,128)(2,1)}, bf16[2,1024,128]{2,1,0:T(8,128)(2,1)}, u32[]{:S(2)}, u32[]{:S(2)}) collective-permute-start(bf16[2,1024,128]{2,1,0:T(8,128)(2,1)} %get-tuple-element.19.refs_2_), channel_id=1, source_target_pairs={{0,8},{4,12},{8,16},{12,20},{16,24},{20,28},{1,9},{5,13},{9,17},{1... | collective-permute-start | bytes 1572872 | tf_op jit(solution)/shard_map/ppermute | solution.py:349
  19.4 37.9 %collective-permute-start.11 = (bf16[2,1024,128]{2,1,0:T(8,128)(2,1)}, bf16[2,1024,128]{2,1,0:T(8,128)(2,1)S(1)}, u32[]{:S(2)}, u32[]{:S(2)}) collective-permute-start(bf16[2,1024,128]{2,1,0:T(8,128)(2,1)} %get-tuple-element.19.refs_2_), channel_id=1, source_target_pairs={{0,24},{4,28},{1,25},{5,29},{2,26},{6,30},{3,27},{7,31}} | collective-permute-start | bytes 1572872 | tf_op jit(solution)/shard_map/ppermute | solution.py:349
  21.4 38.4 %collective-permute-start.5 = (bf16[2,1024,128]{2,1,0:T(8,128)(2,1)}, bf16[2,1024,128]{2,1,0:T(8,128)(2,1)S(1)}, u32[]{:S(2)}, u32[]{:S(2)}) collective-permute-start(bf16[2,1024,128]{2,1,0:T(8,128)(2,1)} %get-tuple-element.17.refs_0_), channel_id=1, source_target_pairs={{24,0},{28,4},{25,1},{29,5},{26,2},{30,6},{27,3},{31,7}} | collective-permute-start | bytes 1572872 | tf_op jit(solution)/shard_map/ppermute | solution.py:349
  29.9 31.3 %collective-permute-start.2 = (bf16[2,1024,128]{2,1,0:T(8,128)(2,1)S(1)}, bf16[2,1024,128]{2,1,0:T(8,128)(2,1)S(1)}, u32[]{:S(2)}, u32[]{:S(2)}) collective-permute-start(bf16[2,1024,128]{2,1,0:T(8,128)(2,1)S(1)} %collective-permute-done.1.refs_4_), channel_id=1, source_target_pairs={{8,0},{12,4},{16,8},{20,12},{24,16},{28,20},{9,1},{13,5},{17,9},{2... | collective-permute-start | bytes 1572872 | tf_op jit(solution)/shard_map/ppermute | solution.py:349
  38.4 26.1 %collective-permute-start.3 = (bf16[2,1024,128]{2,1,0:T(8,128)(2,1)S(1)}, bf16[2,1024,128]{2,1,0:T(8,128)(2,1)S(1)}, u32[]{:S(2)}, u32[]{:S(2)}) collective-permute-start(bf16[2,1024,128]{2,1,0:T(8,128)(2,1)S(1)} %get-tuple-element.28.refs_1_), channel_id=1, source_target_pairs={{8,0},{12,4},{16,8},{20,12},{24,16},{28,20},{9,1},{13,5},{17,9},{2... | collective-permute-start | bytes 1572872 | tf_op jit(solution)/shard_map/ppermute | solution.py:349
  39.7 22.8 %collective-permute-start.9 = (bf16[2,1024,128]{2,1,0:T(8,128)(2,1)S(1)}, bf16[2,1024,128]{2,1,0:T(8,128)(2,1)S(1)}, u32[]{:S(2)}, u32[]{:S(2)}) collective-permute-start(bf16[2,1024,128]{2,1,0:T(8,128)(2,1)S(1)} %get-tuple-element.27.refs_3_), channel_id=1, source_target_pairs={{0,8},{4,12},{8,16},{12,20},{16,24},{20,28},{1,9},{5,13},{9,17},{1... | collective-permute-start | bytes 1572872 | tf_op jit(solution)/shard_map/ppermute | solution.py:349
  57.3 24.6 %copy-start.8 = (bf16[2,1024,128]{2,1,0:T(8,128)(2,1)}, bf16[2,1024,128]{2,1,0:T(8,128)(2,1)S(1)}, u32[]{:S(2)}) copy-start(bf16[2,1024,128]{2,1,0:T(8,128)(2,1)S(1)} %collective-permute-done.11.refs_10_) | copy-start | bytes 1572868
  57.3 24.7 %collective-permute-start.8 = (bf16[2,1024,128]{2,1,0:T(8,128)(2,1)}, bf16[2,1024,128]{2,1,0:T(8,128)(2,1)S(1)}, u32[]{:S(2)}, u32[]{:S(2)}) collective-permute-start(bf16[2,1024,128]{2,1,0:T(8,128)(2,1)} %collective-permute-done.7.refs_6_), channel_id=1, source_target_pairs={{0,8},{4,12},{8,16},{12,20},{16,24},{20,28},{1,9},{5,13},{9,17},{1... | collective-permute-start | bytes 1572872 | tf_op jit(solution)/shard_map/ppermute | solution.py:349
  59.8 22.1 %copy-start.10 = (bf16[2,1024,128]{2,1,0:T(8,128)(2,1)}, bf16[2,1024,128]{2,1,0:T(8,128)(2,1)S(1)}, u32[]{:S(2)}) copy-start(bf16[2,1024,128]{2,1,0:T(8,128)(2,1)S(1)} %collective-permute-done.5.refs_6_) | copy-start | bytes 1572868
  59.8 23.8 %collective-permute-start.12 = (bf16[2,1024,128]{2,1,0:T(8,128)(2,1)S(1)}, bf16[2,1024,128]{2,1,0:T(8,128)(2,1)S(1)}, u32[]{:S(2)}, u32[]{:S(2)}) collective-permute-start(bf16[2,1024,128]{2,1,0:T(8,128)(2,1)S(1)} %get-tuple-element.27.refs_3_), channel_id=1, source_target_pairs={{0,24},{4,28},{1,25},{5,29},{2,26},{6,30},{3,27},{7,31}} | collective-permute-start | bytes 1572872 | tf_op jit(solution)/shard_map/ppermute | solution.py:349
  61.2 22.5 %collective-permute-start.6 = (bf16[2,1024,128]{2,1,0:T(8,128)(2,1)S(1)}, bf16[2,1024,128]{2,1,0:T(8,128)(2,1)S(1)}, u32[]{:S(2)}, u32[]{:S(2)}) collective-permute-start(bf16[2,1024,128]{2,1,0:T(8,128)(2,1)S(1)} %get-tuple-element.28.refs_1_), channel_id=1, source_target_pairs={{24,0},{28,4},{25,1},{29,5},{26,2},{30,6},{27,3},{31,7}} | collective-permute-start | bytes 1572872 | tf_op jit(solution)/shard_map/ppermute | solution.py:349
  62.5 29.4 %collective-permute-start.10 = (bf16[2,1024,128]{2,1,0:T(8,128)(2,1)S(1)}, bf16[2,1024,128]{2,1,0:T(8,128)(2,1)S(1)}, u32[]{:S(2)}, u32[]{:S(2)}) collective-permute-start(bf16[2,1024,128]{2,1,0:T(8,128)(2,1)S(1)} %collective-permute-done.9.refs_7_), channel_id=1, source_target_pairs={{0,8},{4,12},{8,16},{12,20},{16,24},{20,28},{1,9},{5,13},{9,17},{1... | collective-permute-start | bytes 1572872 | tf_op jit(solution)/shard_map/ppermute | solution.py:349
  64.5 27.4 %collective-permute-start.4 = (bf16[2,1024,128]{2,1,0:T(8,128)(2,1)S(1)}, bf16[2,1024,128]{2,1,0:T(8,128)(2,1)S(1)}, u32[]{:S(2)}, u32[]{:S(2)}) collective-permute-start(bf16[2,1024,128]{2,1,0:T(8,128)(2,1)S(1)} %collective-permute-done.3.refs_5_), channel_id=1, source_target_pairs={{8,0},{12,4},{16,8},{20,12},{24,16},{28,20},{9,1},{13,5},{17,9},{2... | collective-permute-start | bytes 1572872 | tf_op jit(solution)/shard_map/ppermute | solution.py:349
  66.0 25.9 %copy-start.7 = (bf16[2,1024,128]{2,1,0:T(8,128)(2,1)S(1)}, bf16[2,1024,128]{2,1,0:T(8,128)(2,1)}, u32[]{:S(2)}) copy-start(bf16[2,1024,128]{2,1,0:T(8,128)(2,1)} %get-tuple-element.19.refs_2_) | copy-start | bytes 1572868
  91.9 1.0 copy-start.9
  93.0 1.0 copy-start.11
  94.0 19.3 %copy-start = (bf16[4,1024,256]{2,1,0:T(8,128)(2,1)S(1)}, bf16[4,1024,256]{2,1,0:T(8,128)(2,1)}, u32[]{:S(2)}) copy-start(bf16[4,1024,256]{2,1,0:T(8,128)(2,1)} %weights.9) | copy-start | bytes 6291460
  94.0 19.3 %copy-start.3 = (bf16[1024,256]{1,0:T(8,128)(2,1)S(1)}, bf16[1024,256]{1,0:T(8,128)(2,1)}, u32[]{:S(2)}) copy-start(bf16[1024,256]{1,0:T(8,128)(2,1)} %get-tuple-element.26.gate_grad) | copy-start | bytes 1572868
  112.1 0.9 copy-start.1
  113.0 16.8 %collective-permute-start.13 = (bf16[3,1024,128]{2,1,0:T(8,128)(2,1)}, bf16[3,1024,128]{2,1,0:T(8,128)(2,1)S(1)}, u32[]{:S(2)}, u32[]{:S(2)}) collective-permute-start(bf16[3,1024,128]{2,1,0:T(8,128)(2,1)} %get-tuple-element.24), channel_id=1, source_target_pairs={{0,4},{4,0},{8,12},{12,8},{16,20},{20,16},{24,28},{28,24},{1,5},{5... | collective-permute-start | bytes 2359304 | tf_op jit(solution)/shard_map/ppermute | solution.py:349
  113.3 1.1 copy-start.2
  131.0 3.0 %collective-permute-start.15 = (bf16[1024,256]{1,0:T(8,128)(2,1)S(1)}, bf16[1024,256]{1,0:T(8,128)(2,1)S(1)}, u32[]{:S(2)}, u32[]{:S(2)}) collective-permute-start(bf16[1024,256]{1,0:T(8,128)(2,1)S(1)} %bitcast.39), channel_id=1, source_target_pairs={{0,1},{1,0},{2,3},{3,2},{4,5},{5,4},{6,7},{7,6},{8,9},{9,8},{10,11... | collective-permute-start | bytes 1572872 | tf_op jit(solution)/shard_map/ppermute | solution.py:409
  132.2 4.6 %collective-permute-start.14 = (bf16[1024,256]{1,0:T(8,128)(2,1)S(1)}, bf16[1024,256]{1,0:T(8,128)(2,1)S(1)}, u32[]{:S(2)}, u32[]{:S(2)}) collective-permute-start(bf16[1024,256]{1,0:T(8,128)(2,1)S(1)} %bitcast.38), channel_id=1, source_target_pairs={{0,1},{1,0},{2,3},{3,2},{4,5},{5,4},{6,7},{7,6},{8,9},{9,8},{10,11... | collective-permute-start | bytes 1572872 | tf_op jit(solution)/shard_map/ppermute | solution.py:409
  134.1 13.9 %collective-permute-start.16 = (bf16[1024,256]{1,0:T(8,128)(2,1)S(1)}, bf16[1024,256]{1,0:T(8,128)(2,1)S(1)}, u32[]{:S(2)}, u32[]{:S(2)}) collective-permute-start(bf16[1024,256]{1,0:T(8,128)(2,1)S(1)} %fusion), channel_id=1, source_target_pairs={{0,2},{1,3},{2,0},{3,1},{4,6},{5,7},{6,4},{7,5},{8,10},{9,11},{10,... | collective-permute-start | bytes 1572872 | tf_op jit(solution)/shard_map/ppermute | solution.py:409
